TPU v7x, 32 devices: a whole 2x2x4 slice. The times are simulated.
32 devices in a mesh: blk: 8 (over z, y), tp: 4 (over x, core).
Axes of the slice: x: 2, y: 2, z: 4, core: 2. Of those that a mesh axis runs over, the one named last changes fastest.
Arguments:
- patches: bfloat16 [1024, 1152], P('blk'), may hold values from -6 to 6
- latents: bfloat16 [512, 4096], P('blk'), may hold values from -6 to 6
- image_patches: int32 [8], replicated, may hold values from 1 to 512, as said below
- span_order: int32 [8], replicated, may hold values from 0 to 7, as said below
- vis_gains: float32 [2, 1152], replicated, may hold values from 0.5 to 1.5
- vis_shifts: float32 [2, 1152], replicated, may hold values from -1.75 to 1.75
- vis_qkv: bfloat16 [1152, 3, 1152], P('blk', None, 'tp'), may hold values from -0.1875 to 0.1875
- vis_qv_bias: float32 [2, 1152], P(None, 'tp'), may hold values from -1.75 to 1.75
- vis_out: bfloat16 [1152, 1152], P('tp', 'blk'), may hold values from -0.75 to 0.75
- vis_out_bias: float32 [2, 1152], replicated, may hold values from -1.75 to 1.75
- vis_fc1: bfloat16 [1152, 4304], P('blk', 'tp'), may hold values from -0.1875 to 0.1875
- vis_fc1_bias: float32 [4304], P('tp'), may hold values from -1.75 to 1.75
- vis_fc2: bfloat16 [4304, 1152], P('tp', 'blk'), may hold values from -0.09375 to 0.09375
- proj_gate_up: bfloat16 [1152, 2, 14336], P('blk', None, 'tp'), may hold values from -0.1875 to 0.1875
- proj_down: bfloat16 [14336, 4096], P('tp', 'blk'), may hold values from -0.046875 to 0.046875
- res_gains: float32 [4, 4096], replicated, may hold values from 0.5 to 1.5
- res_q: bfloat16 [4096, 1536], P('blk', 'tp'), may hold values from -0.09375 to 0.09375
- res_kv: bfloat16 [4096, 2, 384], P('blk', None, 'tp'), may hold values from -0.09375 to 0.09375
- res_out: bfloat16 [1536, 4096], P('tp', 'blk'), may hold values from -0.625 to 0.625
- res_gate_up: bfloat16 [4096, 2, 16384], P(None, None, ('blk', 'tp')), may hold values from -0.09375 to 0.09375
- res_down: bfloat16 [16384, 4096], P(('blk', 'tp')), may hold values from -0.046875 to 0.046875
- out_grad: bfloat16 [512, 4096], P('blk'), may hold values from -6 to 6
Outputs:
- latents_out: float32 [512, 4096], P('blk')
- patches_grad: float32 [1024, 1152], P('blk')
- latents_grad: float32 [512, 4096], P('blk')
- grad_vis_gains: float32 [2, 1152], replicated
- grad_vis_shifts: float32 [2, 1152], replicated
- grad_vis_qkv: float32 [1152, 3, 1152], P('blk', None, 'tp')
- grad_vis_qv_bias: float32 [2, 1152], P(None, 'tp')
- grad_vis_out: float32 [1152, 1152], P('tp', 'blk')
- grad_vis_out_bias: float32 [2, 1152], replicated
- grad_vis_fc1: float32 [1152, 4304], P('blk', 'tp')
- grad_vis_fc1_bias: float32 [4304], P('tp')
- grad_vis_fc2: float32 [4304, 1152], P('tp', 'blk')
- grad_proj_gate_up: float32 [1152, 2, 14336], P('blk', None, 'tp')
- grad_proj_down: float32 [14336, 4096], P('tp', 'blk')
- grad_res_gains: float32 [4, 4096], replicated
- grad_res_q: float32 [4096, 1536], P('blk', 'tp')
- grad_res_kv: float32 [4096, 2, 384], P('blk', None, 'tp')
- grad_res_out: float32 [1536, 4096], P('tp', 'blk')
- grad_res_gate_up: float32 [4096, 2, 16384], P(None, None, ('blk', 'tp'))
- grad_res_down: float32 [16384, 4096], P(('blk', 'tp'))
Inputs may be any that keep to these rules, and one draw needn't show every extreme that they name: `image_patches`: the counts sum to 1024; image 0 has 512 patches, every other image fewer. `span_order`: each span is held by exactly one index of blk; index 0 holds span 0, index 7 holds span 1 and index 4 holds span 2.
All inputs are finite; a program needn't handle non-finite values.
Results may differ from a plain program's by a relative error of at most 0.04.
Values may be sent and summed in bfloat16 or wider, within the bound.
No kernel may reach another device: no remote copies, remote signals or barrier semaphores. Data moves between devices by JAX's collectives and lax.ppermute only.
A program may use at most 384 MiB of HBM per device.

v0:
```python
import jax
import jax.numpy as jnp
from jax import lax
from jax.sharding import PartitionSpec as P

HEADS = 16
HEAD_VIS = 72
RES_HEAD = 96
KV_HEADS = 4
LATENTS = 64


EPSILON = 1e-06


def as_sent(value):

    def short(part):
        return part.astype(jnp.bfloat16) if part.dtype == jnp.float32 else part

    return jax.tree.map(short, value)


def from_behind(block, axis, distance):
    devices = range(lax.axis_size(axis))
    route = [((i - distance) % len(devices), i) for i in devices]
    return lax.ppermute(block, axis, route)


def joined(value, axis, combine):
    everything = jax.tree.map(lambda part: lax.all_gather(part, axis), value)
    first = jax.tree.map(lambda part: part[0], everything)

    def step(k, so_far):
        return combine(so_far, jax.tree.map(lambda part: part[k], everything))

    return lax.fori_loop(1, lax.axis_size(axis), step, first)


def layer_norm(values, gain, shift):
    center = values - jnp.mean(values, axis=-1, keepdims=True)
    spread = jnp.mean(center * center, axis=-1, keepdims=True)
    return center * lax.rsqrt(spread + EPSILON) * gain + shift


def rms_norm(values, gain):
    return values * lax.rsqrt(jnp.mean(values * values, axis=-1, keepdims=True) + EPSILON) * gain


def gelu_tanh(values):
    return jax.nn.gelu(values, approximate=True)


def swiglu(gate_part, up_part):
    return jax.nn.silu(gate_part) * up_part


def matmul(left, right):
    return jnp.dot(left, right, preferred_element_type=jnp.float32)


def dot_inner(left, right):
    return lax.dot_general(
        left, right, (((1,), (1,)), ((), ())), preferred_element_type=jnp.float32
    )


def dot_outer(left, right):
    return lax.dot_general(
        left, right, (((0,), (0,)), ((), ())), preferred_element_type=jnp.float32
    )


def fetch_cols(shards):
    return jax.tree.map(
        lambda part, own: part.astype(own.dtype),
        lax.all_gather(as_sent(shards), "blk", axis=0, tiled=True),
        shards,
    )


def fetch_rows(shards):
    return (
        lax.all_gather(shards[0], "blk", axis=1, tiled=True),
        lax.all_gather(shards[1], "blk", axis=1, tiled=True),
    )


def return_cols(gradients):
    return lax.psum_scatter(gradients, "blk", scatter_dimension=0, tiled=True)


def return_rows(gradients):
    return lax.psum_scatter(gradients, "blk", scatter_dimension=1, tiled=True)


def over_heads(partial_value):
    return lax.psum(partial_value, "tp")


def share_rows(rows_low):
    return lax.all_gather(rows_low, "blk", axis=0, tiled=True)


def sum_rows(row_term, row_total):
    return lax.psum_scatter(
        row_term(jnp.int32(0), lax.axis_size("blk") * row_total),
        "blk",
        scatter_dimension=0,
        tiled=True,
    )


def pass_grads(grad_pair):
    return from_behind((grad_pair[0], grad_pair[1]), "blk", 1)


def span_images(image_patches, span_index, tok_rows):
    bounds = jnp.cumsum(image_patches)
    stream = span_index * tok_rows + jnp.arange(tok_rows, dtype=jnp.int32)
    return jnp.sum((stream[:, None] >= bounds[None, :]).astype(jnp.int32), axis=1)


def vision_attend(state_in, query_heads, key_now, value_now, query_ids, key_ids):
    row_top, weight_sum, weighted = state_in
    key_heads = key_now.reshape(key_now.shape[0], query_heads.shape[1], -1)
    value_heads = value_now.reshape(value_now.shape[0], query_heads.shape[1], -1)
    scores = jnp.einsum("qhd,khd->hqk", query_heads, key_heads, preferred_element_type=jnp.float32)
    scores = scores * query_heads.shape[2] ** (-0.5)
    allowed = query_ids[:, None] == key_ids[None, :]
    scores = jnp.where(allowed[None], scores, -jnp.inf)
    new_top = jnp.maximum(row_top, jnp.max(scores, axis=-1))
    factor = jnp.exp(row_top - new_top)
    weights = jnp.exp(scores - new_top[..., None])
    weight_sum = weight_sum * factor + jnp.sum(weights, axis=-1)
    weighted = weighted * factor[..., None] + jnp.einsum(
        "hqk,khd->hqd",
        weights.astype(jnp.bfloat16),
        value_heads,
        preferred_element_type=jnp.float32,
    )
    return (new_top, weight_sum, weighted)


def maybe_attend(state_in, query_heads, key_now, value_now, query_ids, key_ids):
    return vision_attend(state_in, query_heads, key_now, value_now, query_ids, key_ids)


def vision_grads(
    query_heads, key_now, value_now, dout_heads, row_lse, row_delta, query_ids, key_ids
):
    head_count = query_heads.shape[1]
    factor_scale = query_heads.shape[2] ** (-0.5)
    key_heads = key_now.reshape(key_now.shape[0], head_count, -1)
    value_heads = value_now.reshape(value_now.shape[0], head_count, -1)
    scores = (
        jnp.einsum("qhd,khd->hqk", query_heads, key_heads, preferred_element_type=jnp.float32)
        * factor_scale
    )
    allowed = query_ids[:, None] == key_ids[None, :]
    scores = jnp.where(allowed[None], scores, -jnp.inf)
    weights = jnp.exp(scores - row_lse[..., None])
    dweights = jnp.einsum(
        "qhd,khd->hqk", dout_heads, value_heads, preferred_element_type=jnp.float32
    )
    dscores = (weights * (dweights - row_delta[..., None])).astype(jnp.bfloat16)
    dquery = (
        jnp.einsum("hqk,khd->qhd", dscores, key_heads, preferred_element_type=jnp.float32)
        * factor_scale
    )
    dkey = (
        jnp.einsum("hqk,qhd->khd", dscores, query_heads, preferred_element_type=jnp.float32)
        * factor_scale
    )
    dvalue = jnp.einsum(
        "hqk,qhd->khd", weights.astype(jnp.bfloat16), dout_heads, preferred_element_type=jnp.float32
    )
    return (dquery, dkey, dvalue)


def maybe_grads(
    query_heads, key_now, value_now, dout_heads, row_lse, row_delta, query_ids, key_ids
):
    return vision_grads(
        query_heads, key_now, value_now, dout_heads, row_lse, row_delta, query_ids, key_ids
    )


def latent_scores(query_all, key_all, query_images, key_images, kv_local):
    query_heads = query_all.reshape(query_all.shape[0], kv_local, -1, RES_HEAD)
    key_heads = key_all.reshape(key_all.shape[0], kv_local, RES_HEAD)
    scores = jnp.einsum(
        "qkgd,nkd->kgqn", query_heads, key_heads, preferred_element_type=jnp.float32
    )
    scores = scores * RES_HEAD ** (-0.5)
    allowed = query_images[:, None] == key_images[None, :]
    return (jnp.where(allowed, scores, -jnp.inf), allowed)


def latent_partial(query_all, key_all, value_all, query_images, key_images, kv_local):
    scores, allowed = latent_scores(query_all, key_all, query_images, key_images, kv_local)
    row_top = jnp.where(jnp.any(allowed, axis=-1), jnp.max(scores, axis=-1), -1e30)
    weights = jnp.exp(scores - row_top[..., None])
    value_heads = value_all.reshape(value_all.shape[0], kv_local, RES_HEAD)
    weighted = jnp.einsum(
        "kgqn,nkd->kgqd",
        weights.astype(jnp.bfloat16),
        value_heads,
        preferred_element_type=jnp.float32,
    )
    return (row_top, jnp.sum(weights, axis=-1), weighted)


def merge_parts(earlier, later_part):
    row_top = jnp.maximum(earlier[0], later_part[0])
    scale_one = jnp.exp(earlier[0] - row_top)
    scale_two = jnp.exp(later_part[0] - row_top)
    return (
        row_top,
        earlier[1] * scale_one + later_part[1] * scale_two,
        earlier[2] * scale_one[..., None] + later_part[2] * scale_two[..., None],
    )


def latent_grads(
    query_all, key_all, value_all, dout_all, result_all, row_lse, query_images, key_images, kv_local
):
    scores, allowed = latent_scores(query_all, key_all, query_images, key_images, kv_local)
    weights = jnp.exp(scores - row_lse[..., None])
    all_rows = query_all.shape[0]
    query_heads = query_all.reshape(all_rows, kv_local, -1, RES_HEAD)
    key_heads = key_all.reshape(key_all.shape[0], kv_local, RES_HEAD)
    value_heads = value_all.reshape(value_all.shape[0], kv_local, RES_HEAD)
    dout_heads = dout_all.reshape(all_rows, kv_local, -1, RES_HEAD)
    result_heads = result_all.reshape(all_rows, kv_local, -1, RES_HEAD)
    row_delta = jnp.sum(dout_heads.astype(jnp.float32) * result_heads, axis=-1).transpose(1, 2, 0)
    dweights = jnp.einsum(
        "qkgd,nkd->kgqn", dout_heads, value_heads, preferred_element_type=jnp.float32
    )
    dscores = (weights * (dweights - row_delta[..., None])).astype(jnp.bfloat16)
    factor_scale = RES_HEAD ** (-0.5)
    dquery = (
        jnp.einsum("kgqn,nkd->qkgd", dscores, key_heads, preferred_element_type=jnp.float32)
        * factor_scale
    )
    dkey = (
        jnp.einsum("kgqn,qkgd->nkd", dscores, query_heads, preferred_element_type=jnp.float32)
        * factor_scale
    )
    dvalue = jnp.einsum(
        "kgqn,qkgd->nkd",
        weights.astype(jnp.bfloat16),
        dout_heads,
        preferred_element_type=jnp.float32,
    )
    return (
        dquery.reshape(all_rows, -1),
        dkey.reshape(key_all.shape[0], -1),
        dvalue.reshape(key_all.shape[0], -1),
    )


def per_device(
    patches,
    latents,
    image_patches,
    span_order,
    vis_gains,
    vis_shifts,
    vis_qkv,
    vis_qv_bias,
    vis_out,
    vis_out_bias,
    vis_fc1,
    vis_fc1_bias,
    vis_fc2,
    proj_gate_up,
    proj_down,
    res_gains,
    res_q,
    res_kv,
    res_out,
    res_gate_up,
    res_down,
    out_grad,
):
    tok_rows = patches.shape[0]
    lat_rows = latents.shape[0]
    position = lax.axis_index("blk")
    cycle_size = lax.axis_size("blk")
    head_local = HEADS // lax.axis_size("tp")
    kv_local = KV_HEADS // lax.axis_size("tp")
    query_ids = span_images(image_patches, span_order[position], tok_rows)
    qkv_full, fc1_full = fetch_cols((vis_qkv, vis_fc1))
    out_full, fc2_full = fetch_rows((vis_out, vis_fc2))
    inputs = patches.astype(jnp.float32)
    normed_one, norm_one_pull = jax.vjp(layer_norm, inputs, vis_gains[0], vis_shifts[0])
    attn_input = normed_one.astype(jnp.bfloat16)
    projected = jnp.einsum("td,dje->tje", attn_input, qkv_full, preferred_element_type=jnp.float32)
    query_rows = (projected[:, 0] + vis_qv_bias[0]).astype(jnp.bfloat16)
    key_rows = projected[:, 1].astype(jnp.bfloat16)
    value_rows = (projected[:, 2] + vis_qv_bias[1]).astype(jnp.bfloat16)
    query_heads = query_rows.reshape(tok_rows, head_local, HEAD_VIS)
    start_state = (
        jnp.full((head_local, tok_rows), -jnp.inf, jnp.float32),
        jnp.zeros((head_local, tok_rows), jnp.float32),
        jnp.zeros((head_local, tok_rows, HEAD_VIS), jnp.float32),
    )

    def cycle_step(step_index, loop_state):
        key_now, value_now, state_in = loop_state
        key_ids = span_images(
            image_patches, span_order[(position - step_index) % cycle_size], tok_rows
        )
        state_in = maybe_attend(state_in, query_heads, key_now, value_now, query_ids, key_ids)
        key_now, value_now = from_behind((key_now, value_now), "blk", 1)
        return (key_now, value_now, state_in)

    key_last, value_last, cycle_state = lax.fori_loop(
        0, cycle_size - 1, cycle_step, (key_rows, value_rows, start_state)
    )
    last_ids = span_images(image_patches, span_order[(position + 1) % cycle_size], tok_rows)
    row_top, weight_sum, weighted = maybe_attend(
        cycle_state, query_heads, key_last, value_last, query_ids, last_ids
    )
    vision_lse = row_top + jnp.log(weight_sum)
    vision_result = (weighted / weight_sum[..., None]).transpose(1, 0, 2).reshape(tok_rows, -1)
    attn_output = vision_result.astype(jnp.bfloat16)
    hidden_one = inputs + over_heads(matmul(attn_output, out_full)) + vis_out_bias[0]
    normed_two, norm_two_pull = jax.vjp(layer_norm, hidden_one, vis_gains[1], vis_shifts[1])
    mlp_input = normed_two.astype(jnp.bfloat16)
    fc1_pre = matmul(mlp_input, fc1_full) + vis_fc1_bias
    fc1_act, gelu_pull = jax.vjp(gelu_tanh, fc1_pre)
    fc1_low = fc1_act.astype(jnp.bfloat16)
    vision_out = hidden_one + over_heads(matmul(fc1_low, fc2_full)) + vis_out_bias[1]
    pgu_full, rq_full, rkv_full = fetch_cols((proj_gate_up, res_q, res_kv))
    pdown_full, rout_full = fetch_rows((proj_down, res_out))
    vision_low = vision_out.astype(jnp.bfloat16)
    gate_up = jnp.einsum("td,dje->tje", vision_low, pgu_full, preferred_element_type=jnp.float32)
    proj_hidden, proj_pull = jax.vjp(swiglu, gate_up[:, 0], gate_up[:, 1])
    proj_low = proj_hidden.astype(jnp.bfloat16)
    context = over_heads(matmul(proj_low, pdown_full))
    context_normed, context_pull = jax.vjp(rms_norm, context, res_gains[0])
    context_low = context_normed.astype(jnp.bfloat16)
    patch_kv = jnp.einsum(
        "td,dje->tje", context_low, rkv_full, preferred_element_type=jnp.float32
    ).astype(jnp.bfloat16)
    latent_in = latents.astype(jnp.float32)
    latent_normed, latent_pull = jax.vjp(rms_norm, latent_in, res_gains[1])
    latent_low = latent_normed.astype(jnp.bfloat16)
    query_own = matmul(latent_low, rq_full).astype(jnp.bfloat16)
    latent_kv = jnp.einsum(
        "td,dje->tje", latent_low, rkv_full, preferred_element_type=jnp.float32
    ).astype(jnp.bfloat16)
    key_all = jnp.concatenate([patch_kv[:, 0], latent_kv[:, 0]], axis=0)
    value_all = jnp.concatenate([patch_kv[:, 1], latent_kv[:, 1]], axis=0)
    latent_images = (
        position * (lat_rows // LATENTS) + jnp.arange(lat_rows, dtype=jnp.int32) // LATENTS
    )
    key_images = jnp.concatenate([query_ids, latent_images])
    query_all = share_rows(query_own)
    all_rows = query_all.shape[0]
    query_images = jnp.arange(all_rows, dtype=jnp.int32) // LATENTS
    partial_value = latent_partial(
        query_all, key_all, value_all, query_images, key_images, kv_local
    )
    merged_top, merged_sum, merged_weighted = joined(partial_value, "blk", merge_parts)
    latent_lse = merged_top + jnp.log(merged_sum)
    latent_result = (
        (merged_weighted / merged_sum[..., None]).transpose(2, 0, 1, 3).reshape(all_rows, -1)
    )
    own_low = lax.dynamic_slice_in_dim(latent_result, position * lat_rows, lat_rows, 0).astype(
        jnp.bfloat16
    )
    latent_one = latent_in + over_heads(matmul(own_low, rout_full))
    post_normed, post_pull = jax.vjp(rms_norm, latent_one, res_gains[2])
    post_all = share_rows(post_normed.astype(jnp.bfloat16))
    gate_up_two = jnp.einsum(
        "td,dje->tje", post_all, res_gate_up, preferred_element_type=jnp.float32
    )
    mlp_hidden, mlp_pull = jax.vjp(swiglu, gate_up_two[:, 0], gate_up_two[:, 1])
    mlp_low = mlp_hidden.astype(jnp.bfloat16)

    def down_rows(row_start, row_count):
        return matmul(mlp_low, res_down)

    latent_two = latent_one + over_heads(sum_rows(down_rows, lat_rows))
    final_normed, final_pull = jax.vjp(rms_norm, latent_two, res_gains[3])
    pgu_back, rq_back, rkv_back = fetch_cols((proj_gate_up, res_q, res_kv))
    pdown_back, rout_back = fetch_rows((proj_down, res_out))
    dlatent_two, gain_final = final_pull(out_grad.astype(jnp.float32))
    dmlp_all = share_rows(dlatent_two.astype(jnp.bfloat16))
    grad_res_down = dot_outer(mlp_low, dmlp_all)
    dgate_two, dup_two = mlp_pull(dot_inner(dmlp_all, res_down))
    dgate_up_two = jnp.stack([dgate_two, dup_two], axis=1).astype(jnp.bfloat16)
    grad_res_gate_up = jnp.einsum(
        "td,tje->dje", post_all, dgate_up_two, preferred_element_type=jnp.float32
    )

    def post_rows(row_start, row_count):
        return jnp.einsum(
            "tje,dje->td", dgate_up_two, res_gate_up, preferred_element_type=jnp.float32
        )

    dpost = over_heads(sum_rows(post_rows, lat_rows))
    dlatent_part, gain_post = post_pull(dpost)
    dlatent_one = dlatent_two + dlatent_part
    dattn_low = dlatent_one.astype(jnp.bfloat16)
    grad_res_out = dot_outer(own_low, dattn_low)
    dresult_all = share_rows(dot_inner(dattn_low, rout_back).astype(jnp.bfloat16))
    dquery_all, dkey_all, dvalue_all = latent_grads(
        query_all,
        key_all,
        value_all,
        dresult_all,
        latent_result,
        latent_lse,
        query_images,
        key_images,
        kv_local,
    )

    def query_grad_rows(row_start, row_count):
        return dquery_all

    dquery_own = sum_rows(query_grad_rows, lat_rows).astype(jnp.bfloat16)
    dkey_low = dkey_all.astype(jnp.bfloat16)
    dvalue_low = dvalue_all.astype(jnp.bfloat16)
    dpatch_kv = jnp.stack([dkey_low[:tok_rows], dvalue_low[:tok_rows]], axis=1)
    dlatent_kv = jnp.stack([dkey_low[tok_rows:], dvalue_low[tok_rows:]], axis=1)
    grad_res_q = dot_outer(latent_low, dquery_own)
    grad_res_kv = jnp.einsum(
        "td,tje->dje", context_low, dpatch_kv, preferred_element_type=jnp.float32
    ) + jnp.einsum("td,tje->dje", latent_low, dlatent_kv, preferred_element_type=jnp.float32)
    dlatent_normed, dcontext_normed = over_heads(
        (
            dot_inner(dquery_own, rq_back)
            + jnp.einsum("tje,dje->td", dlatent_kv, rkv_back, preferred_element_type=jnp.float32),
            jnp.einsum("tje,dje->td", dpatch_kv, rkv_back, preferred_element_type=jnp.float32),
        )
    )
    dlatent_in, gain_latent = latent_pull(dlatent_normed)
    latents_grad = dlatent_one + dlatent_in
    dcontext, gain_context = context_pull(dcontext_normed)
    grad_res_q, grad_res_kv = return_cols((grad_res_q, grad_res_kv))
    grad_res_out = return_rows(grad_res_out)
    dcontext_low = dcontext.astype(jnp.bfloat16)
    grad_proj_down = dot_outer(proj_low, dcontext_low)
    dproj_gate, dproj_up = proj_pull(dot_inner(dcontext_low, pdown_back))
    dproj_gate_up = jnp.stack([dproj_gate, dproj_up], axis=1).astype(jnp.bfloat16)
    grad_proj_gate_up = jnp.einsum(
        "td,tje->dje", vision_low, dproj_gate_up, preferred_element_type=jnp.float32
    )
    dvision_out = over_heads(
        jnp.einsum("tje,dje->td", dproj_gate_up, pgu_back, preferred_element_type=jnp.float32)
    )
    grad_proj_gate_up = return_cols(grad_proj_gate_up)
    grad_proj_down = return_rows(grad_proj_down)
    qkv_back, fc1_back = fetch_cols((vis_qkv, vis_fc1))
    out_back, fc2_back = fetch_rows((vis_out, vis_fc2))
    dfc2_low = dvision_out.astype(jnp.bfloat16)
    bias_two = jnp.sum(dfc2_low.astype(jnp.float32), axis=0)
    grad_vis_fc2 = dot_outer(fc1_low, dfc2_low)
    (dfc1_pre,) = gelu_pull(dot_inner(dfc2_low, fc2_back))
    dfc1_low = dfc1_pre.astype(jnp.bfloat16)
    bias_fc1 = jnp.sum(dfc1_low.astype(jnp.float32), axis=0)
    grad_vis_fc1 = dot_outer(mlp_input, dfc1_low)
    dnormed_two = over_heads(dot_inner(dfc1_low, fc1_back))
    dhidden_part, gain_two, shift_two = norm_two_pull(dnormed_two)
    dhidden_one = dvision_out + dhidden_part
    dattn_total = dhidden_one.astype(jnp.bfloat16)
    bias_one = jnp.sum(dattn_total.astype(jnp.float32), axis=0)
    grad_vis_out = dot_outer(attn_output, dattn_total)
    dattn_output = dot_inner(dattn_total, out_back).astype(jnp.bfloat16)
    dout_heads = dattn_output.reshape(tok_rows, head_local, HEAD_VIS)
    vision_delta = jnp.sum(
        (dattn_output.astype(jnp.float32) * vision_result).reshape(tok_rows, head_local, HEAD_VIS),
        axis=-1,
    ).T
    zero_heads = jnp.zeros((tok_rows, head_local, HEAD_VIS), jnp.float32)

    def back_step(step_index, loop_state):
        key_now, value_now, dkey, dvalue, dquery = loop_state
        key_ids = span_images(
            image_patches, span_order[(position - step_index) % cycle_size], tok_rows
        )
        part_query, part_key, part_value = maybe_grads(
            query_heads,
            key_now,
            value_now,
            dout_heads,
            vision_lse,
            vision_delta,
            query_ids,
            key_ids,
        )
        dkey, dvalue = pass_grads((dkey + part_key, dvalue + part_value))
        key_now, value_now = from_behind((key_now, value_now), "blk", 1)
        return (key_now, value_now, dkey, dvalue, dquery + part_query)

    key_last, value_last, dkey_cycle, dvalue_cycle, dquery_cycle = lax.fori_loop(
        0, cycle_size - 1, back_step, (key_rows, value_rows, zero_heads, zero_heads, zero_heads)
    )
    part_query, part_key, part_value = maybe_grads(
        query_heads, key_last, value_last, dout_heads, vision_lse, vision_delta, query_ids, last_ids
    )
    dkey_home, dvalue_home = pass_grads((dkey_cycle + part_key, dvalue_cycle + part_value))
    dquery_home = dquery_cycle + part_query
    dqkv_low = jnp.stack(
        [
            dquery_home.reshape(tok_rows, -1),
            dkey_home.reshape(tok_rows, -1),
            dvalue_home.reshape(tok_rows, -1),
        ],
        axis=1,
    ).astype(jnp.bfloat16)
    bias_qv = jnp.stack(
        [
            jnp.sum(dqkv_low[:, 0].astype(jnp.float32), axis=0),
            jnp.sum(dqkv_low[:, 2].astype(jnp.float32), axis=0),
        ]
    )
    grad_vis_qkv = jnp.einsum(
        "td,tje->dje", attn_input, dqkv_low, preferred_element_type=jnp.float32
    )
    dnormed_one = over_heads(
        jnp.einsum("tje,dje->td", dqkv_low, qkv_back, preferred_element_type=jnp.float32)
    )
    dinput_part, gain_one, shift_one = norm_one_pull(dnormed_one)
    patches_grad = dhidden_one + dinput_part
    grad_vis_qkv, grad_vis_fc1 = return_cols((grad_vis_qkv, grad_vis_fc1))
    grad_vis_out, grad_vis_fc2 = return_rows((grad_vis_out, grad_vis_fc2))
    small_sums = lax.psum(
        (
            jnp.stack([gain_one, gain_two]),
            jnp.stack([shift_one, shift_two]),
            bias_qv,
            jnp.stack([bias_one, bias_two]),
            bias_fc1,
            jnp.stack([gain_context, gain_latent, gain_post, gain_final]),
        ),
        "blk",
    )
    (
        grad_vis_gains,
        grad_vis_shifts,
        grad_vis_qv_bias,
        grad_vis_out_bias,
        grad_vis_fc1_bias,
        grad_res_gains,
    ) = small_sums
    return (
        final_normed,
        patches_grad,
        latents_grad,
        grad_vis_gains,
        grad_vis_shifts,
        grad_vis_qkv,
        grad_vis_qv_bias,
        grad_vis_out,
        grad_vis_out_bias,
        grad_vis_fc1,
        grad_vis_fc1_bias,
        grad_vis_fc2,
        grad_proj_gate_up,
        grad_proj_down,
        grad_res_gains,
        grad_res_q,
        grad_res_kv,
        grad_res_out,
        grad_res_gate_up,
        grad_res_down,
    )


def solution(mesh):
    placed = (
        P("blk", None),
        P("blk", None),
        P(),
        P(),
        P(),
        P(),
        P("blk", None, "tp"),
        P(None, "tp"),
        P("tp", "blk"),
        P(),
        P("blk", "tp"),
        P("tp"),
        P("tp", "blk"),
        P("blk", None, "tp"),
        P("tp", "blk"),
        P(),
        P("blk", "tp"),
        P("blk", None, "tp"),
        P("tp", "blk"),
        P(None, None, ("blk", "tp")),
        P(("blk", "tp"), None),
        P("blk", None),
    )
    return jax.shard_map(
        per_device,
        mesh=mesh,
        in_specs=placed,
        out_specs=(
            P("blk", None),
            P("blk", None),
            P("blk", None),
            P(),
            P(),
            P("blk", None, "tp"),
            P(None, "tp"),
            P("tp", "blk"),
            P(),
            P("blk", "tp"),
            P("tp"),
            P("tp", "blk"),
            P("blk", None, "tp"),
            P("tp", "blk"),
            P(),
            P("blk", "tp"),
            P("blk", None, "tp"),
            P("tp", "blk"),
            P(None, None, ("blk", "tp")),
            P(("blk", "tp"), None),
        ),
        check_vma=False,
    )
```

profile of v0, /device:TPU:0, one launch (start us, length us, event | category | flops | bytes accessed | tf_op | source)
XLA Modules:
  0.0 4774.8 jit_solution(12671063202276791964)
XLA Ops:
  17.0 35.7 all_gather.65
  52.7 21.2 all-gather.15.cloned.1.call-done
  80.0 57.3 %while.68 = (s32[]{:T(128)}, bf16[128,288]{0,1:T(8,128)(2,1)S(1)}, bf16[128,288]{0,1:T(8,128)(2,1)S(1)}, f32[4,128]{1,0:T(4,128)S(1)}, f32[4,128]{1,0:T(4,128)S(...) while((s32[]{:T(128)}, bf16[128,288]{0,1:T(8,128)(2,1)S(1)}, ...), condition=%wide.region_9.10_spmd.clone, body=%wide.region_5.0_spmd.clone.sunk | while | flops 19465748 | bytes 2255816 | solution.py:319
  141.8 30.5 all-reduce.14.cloned.1.call-done
  173.7 55.7 %all-gather.17.cloned.1.call-done = bf16[1152,1076]{1,0:T(8,128)(2,1)} async-done(((bf16[144,1076]{1,0:T(8,128)(2,1)}), bf16[1152,1076]{1,0:T(8,128)(2,1)}) %all-gather.17.cloned.1.call-update) | async-done | bytes 2479120 | tf_op jit(solution)/shard_map/all_gather | solution.py:77
  232.4 52.7 %all-gather.19.cloned.1.call-done = bf16[1076,1152]{0,1:T(8,128)(2,1)} async-done(((bf16[1076,144]{0,1:T(8,128)(2,1)}), bf16[1076,1152]{0,1:T(8,128)(2,1)}) %all-gather.19.cloned.1.call-update) | async-done | bytes 2479120 | tf_op jit(solution)/shard_map/all_gather | solution.py:85
  295.6 25.4 all-reduce.16.cloned.1.call-done
  322.1 225.9 %all-gather.21.cloned.1.call-done = bf16[1152,2,3584]{2,0,1:T(8,128)(2,1)} async-done(((bf16[144,2,3584]{2,0,1:T(8,128)(2,1)}), bf16[1152,2,3584]{2,0,1:T(8,128)(2,1)}) %all-gather.21.cloned.1.call-update) | async-done | bytes 16515088 | tf_op jit(solution)/shard_map/all_gather | solution.py:77
  558.7 548.2 %all-gather.23.cloned.1.call-done = bf16[3584,4096]{1,0:T(8,128)(2,1)} async-done(((bf16[3584,512]{1,0:T(8,128)(2,1)}), bf16[3584,4096]{1,0:T(8,128)(2,1)}) %all-gather.23.cloned.1.call-update) | async-done | bytes 29360144 | tf_op jit(solution)/shard_map/all_gather | solution.py:84
  1106.9 12.9 fusion.186
  1119.9 34.3 all-gather.25.cloned.1.call-done
  1156.3 58.8 %all-gather.27.cloned.1.call-done = bf16[4096,384]{1,0:T(8,128)(2,1)} async-done(((bf16[512,384]{1,0:T(8,128)(2,1)}), bf16[4096,384]{1,0:T(8,128)(2,1)}) %all-gather.27.cloned.1.call-update) | async-done | bytes 3145744 | tf_op jit(solution)/shard_map/all_gather | solution.py:77
  1217.8 31.2 all_gather.72
  1249.2 18.7 all-reduce.18.cloned.1.call-done
  1273.7 33.0 all_gather.73
  1307.4 32.9 all-gather.2
  1341.0 32.3 all-gather.35.cloned.1.call-done
  1374.8 27.4 while.67
  1402.7 34.0 all-gather.29.cloned.1.call-done
  1440.4 34.4 all-reduce.20.cloned.1.call-done
  1477.8 73.4 %all-gather.31.cloned.1.call-done = bf16[512,4096]{1,0:T(8,128)(2,1)} async-done(((bf16[64,4096]{1,0:T(8,128)(2,1)}), bf16[512,4096]{1,0:T(8,128)(2,1)}) %all-gather.31.cloned.1.call-update) | async-done | bytes 4194320 | tf_op jit(solution)/shard_map/all_gather | solution.py:102
  1567.1 147.4 %reduce-scatter.15.cloned.1.call-done = f32[64,4096]{1,0:T(8,128)} async-done(((f32[512,4096]{1,0:T(8,128)}), f32[64,4096]{1,0:T(8,128)}) %reduce-scatter.15.cloned.1.call-update) | async-done | bytes 1048592 | tf_op jit(solution)/shard_map/reduce_scatter | solution.py:106
  1714.6 37.4 all-reduce.22.cloned.1.call-done
  1758.1 73.9 %all-gather.33.cloned.1.call-done = bf16[512,4096]{1,0:T(8,128)(2,1)} async-done(((bf16[64,4096]{1,0:T(8,128)(2,1)}), bf16[512,4096]{1,0:T(8,128)(2,1)}) %all-gather.33.cloned.1.call-update) | async-done | bytes 4194320 | tf_op jit(solution)/shard_map/all_gather | solution.py:102
  1849.8 147.4 %reduce-scatter.17.cloned.1.call-done = f32[64,4096]{1,0:T(8,128)} async-done(((f32[512,4096]{1,0:T(8,128)}), f32[64,4096]{1,0:T(8,128)}) %reduce-scatter.17.cloned.1.call-update) | async-done | bytes 1048592 | tf_op jit(solution)/shard_map/reduce_scatter | solution.py:106
  1997.9 36.9 all-reduce.24.cloned.1.call-done
  2040.7 31.5 all_gather.81
  2080.3 51.8 %all-reduce.26.cloned.1.call-done = f32[128,4096]{1,0:T(8,128)} async-done(((f32[128,4096]{1,0:T(8,128)}), f32[128,4096]{1,0:T(8,128)}) %all-reduce.26.cloned.1.call-update) | async-done | bytes 2097168 | tf_op jit(solution)/shard_map/psum | solution.py:98
  2137.2 16.7 fusion.79
  2173.5 26.4 all-reduce.28.cloned.1.call-done
  2206.8 59.9 %reduce-scatter.37.cloned.1.call-done = f32[64,384]{1,0:T(8,128)} async-done(((f32[512,384]{1,0:T(8,128)}), f32[64,384]{1,0:T(8,128)}) %reduce-scatter.37.cloned.1.call-update) | async-done | bytes 98320
  2272.1 30.0 all-reduce.30.cloned.1.call-done
  2309.8 153.6 %while.69 = (s32[]{:T(128)}, bf16[128,288]{0,1:T(8,128)(2,1)}, bf16[128,288]{0,1:T(8,128)(2,1)}, f32[128,4,72]{0,2,1:T(8,128)}, f32[128,4,72]{0,2,1:T(8,128)}, /...) while((s32[]{:T(128)}, bf16[128,288]{0,1:T(8,128)(2,1)}, ...), condition=%wide.region_43.44_spmd.clone, body=%wide.region_41.43_spmd.clone.sunk | while | flops 47885328 | bytes 4685010 | solution.py:501
  2479.4 14.0 fusion.47
  2493.5 27.9 all-reduce.34.cloned.1.call-done
  2556.4 24.9 fusion.190
  2588.9 32.2 copy.144
  2631.5 41.0 all-reduce
  2675.0 385.8 %reduce-scatter.27.cloned.1.call-done = f32[144,2,3584]{2,0,1:T(8,128)} async-done(((f32[1152,2,3584]{2,0,1:T(8,128)}), f32[144,2,3584]{2,0,1:T(8,128)}) %reduce-scatter.27.cloned.1.call-update) | async-done | bytes 4128784 | tf_op jit(solution)/shard_map/reduce_scatter | solution.py:90
  3068.2 64.5 %all-reduce.32.cloned.1.call-done = f32[4,4096]{1,0:T(4,128)} async-done(((f32[4,4096]{1,0:T(4,128)}), f32[4,4096]{1,0:T(4,128)}) %all-reduce.32.cloned.1.call-update) | async-done | bytes 65552 | tf_op jit(solution)/shard_map/psum | solution.py:533
  3132.7 70.3 %reduce-scatter.21.cloned.1.call-done = f32[288,144]{0,1:T(8,128)} async-done(((f32[288,1152]{0,1:T(8,128)}), f32[288,144]{0,1:T(8,128)}) %reduce-scatter.21.cloned.1.call-update) | async-done | bytes 165904 | tf_op jit(solution)/shard_map/reduce_scatter | solution.py:94
  3203.0 78.2 %reduce-scatter.33.cloned.1.call-done = f32[512,2,96]{0,2,1:T(8,128)} async-done(((f32[4096,2,96]{0,2,1:T(8,128)}), f32[512,2,96]{0,2,1:T(8,128)}) %reduce-scatter.33.cloned.1.call-update) | async-done | bytes 393232 | tf_op jit(solution)/shard_map/reduce_scatter | solution.py:90
  3281.2 107.5 %reduce-scatter.19.cloned.1.call-done = f32[144,3,288]{2,0,1:T(8,128)} async-done(((f32[1152,3,288]{2,0,1:T(8,128)}), f32[144,3,288]{2,0,1:T(8,128)}) %reduce-scatter.19.cloned.1.call-update) | async-done | bytes 497680 | tf_op jit(solution)/shard_map/reduce_scatter | solution.py:90
  3388.7 108.4 %reduce-scatter.23.cloned.1.call-done = f32[144,1076]{1,0:T(8,128)} async-done(((f32[1152,1076]{1,0:T(8,128)}), f32[144,1076]{1,0:T(8,128)}) %reduce-scatter.23.cloned.1.call-update) | async-done | bytes 619792 | tf_op jit(solution)/shard_map/reduce_scatter | solution.py:90
  3497.1 108.2 %reduce-scatter.25.cloned.1.call-done = f32[1076,144]{0,1:T(8,128)} async-done(((f32[1076,1152]{0,1:T(8,128)}), f32[1076,144]{0,1:T(8,128)}) %reduce-scatter.25.cloned.1.call-update) | async-done | bytes 619792 | tf_op jit(solution)/shard_map/reduce_scatter | solution.py:94
  3605.3 122.7 %reduce-scatter.35.cloned.1.call-done = f32[384,512]{1,0:T(8,128)} async-done(((f32[384,4096]{1,0:T(8,128)}), f32[384,512]{1,0:T(8,128)}) %reduce-scatter.35.cloned.1.call-update) | async-done | bytes 786448 | tf_op jit(solution)/shard_map/reduce_scatter | solution.py:94
  3728.0 121.5 %reduce-scatter.31.cloned.1.call-done = f32[512,384]{1,0:T(8,128)} async-done(((f32[4096,384]{1,0:T(8,128)}), f32[512,384]{1,0:T(8,128)}) %reduce-scatter.31.cloned.1.call-update) | async-done | bytes 786448 | tf_op jit(solution)/shard_map/reduce_scatter | solution.py:90
  3849.6 916.8 %reduce-scatter.29.cloned.1.call-done = f32[3584,512]{1,0:T(8,128)} async-done(((f32[3584,4096]{1,0:T(8,128)}), f32[3584,512]{1,0:T(8,128)}) %reduce-scatter.29.cloned.1.call-update) | async-done | bytes 7340048 | tf_op jit(solution)/shard_map/reduce_scatter | solution.py:94
  (808 shorter events, 472.2 us)
Async XLA Ops:
  7.2 66.7 %all-gather.15.cloned.1.call-start = ((), (), s32[]{:S(2)}) async-start(), calls=%async_computation.12 | async-start | bytes 2985984 | tf_op jit(solution)/shard_map/all_gather | solution.py:77
  7.9 164.3 %all-reduce.14.cloned.1.call-start = ((), (), s32[]{:S(2)}) async-start(), calls=%async_computation.13 | async-start | bytes 1179648 | tf_op jit(solution)/shard_map/psum | solution.py:98
  140.4 89.1 %all-gather.17.cloned.1.call-start = ((), (), s32[]{:S(2)}) async-start(), calls=%async_computation.14 | async-start | bytes 2985984 | tf_op jit(solution)/shard_map/all_gather | solution.py:77
  141.1 144.0 %all-gather.19.cloned.1.call-start = ((), (), s32[]{:S(2)}) async-start(), calls=%async_computation.15 | async-start | bytes 2985984 | tf_op jit(solution)/shard_map/all_gather | solution.py:85
  141.7 179.3 %all-reduce.16.cloned.1.call-start = ((), (), s32[]{:S(2)}) async-start(), calls=%async_computation.16 | async-start | bytes 1179648 | tf_op jit(solution)/shard_map/psum | solution.py:98
  288.7 259.3 %all-gather.21.cloned.1.call-start = ((), (), s32[]{:S(2)}) async-start(), calls=%async_computation.17 | async-start | bytes 18579456 | tf_op jit(solution)/shard_map/all_gather | solution.py:77
  291.9 815.0 %all-gather.23.cloned.1.call-start = ((), (), s32[]{:S(2)}) async-start(), calls=%async_computation.18 | async-start | bytes 33030144 | tf_op jit(solution)/shard_map/all_gather | solution.py:84
  292.7 861.6 %all-gather.25.cloned.1.call-start = ((), (), s32[]{:S(2)}) async-start(), calls=%async_computation.20 | async-start | bytes 1769472 | tf_op jit(solution)/shard_map/all_gather | solution.py:77
  293.4 921.7 %all-gather.27.cloned.1.call-start = ((), (), s32[]{:S(2)}) async-start(), calls=%async_computation.21 | async-start | bytes 3538944 | tf_op jit(solution)/shard_map/all_gather | solution.py:77
  294.2 973.8 %all-reduce.18.cloned.1.call-start = ((), (), s32[]{:S(2)}) async-start(), calls=%async_computation.19 | async-start | bytes 4194304 | tf_op jit(solution)/shard_map/psum | solution.py:98
  1119.9 253.4 %all-gather.35.cloned.1.call-start = ((), (), s32[]{:S(2)}) async-start(), calls=%async_computation.43 | async-start | bytes 7077888 | tf_op jit(solution)/shard_map/all_gather | solution.py:31
  1272.8 163.9 %all-gather.29.cloned.1.call-start = ((), (), s32[]{:S(2)}) async-start(), calls=%async_computation.22 | async-start | bytes 3538944 | tf_op jit(solution)/shard_map/all_gather | solution.py:85
  1273.4 201.3 %all-reduce.20.cloned.1.call-start = ((), (), s32[]{:S(2)}) async-start(), calls=%async_computation.23 | async-start | bytes 2097152 | tf_op jit(solution)/shard_map/psum | solution.py:98
  1440.3 110.9 %all-gather.31.cloned.1.call-start = ((), (), s32[]{:S(2)}) async-start(), calls=%async_computation.24 | async-start | bytes 4718592 | tf_op jit(solution)/shard_map/all_gather | solution.py:102
  1477.2 237.3 %reduce-scatter.15.cloned.1.call-start = ((), (), s32[]{:S(2)}) async-start(), calls=%async_computation.25 | async-start | bytes 9437184 | tf_op jit(solution)/shard_map/reduce_scatter | solution.py:106
  1567.1 184.9 %all-reduce.22.cloned.1.call-start = ((), (), s32[]{:S(2)}) async-start(), calls=%async_computation.26 | async-start | bytes 2097152 | tf_op jit(solution)/shard_map/psum | solution.py:98
  1714.5 117.4 %all-gather.33.cloned.1.call-start = ((), (), s32[]{:S(2)}) async-start(), calls=%async_computation.27 | async-start | bytes 4718592 | tf_op jit(solution)/shard_map/all_gather | solution.py:102
  1758.0 239.2 %reduce-scatter.17.cloned.1.call-start = ((), (), s32[]{:S(2)}) async-start(), calls=%async_computation.28 | async-start | bytes 9437184 | tf_op jit(solution)/shard_map/reduce_scatter | solution.py:106
  1849.8 185.0 %all-reduce.24.cloned.1.call-start = ((), (), s32[]{:S(2)}) async-start(), calls=%async_computation.29 | async-start | bytes 2097152 | tf_op jit(solution)/shard_map/psum | solution.py:98
  1997.2 134.9 %all-reduce.26.cloned.1.call-start = ((), (), s32[]{:S(2)}) async-start(), calls=%async_computation.30 | async-start | bytes 4194304 | tf_op jit(solution)/shard_map/psum | solution.py:98
  2080.3 119.7 %all-reduce.28.cloned.1.call-start = ((), (), s32[]{:S(2)}) async-start(), calls=%async_computation.31 | async-start | bytes 1179648 | tf_op jit(solution)/shard_map/psum | solution.py:98
  2166.2 100.5 %reduce-scatter.37.cloned.1.call-start = ((), (), s32[]{:S(2)}) async-start(), calls=%async_computation.44 | async-start | bytes 884736
  2170.5 131.6 %all-reduce.30.cloned.1.call-start = ((), (), s32[]{:S(2)}) async-start(), calls=%async_computation.32 | async-start | bytes 1179648 | tf_op jit(solution)/shard_map/psum | solution.py:98
  2206.5 314.9 %all-reduce.34.cloned.1.call-start = ((), (), s32[]{:S(2)}) async-start(), calls=%async_computation.45 | async-start | bytes 3276800 | tf_op jit(solution)/shard_map/psum | solution.py:98
  2311.3 17.1 collective-permute-start.2
  2314.3 14.1 collective-permute-start.3
  2334.8 15.3 collective-permute-start.2
  2336.3 13.8 collective-permute-start.3
  2355.6 15.1 collective-permute-start.2
  2357.2 13.6 collective-permute-start.3
  2376.4 15.3 collective-permute-start.2
  2377.9 13.8 collective-permute-start.3
  2399.8 12.5 collective-permute-start.2
  2401.3 11.0 collective-permute-start.3
  2419.2 16.6 collective-permute-start.2
  2420.7 15.0 collective-permute-start.3
  2440.2 17.7 collective-permute-start.2
  2443.2 14.7 collective-permute-start.3
  2479.3 581.5 %reduce-scatter.27.cloned.1.call-start = ((), (), s32[]{:S(2)}) async-start(), calls=%async_computation.37 | async-start | bytes 37158912 | tf_op jit(solution)/shard_map/reduce_scatter | solution.py:90
  2493.5 639.2 %all-reduce.32.cloned.1.call-start = ((), (), s32[]{:S(2)}) async-start(), calls=%async_computation.39 | async-start | bytes 131072 | tf_op jit(solution)/shard_map/psum | solution.py:533
  2525.0 678.0 %reduce-scatter.21.cloned.1.call-start = ((), (), s32[]{:S(2)}) async-start(), calls=%async_computation.34 | async-start | bytes 1990656 | tf_op jit(solution)/shard_map/reduce_scatter | solution.py:94
  2527.6 753.5 %reduce-scatter.33.cloned.1.call-start = ((), (), s32[]{:S(2)}) async-start(), calls=%async_computation.41 | async-start | bytes 3538944 | tf_op jit(solution)/shard_map/reduce_scatter | solution.py:90
  2531.6 857.1 %reduce-scatter.19.cloned.1.call-start = ((), (), s32[]{:S(2)}) async-start(), calls=%async_computation.33 | async-start | bytes 5971968 | tf_op jit(solution)/shard_map/reduce_scatter | solution.py:90
  2536.0 961.2 %reduce-scatter.23.cloned.1.call-start = ((), (), s32[]{:S(2)}) async-start(), calls=%async_computation.35 | async-start | bytes 5971968 | tf_op jit(solution)/shard_map/reduce_scatter | solution.py:90
  2540.3 1065.0 %reduce-scatter.25.cloned.1.call-start = ((), (), s32[]{:S(2)}) async-start(), calls=%async_computation.36 | async-start | bytes 5971968 | tf_op jit(solution)/shard_map/reduce_scatter | solution.py:94
  2544.7 1183.3 %reduce-scatter.35.cloned.1.call-start = ((), (), s32[]{:S(2)}) async-start(), calls=%async_computation.42 | async-start | bytes 7077888 | tf_op jit(solution)/shard_map/reduce_scatter | solution.py:94
  2550.6 1299.0 %reduce-scatter.31.cloned.1.call-start = ((), (), s32[]{:S(2)}) async-start(), calls=%async_computation.40 | async-start | bytes 7077888 | tf_op jit(solution)/shard_map/reduce_scatter | solution.py:90
  2555.2 2211.1 %reduce-scatter.29.cloned.1.call-start = ((), (), s32[]{:S(2)}) async-start(), calls=%async_computation.38 | async-start | bytes 66060288 | tf_op jit(solution)/shard_map/reduce_scatter | solution.py:94
  (174 other events, 5127.9 us)
Sparse Core Ops, SparseCore 0:
  10.3 63.5 all-gather.14
  140.5 31.7 all-reduce.13
  174.4 55.0 all-gather.16
  231.5 53.5 all-gather.18
  288.8 32.0 all-reduce.15
  323.6 224.3 all-gather.20
  549.6 557.2 all-gather.22
  1108.9 45.2 all-gather.24
  1156.4 58.6 all-gather.26
  1217.9 49.9 all-reduce.17
  1272.9 100.3 all-gather.34
  1375.4 61.2 all-gather.28
  1440.4 34.2 all-reduce.19
  1477.4 73.7 all-gather.30
  1567.2 147.2 reduce-scatter.14
  1716.9 35.0 all-reduce.21
  1758.2 73.7 all-gather.32
  1849.9 147.2 reduce-scatter.16
  1999.7 35.0 all-reduce.23
  2080.4 51.7 all-reduce.25
  2166.3 33.5 all-reduce.27
  2204.2 62.5 reduce-scatter.36
  2269.7 32.4 all-reduce.29
  2479.5 41.8 all-reduce.33
  2525.9 534.9 reduce-scatter.26
  3065.0 67.5 all-reduce.31
  3137.0 65.9 reduce-scatter.20
  3207.1 73.9 reduce-scatter.32
  3285.4 103.3 reduce-scatter.18
  3393.2 103.9 reduce-scatter.22
  3501.3 103.9 reduce-scatter.24
  3609.9 118.0 reduce-scatter.34
  3732.5 117.0 reduce-scatter.30
  3854.5 911.7 reduce-scatter.28
where the time goes:
time: 4790 us; the launch traced here: 4770 us
  waiting for transfers between devices  4050 us (85%)
  matrix products  267 us (6%)
  blocking collectives  205 us (4%)
  local copies, waits for them, and re-layouts  125 us (3%)
  other arithmetic  60.2 us (1%)
    reduce_scatter x4, waiting for transfers between devices, return_rows(): return lax.psum_scatter(gradients, 'blk', scatter_dimension=1, tiled=True)  1220 us
    reduce_scatter x5, waiting for transfers between devices, return_cols(): return lax.psum_scatter(gradients, 'blk', scatter_dimension=0, tiled=True)  802 us
    all_gather x1, waiting for transfers between devices, fetch_rows(): lax.all_gather(shards[0], 'blk', axis=1, tiled=True)  548 us
    all_gather x5, waiting for transfers between devices, fetch_cols(): lax.all_gather(as_sent(shards), 'blk', axis=0, tiled=True)  396 us
    psum x10, waiting for transfers between devices, over_heads(): return lax.psum(partial_value, 'tp')  319 us
    reduce_scatter x2, waiting for transfers between devices, sum_rows(): lax.psum_scatter(row_term(jnp.int32(0), lax.axis_size('blk') * row_total)...  295 us
    all_gather x2, waiting for transfers between devices, share_rows(): return lax.all_gather(rows_low, 'blk', axis=0, tiled=True)  147 us
  transfers between devices with their start and end apart: 78, of which 64 were waited for; matrix products, arithmetic and copies ran while one was open for 6% of the time, Pallas kernels for 0%

commit v1 on v0

v1 whole, which is shorter than its diff:
```python
import jax
import jax.numpy as jnp
from jax import lax
from jax.sharding import PartitionSpec as P

HEADS = 16
HEAD_VIS = 72
RES_HEAD = 96
LATENTS = 64
EPSILON = 1e-06
EVERY = ("blk", "tp")
BF = jnp.bfloat16
F32 = jnp.float32


def swap_core(value):
    return lax.ppermute(value, "tp", [(i, i ^ 1) for i in range(lax.axis_size("tp"))])


def swap_x(value):
    return lax.ppermute(value, "tp", [(i, i ^ 2) for i in range(lax.axis_size("tp"))])


def my_x():
    return lax.axis_index("tp") // 2


def my_core():
    return lax.axis_index("tp") % 2


def pick(flag, one, zero):
    return jnp.where(flag == 1, one, zero)


def exchange(chunks, axis):
    return lax.all_to_all(chunks, axis, 0, 0, tiled=True)


def gather_direct(value, axis, count):
    return exchange(jnp.broadcast_to(value[None], (count,) + value.shape), axis)


def sum_blk(partial):
    return jnp.sum(exchange(partial.astype(BF), "blk").astype(F32), axis=0)


def sum_tp_quarter(partial):
    pairs = partial.reshape((2, 2) + partial.shape[1:])
    core, x = my_core(), my_x()
    keep = pick(core, pairs[:, 1], pairs[:, 0])
    send = pick(core, pairs[:, 0], pairs[:, 1]).astype(BF)
    half = keep + swap_core(send).astype(F32)
    keep = pick(x, half[1], half[0])
    send = pick(x, half[0], half[1]).astype(BF)
    return keep + swap_x(send).astype(F32)


def gather_tp(value):
    other = swap_x(value)
    x, core = my_x(), my_core()
    both = pick(x, jnp.stack([other, value]), jnp.stack([value, other]))
    far = swap_core(both)
    quad = pick(core, jnp.stack([far, both], axis=1), jnp.stack([both, far], axis=1))
    return quad.reshape((4,) + value.shape)


def sum_tp(partial):
    chip = (partial + swap_core(partial)).astype(BF)
    return chip.astype(F32) + swap_x(chip).astype(F32)


def gather_blk(value):
    return gather_direct(value, "blk", lax.axis_size("blk"))


def gather_blk_later(value):
    return lax.all_gather(value, "blk", axis=0, tiled=False)


def gather_every(value):
    return gather_tp(gather_blk(value))


def sum_every(partial):
    return sum_blk(sum_tp_quarter(partial))


def sum_small(rows):
    blk, tp = lax.axis_size("blk"), lax.axis_size("tp")
    count = blk * tp
    width = rows.shape[0]
    unit = count * 128
    padded = jnp.pad(rows, (0, (-width) % unit)).reshape(count, -1)
    own = jnp.sum(exchange(padded, EVERY), axis=0)
    return gather_direct(own, EVERY, count).reshape(-1)[:width]


def layer_norm(values, gain, shift):
    center = values - jnp.mean(values, axis=-1, keepdims=True)
    spread = jnp.mean(center * center, axis=-1, keepdims=True)
    return center * lax.rsqrt(spread + EPSILON) * gain + shift


def rms_norm(values, gain):
    return values * lax.rsqrt(jnp.mean(values * values, axis=-1, keepdims=True) + EPSILON) * gain


def gelu_tanh(values):
    return jax.nn.gelu(values, approximate=True)


def swiglu(gate_part, up_part):
    return jax.nn.silu(gate_part) * up_part


def mm(spec, left, right):
    return jnp.einsum(spec, left, right, preferred_element_type=F32)


def dot(left, right, on_left, on_right):
    return lax.dot_general(
        left, right, (((on_left,), (on_right,)), ((), ())), preferred_element_type=F32
    )


def halves(value):
    high = lax.reduce_precision(value, 8, 7)
    return high, lax.reduce_precision(value - high, 8, 7)


def stream_images(image_patches, span_order, tok_rows):
    bounds = jnp.cumsum(image_patches)
    rows = span_order[:, None] * tok_rows + jnp.arange(tok_rows, dtype=jnp.int32)[None, :]
    stream = rows.reshape(-1)
    return jnp.sum((stream[:, None] >= bounds[None, :]).astype(jnp.int32), axis=1)


def per_device(
    patches,
    latents,
    image_patches,
    span_order,
    vis_gains,
    vis_shifts,
    vis_qkv,
    vis_qv_bias,
    vis_out,
    vis_out_bias,
    vis_fc1,
    vis_fc1_bias,
    vis_fc2,
    proj_gate_up,
    proj_down,
    res_gains,
    res_q,
    res_kv,
    res_out,
    res_gate_up,
    res_down,
    out_grad,
):
    blk = lax.axis_size("blk")
    b, t = lax.axis_index("blk"), lax.axis_index("tp")
    tok, wide = patches.shape
    lat, text = latents.shape
    sub, lsub = tok // 4, lat // 4
    tokens, lats = tok * blk, lat * blk
    wcol, tcol = wide // blk, text // blk
    heads = HEADS // 4
    unit = proj_down.shape[0] // blk
    hidden = proj_down.shape[0]
    qcols = res_q.shape[1]
    kvcols = RES_HEAD

    qkv_shard = vis_qkv.transpose(1, 0, 2)
    qkv_full = gather_blk_later(qkv_shard)
    qkv_full = qkv_full.transpose(1, 0, 2, 3).reshape(3, wide, -1)
    gu_chunks = proj_gate_up.reshape(wcol, 2, blk, unit).transpose(2, 1, 0, 3)
    gu_own = exchange(gu_chunks, "blk").transpose(1, 0, 2, 3).reshape(2, wide, unit)
    out_full = gather_blk_later(vis_out.T).reshape(wide, -1)
    fc1_full = gather_blk_later(vis_fc1).reshape(wide, -1)
    fc2_full = gather_blk_later(vis_fc2.T).reshape(wide, -1)
    rout_full = gather_blk_later(res_out.T).reshape(text, -1)
    rkv_own = res_kv.reshape(tcol, 2 * kvcols)
    rkv_quad = gather_tp(rkv_own)

    latent_in = latents.astype(F32)
    latent_low = rms_norm(latent_in, res_gains[1]).astype(BF)
    latent_cols = exchange(latent_low.reshape(lat, blk, tcol).transpose(1, 0, 2), "blk")
    latent_cols = latent_cols.reshape(lats, tcol)
    latent_qkv = sum_blk(
        jnp.concatenate([dot(latent_cols, res_q, 1, 0), dot(latent_cols, rkv_own, 1, 0)], axis=1)
        .astype(BF)
        .reshape(blk, lat, qcols + 2 * kvcols)
    ).astype(BF)
    latent_query = latent_qkv[:, :qcols]
    latent_kv = latent_qkv[:, qcols:]

    all_images = stream_images(image_patches, span_order, tok)
    own_images = lax.dynamic_slice_in_dim(all_images, b * tok, tok)
    allowed_vis = own_images[:, None] == all_images[None, :]
    inputs = patches.astype(F32)
    normed_one, norm_one_pull = jax.vjp(layer_norm, inputs, vis_gains[0], vis_shifts[0])
    attn_input = normed_one.astype(BF)
    attn_cols = exchange(attn_input.reshape(tok, blk, wcol).transpose(1, 0, 2), "blk")
    attn_cols = attn_cols.reshape(tokens, wcol)
    query_rows = (dot(attn_input, qkv_full[0], 1, 0) + vis_qv_bias[0]).astype(BF)
    key_rows = dot(attn_input, qkv_full[1], 1, 0).astype(BF)
    value_rows = (dot(attn_input, qkv_full[2], 1, 0) + vis_qv_bias[1]).astype(BF)
    kv_all = gather_blk(jnp.stack([key_rows, value_rows]))
    query_all = gather_blk_later(query_rows).reshape(tokens, heads, HEAD_VIS)
    key_all = kv_all[:, 0].reshape(tokens, heads, HEAD_VIS)
    value_all = kv_all[:, 1].reshape(tokens, heads, HEAD_VIS)
    query_heads = query_rows.reshape(tok, heads, HEAD_VIS)
    key_heads = key_rows.reshape(tok, heads, HEAD_VIS)
    value_heads = value_rows.reshape(tok, heads, HEAD_VIS)
    vis_scale = HEAD_VIS ** (-0.5)
    scores = mm("qhd,khd->hqk", query_heads, key_all) * vis_scale
    scores = jnp.where(allowed_vis[None], scores, -jnp.inf)
    row_top = jnp.max(scores, axis=-1)
    weights = jnp.exp(scores - row_top[..., None])
    weight_sum = jnp.sum(weights, axis=-1)
    weighted = mm("hqk,khd->hqd", weights.astype(BF), value_all)
    vis_lse = row_top + jnp.log(weight_sum)
    vis_result = (weighted / weight_sum[..., None]).transpose(1, 0, 2)
    attn_output = vis_result.astype(BF).reshape(tok, -1)

    hidden_one = inputs + sum_tp(dot(attn_output, out_full, 1, 1)) + vis_out_bias[0]
    normed_two, norm_two_pull = jax.vjp(layer_norm, hidden_one, vis_gains[1], vis_shifts[1])
    mlp_input = normed_two.astype(BF)
    mlp_cols = exchange(mlp_input.reshape(tok, blk, wcol).transpose(1, 0, 2), "blk")
    mlp_cols = mlp_cols.reshape(tokens, wcol)
    fc1_pre = dot(mlp_input, fc1_full, 1, 0) + vis_fc1_bias
    fc1_act, gelu_pull = jax.vjp(gelu_tanh, fc1_pre)
    fc1_low = fc1_act.astype(BF)
    fc2_part = dot(fc1_low, fc2_full, 1, 1).reshape(4, sub, wide)
    hidden_sub = lax.dynamic_slice_in_dim(hidden_one, t * sub, sub)
    vision_sub = hidden_sub + sum_tp_quarter(fc2_part) + vis_out_bias[1]
    vision_low = gather_every(vision_sub.astype(BF)).reshape(tokens, wide)
    attn_out_all = gather_blk_later(attn_output).reshape(tokens, -1)
    fc1_low_all = gather_blk_later(fc1_low).reshape(tokens, -1)

    gate = dot(vision_low, gu_own[0], 1, 0)
    up = dot(vision_low, gu_own[1], 1, 0)
    proj_hidden, proj_pull = jax.vjp(swiglu, gate, up)
    proj_all = gather_blk_later(proj_hidden.astype(BF))
    pdown = proj_down.reshape(blk, unit, tcol)
    context_part = mm("bth,bhc->tc", proj_all, pdown)
    quarter = tokens // 4
    context = sum_tp_quarter(context_part.reshape(4, quarter, tcol))
    gain_context_own = lax.dynamic_slice_in_dim(res_gains[0], b * tcol, tcol)
    scaled_low = (context * gain_context_own).astype(BF)
    kv_part = mm("kc,tcj->tkj", scaled_low, rkv_quad)
    square_part = jnp.sum(context * context, axis=-1)
    high, low = halves(square_part)
    stats = jnp.pad(jnp.stack([high, low], axis=1), ((0, 0), (0, 2 * kvcols - 2)))
    kv_sums = sum_blk(
        jnp.concatenate([kv_part, stats[None]], axis=0)
        .astype(BF)
        .reshape(5, blk, sub, 2 * kvcols)
        .transpose(1, 0, 2, 3)
    )
    scale_sub = lax.rsqrt((kv_sums[4, :, 0] + kv_sums[4, :, 1]) / text + EPSILON)
    patch_kv = (kv_sums[:4] * scale_sub[None, :, None]).astype(BF)
    patch_all = exchange(
        jnp.broadcast_to(patch_kv[None], (blk,) + patch_kv.shape).reshape(4 * blk, sub, -1), EVERY
    ).reshape(tokens, 2 * kvcols)

    latent_images = b * (lat // LATENTS) + jnp.arange(lat, dtype=jnp.int32) // LATENTS
    key_images = jnp.concatenate([all_images, latent_images])
    allowed_res = latent_images[:, None] == key_images[None, :]
    res_kv_all = jnp.concatenate([patch_all, latent_kv], axis=0)
    res_key, res_value = res_kv_all[:, :kvcols], res_kv_all[:, kvcols:]
    group = qcols // RES_HEAD
    res_query = latent_query.reshape(lat, group, RES_HEAD)
    res_scale = RES_HEAD ** (-0.5)
    res_scores = mm("qgd,nd->gqn", res_query, res_key) * res_scale
    res_scores = jnp.where(allowed_res[None], res_scores, -jnp.inf)
    res_top = jnp.max(res_scores, axis=-1)
    res_weights = jnp.exp(res_scores - res_top[..., None])
    res_sum = jnp.sum(res_weights, axis=-1)
    res_result = (
        mm("gqn,nd->gqd", res_weights.astype(BF), res_value) / res_sum[..., None]
    ).transpose(1, 0, 2)
    res_lse = res_top + jnp.log(res_sum)
    result_low = res_result.astype(BF).reshape(lat, qcols)

    latent_sub = lax.dynamic_slice_in_dim(latent_in, t * lsub, lsub)
    latent_one = latent_sub + sum_tp_quarter(
        dot(result_low, rout_full, 1, 1).reshape(4, lsub, text)
    )
    post_normed, post_pull = jax.vjp(rms_norm, latent_one, res_gains[2])
    post_all = gather_every(post_normed.astype(BF)).reshape(lats, text)
    result_all = gather_blk_later(result_low).reshape(lats, qcols)
    gate_up_two = mm("td,dje->tje", post_all, res_gate_up)
    mlp_hidden, mlp_pull = jax.vjp(swiglu, gate_up_two[:, 0], gate_up_two[:, 1])
    mlp_low = mlp_hidden.astype(BF)
    down_part = dot(mlp_low, res_down, 1, 0).reshape(4, blk, lsub, text)
    latent_two = latent_one + sum_every(down_part)
    final_normed, final_pull = jax.vjp(rms_norm, latent_two, res_gains[3])
    grad_sub = lax.dynamic_slice_in_dim(out_grad, t * lsub, lsub).astype(F32)
    dlatent_two, gain_final = final_pull(grad_sub)
    latents_out = gather_tp(final_normed).reshape(lat, text)

    dmlp_all = gather_every(dlatent_two.astype(BF)).reshape(lats, text)
    dgate_two, dup_two = mlp_pull(dot(dmlp_all, res_down, 1, 1))
    dgate_up_two = jnp.stack([dgate_two, dup_two], axis=1).astype(BF)
    dpost_part = mm("tje,dje->td", dgate_up_two, res_gate_up).reshape(4, blk, lsub, text)
    dpost = sum_every(dpost_part)
    grad_res_down = dot(mlp_low, dmlp_all, 0, 0)
    grad_res_gate_up = mm("td,tje->dje", post_all, dgate_up_two)
    dlatent_part, gain_post = post_pull(dpost)
    dlatent_one = dlatent_two + dlatent_part
    dattn_low = gather_tp(dlatent_one.astype(BF)).reshape(lat, text)

    dresult = dot(dattn_low, rout_full, 1, 0).astype(BF)
    dresult_heads = dresult.reshape(lat, group, RES_HEAD)
    res_delta = jnp.sum(dresult_heads.astype(F32) * res_result, axis=-1).T
    res_prob = jnp.exp(res_scores - res_lse[..., None])
    dprob = mm("qgd,nd->gqn", dresult_heads, res_value)
    dscores = (res_prob * (dprob - res_delta[..., None])).astype(BF)
    dquery = mm("gqn,nd->qgd", dscores, res_key) * res_scale
    dkey = mm("gqn,qgd->nd", dscores, res_query) * res_scale
    dvalue = mm("gqn,qgd->nd", res_prob.astype(BF), dresult_heads)
    dquery_own = dquery.reshape(lat, qcols).astype(BF)
    dkv_low = jnp.concatenate([dkey, dvalue], axis=1).astype(BF)
    dpatch_local, dlatent_kv = dkv_low[:tokens], dkv_low[tokens:]
    dpatch_sub = jnp.sum(
        exchange(dpatch_local.reshape(4 * blk, sub, 2 * kvcols), EVERY)
        .reshape(blk, 4, sub, 2 * kvcols)
        .astype(F32),
        axis=0,
    )
    along = jnp.sum(dpatch_sub * patch_kv.astype(F32), axis=(0, 2)) / text
    a_high, a_low = halves(along)
    s_high, s_low = halves(scale_sub)
    row_stats = jnp.pad(
        jnp.stack([a_high, a_low, s_high, s_low], axis=1), ((0, 0), (0, 2 * kvcols - 4))
    )
    dpatch_rows = gather_blk(jnp.concatenate([dpatch_sub, row_stats[None]], axis=0).astype(BF))
    dpatch_rows = dpatch_rows.transpose(1, 0, 2, 3).reshape(5, quarter, 2 * kvcols)
    dpatch_quad = dpatch_rows[:4]
    along_rows = dpatch_rows[4, :, 0].astype(F32) + dpatch_rows[4, :, 1].astype(F32)
    scale_rows = dpatch_rows[4, :, 2].astype(F32) + dpatch_rows[4, :, 3].astype(F32)
    dcontext_normed = mm("tkj,tcj->kc", dpatch_quad, rkv_quad)
    unit_context = context * scale_rows[:, None]
    dcontext = scale_rows[:, None] * (
        dcontext_normed * gain_context_own - unit_context * along_rows[:, None]
    )
    gain_context = jnp.sum(dcontext_normed * unit_context, axis=0)
    context_low = (unit_context * gain_context_own).astype(BF)

    dcontext_low = gather_tp(dcontext.astype(BF)).reshape(tokens, tcol)
    dproj_part = mm("tc,bhc->bth", dcontext_low, pdown)
    dproj = sum_blk(dproj_part)
    dgate, dup = proj_pull(dproj)
    dgate_low, dup_low = dgate.astype(BF), dup.astype(BF)
    dvision_part = dot(dgate_low, gu_own[0], 1, 1) + dot(dup_low, gu_own[1], 1, 1)
    dvision_sub = sum_every(dvision_part.reshape(4, blk, sub, wide))
    dvision_out = gather_tp(dvision_sub).reshape(tok, wide)
    grad_proj_down = mm("bth,tc->bhc", proj_all, dcontext_low).reshape(hidden, tcol)
    grad_gu = jnp.stack([dot(vision_low, dgate_low, 0, 0), dot(vision_low, dup_low, 0, 0)])
    grad_gu = exchange(grad_gu.astype(BF).reshape(2, blk, wcol, unit).transpose(1, 0, 2, 3), "blk")
    grad_proj_gate_up = grad_gu.transpose(2, 1, 0, 3).reshape(wcol, 2, hidden).astype(F32)

    dqkv_rows = gather_blk_later(jnp.concatenate([dquery_own, dlatent_kv], axis=1))
    dqkv_rows = dqkv_rows.reshape(lats, qcols + 2 * kvcols)
    dquery_all, dlkv_all = dqkv_rows[:, :qcols], dqkv_rows[:, qcols:]
    grad_res_q = dot(latent_cols, dquery_all, 0, 0)
    grad_res_kv = dot(latent_cols, dlkv_all, 0, 0) + sum_tp_quarter(
        mm("kc,tkj->tcj", context_low, dpatch_quad)
    )
    grad_res_kv = grad_res_kv.reshape(tcol, 2, kvcols)
    dlatent_part = dot(dquery_all, res_q, 1, 1) + dot(dlkv_all, rkv_own, 1, 1)
    dlatent_rows = exchange(dlatent_part.astype(BF).reshape(4 * blk, lsub, tcol), EVERY)
    dlatent_normed = (
        jnp.sum(dlatent_rows.reshape(blk, 4, lsub, tcol).astype(F32), axis=1)
        .transpose(1, 0, 2)
        .reshape(lsub, text)
    )
    latent_pull = jax.vjp(rms_norm, latent_sub, res_gains[1])[1]
    dlatent_in, gain_latent = latent_pull(dlatent_normed)
    latents_grad = gather_tp(dlatent_one + dlatent_in).reshape(lat, text)
    dattn_cols = exchange(dattn_low.reshape(lat, blk, tcol).transpose(1, 0, 2), "blk")
    grad_res_out = dot(result_all, dattn_cols.reshape(lats, tcol), 0, 0)
    gain_context_full = lax.dynamic_update_slice_in_dim(
        jnp.zeros((text,), F32), gain_context, b * tcol, 0
    )
    grad_res_gains = sum_small(
        jnp.concatenate([gain_context_full, gain_latent, gain_post, gain_final])
    ).reshape(4, text)

    dfc2_low = dvision_out.astype(BF)
    bias_two = jnp.sum(dfc2_low.astype(F32), axis=0)
    (dfc1_pre,) = gelu_pull(dot(dfc2_low, fc2_full, 1, 0))
    dfc1_low = dfc1_pre.astype(BF)
    bias_fc1 = jnp.sum(dfc1_low.astype(F32), axis=0)
    dfc1_all = gather_blk_later(dfc1_low).reshape(tokens, -1)
    dnormed_two = sum_tp(dot(dfc1_low, fc1_full, 1, 1))
    dhidden_part, gain_two, shift_two = norm_two_pull(dnormed_two)
    dhidden_one = dvision_out + dhidden_part
    dattn_total = dhidden_one.astype(BF)
    bias_one = jnp.sum(dattn_total.astype(F32), axis=0)
    dattn_output = dot(dattn_total, out_full, 1, 0).astype(BF)

    dout_heads = dattn_output.reshape(tok, heads, HEAD_VIS)
    vis_delta = jnp.sum(dout_heads.astype(F32) * vis_result, axis=-1)
    d_high, d_low = halves(vis_delta)
    l_high, l_low = halves(vis_lse.T)
    dout_all = gather_blk(
        jnp.concatenate(
            [dattn_output, jnp.concatenate([d_high, d_low, l_high, l_low], axis=1).astype(BF)],
            axis=1,
        )
    ).reshape(tokens, -1)
    width = heads * HEAD_VIS
    row_values = dout_all[:, width:].astype(F32).reshape(tokens, 2, 2, heads).sum(axis=2)
    delta_all, lse_all = row_values[:, 0].T, row_values[:, 1].T
    dout_all_heads = dout_all[:, :width].reshape(tokens, heads, HEAD_VIS)
    prob = jnp.exp(scores - vis_lse[..., None])
    dprob_vis = mm("qhd,khd->hqk", dout_heads, value_all)
    dscores_vis = (prob * (dprob_vis - vis_delta.T[..., None])).astype(BF)
    dquery_home = mm("hqk,khd->qhd", dscores_vis, key_all) * vis_scale
    scores_in = mm("khd,qhd->hkq", key_heads, query_all) * vis_scale
    scores_in = jnp.where(allowed_vis[None], scores_in, -jnp.inf)
    prob_in = jnp.exp(scores_in - lse_all[:, None, :])
    dprob_in = mm("khd,qhd->hkq", value_heads, dout_all_heads)
    dscores_in = (prob_in * (dprob_in - delta_all[:, None, :])).astype(BF)
    dkey_home = mm("hkq,qhd->khd", dscores_in, query_all) * vis_scale
    dvalue_home = mm("hkq,qhd->khd", prob_in.astype(BF), dout_all_heads)
    dqkv_low = jnp.stack(
        [
            dquery_home.reshape(tok, -1),
            dkey_home.reshape(tok, -1),
            dvalue_home.reshape(tok, -1),
        ]
    ).astype(BF)
    bias_qv = jnp.stack(
        [jnp.sum(dqkv_low[0].astype(F32), axis=0), jnp.sum(dqkv_low[2].astype(F32), axis=0)]
    )
    dqkv_all = gather_blk(dqkv_low)
    dnormed_one = sum_tp(
        dot(dqkv_low[0], qkv_full[0], 1, 1)
        + dot(dqkv_low[1], qkv_full[1], 1, 1)
        + dot(dqkv_low[2], qkv_full[2], 1, 1)
    )
    dinput_part, gain_one, shift_one = norm_one_pull(dnormed_one)
    patches_grad = dhidden_one + dinput_part

    dcols = exchange(
        jnp.stack([dfc2_low, dattn_total]).reshape(2, tok, blk, wcol).transpose(2, 0, 1, 3), "blk"
    )
    dfc2_cols = dcols[:, 0].reshape(tokens, wcol)
    dattn_vis_cols = dcols[:, 1].reshape(tokens, wcol)
    grad_vis_fc2 = dot(dfc2_cols, fc1_low_all, 0, 0).T
    grad_vis_out = dot(dattn_vis_cols, attn_out_all, 0, 0).T
    grad_vis_fc1 = dot(mlp_cols, dfc1_all, 0, 0)
    grad_vis_qkv = jnp.stack(
        [
            dot(attn_cols, dqkv_all[:, j].reshape(tokens, -1), 0, 0)
            for j in range(3)
        ],
        axis=1,
    )
    small = jnp.concatenate(
        [
            gain_one,
            gain_two,
            shift_one,
            shift_two,
            bias_one,
            bias_two,
            bias_qv.reshape(-1),
            bias_fc1,
        ]
    )
    small = jnp.sum(gather_blk(small), axis=0)
    grad_vis_gains = small[: 2 * wide].reshape(2, wide)
    grad_vis_shifts = small[2 * wide : 4 * wide].reshape(2, wide)
    grad_vis_out_bias = small[4 * wide : 6 * wide].reshape(2, wide)
    grad_vis_qv_bias = small[6 * wide : 6 * wide + 2 * width].reshape(2, width)
    grad_vis_fc1_bias = small[6 * wide + 2 * width :]
    return (
        latents_out,
        patches_grad,
        latents_grad,
        grad_vis_gains,
        grad_vis_shifts,
        grad_vis_qkv,
        grad_vis_qv_bias,
        grad_vis_out,
        grad_vis_out_bias,
        grad_vis_fc1,
        grad_vis_fc1_bias,
        grad_vis_fc2,
        grad_proj_gate_up,
        grad_proj_down,
        grad_res_gains,
        grad_res_q,
        grad_res_kv,
        grad_res_out,
        grad_res_gate_up,
        grad_res_down,
    )


def solution(mesh):
    placed = (
        P("blk", None),
        P("blk", None),
        P(),
        P(),
        P(),
        P(),
        P("blk", None, "tp"),
        P(None, "tp"),
        P("tp", "blk"),
        P(),
        P("blk", "tp"),
        P("tp"),
        P("tp", "blk"),
        P("blk", None, "tp"),
        P("tp", "blk"),
        P(),
        P("blk", "tp"),
        P("blk", None, "tp"),
        P("tp", "blk"),
        P(None, None, ("blk", "tp")),
        P(("blk", "tp"), None),
        P("blk", None),
    )
    return jax.shard_map(
        per_device,
        mesh=mesh,
        in_specs=placed,
        out_specs=(
            P("blk", None),
            P("blk", None),
            P("blk", None),
            P(),
            P(),
            P("blk", None, "tp"),
            P(None, "tp"),
            P("tp", "blk"),
            P(),
            P("blk", "tp"),
            P("tp"),
            P("tp", "blk"),
            P("blk", None, "tp"),
            P("tp", "blk"),
            P(),
            P("blk", "tp"),
            P("blk", None, "tp"),
            P("tp", "blk"),
            P(None, None, ("blk", "tp")),
            P(("blk", "tp"), None),
        ),
        check_vma=False,
    )
```

time: 4790 us -> 1560 us (0.33)
  waiting for transfers between devices: 4050 us -> 596 us
  blocking collectives: 205 us -> 489 us
  matrix products: 267 us -> 120 us
  starting transfers between devices: 39.6 us -> 111 us
    reduce_scatter x11 -> x0, waiting for transfers between devices: 2310 us -> none  [the longest x4 1220 us: return_rows(): return lax.psum_scatter(gradients, 'blk', scatter_dimension=1, tiled=True)]
    all_gather x11 -> x7, waiting for transfers between devices: 1210 us -> 190 us  [gather_blk_later(): return lax.all_gather(value, 'blk', axis=0, tiled=False)]
    psum x11 -> x0, waiting for transfers between devices: 384 us -> none  [the longest x10 319 us: over_heads(): return lax.psum(partial_value, 'tp')]
    all_to_all x0 -> x21, waiting for transfers between devices: none -> 228 us  [exchange(): return lax.all_to_all(chunks, axis, 0, 0, tiled=True)]
    all_gather x5, blocking collectives: 164 us -> 352 us  [gather_blk_later(): return lax.all_gather(value, 'blk', axis=0, tiled=False)]
    dot_general x96 -> x57, matrix products: 266 us -> 120 us  [the longest x36 62.1 us: dot(): lax.dot_general(left, right, (((on_left,), (on_right,)), ((), ())), prefe...]
    all_to_all x0 -> x5, blocking collectives: none -> 137 us  [exchange(): return lax.all_to_all(chunks, axis, 0, 0, tiled=True)]
    ppermute x44 -> x38, waiting for transfers between devices: 76.3 us -> 177 us  [the longest x19 153 us: swap_x(): lax.ppermute(value, 'tp', [(i, i ^ 2) for i in range(lax.axis_size('tp'))])]
  transfers between devices with their start and end apart: 78 -> 66, of which waited for: 64 -> 45; matrix products, arithmetic and copies ran while one was open for 6% -> 17% of each run, Pallas kernels for 0% -> 0%
where the time goes in v1:
time: 1560 us; the launch traced here: 1550 us
  waiting for transfers between devices  596 us (38%)
  blocking collectives  489 us (31%)
  local copies, waits for them, and re-layouts  140 us (9%)
  matrix products  120 us (8%)
  starting transfers between devices  111 us (7%)
  other arithmetic  76.3 us (5%)
  between operations  17.7 us (1%)
    all_gather x5, blocking collectives, gather_blk_later(): return lax.all_gather(value, 'blk', axis=0, tiled=False)  352 us
    all_to_all x21, waiting for transfers between devices, exchange(): return lax.all_to_all(chunks, axis, 0, 0, tiled=True)  228 us
    all_gather x7, waiting for transfers between devices, gather_blk_later(): return lax.all_gather(value, 'blk', axis=0, tiled=False)  190 us
    ppermute x19, waiting for transfers between devices, swap_x(): lax.ppermute(value, 'tp', [(i, i ^ 2) for i in range(lax.axis_size('tp'))])  153 us
    all_to_all x5, blocking collectives, exchange(): return lax.all_to_all(chunks, axis, 0, 0, tiled=True)  137 us
    all_to_all x21, starting transfers between devices, exchange(): return lax.all_to_all(chunks, axis, 0, 0, tiled=True)  82.6 us
    unnamed x370, local copies, waits for them, and re-layouts  64.3 us
    dot_general x36, matrix products, dot(): lax.dot_general(left, right, (((on_left,), (on_right,)), ((), ())), prefe...  62.1 us
  transfers between devices with their start and end apart: 66, of which 45 were waited for; matrix products, arithmetic and copies ran while one was open for 17% of the time, Pallas kernels for 0%

profile of v1, /device:TPU:0, one launch (start us, length us, event | category | flops | bytes accessed | tf_op | source)
XLA Modules:
  0.0 1550.8 jit_solution(4940839784202044560)
XLA Ops:
  15.3 52.7 %all-gather.18.cloned.1.call-done = bf16[24,144,288]{2,1,0:T(8,128)(2,1)} async-done(((bf16[3,144,288]{2,1,0:T(8,128)(2,1)}), bf16[24,144,288]{2,1,0:T(8,128)(2,1)}) %all-gather.18.cloned.1.call-update) | async-done | bytes 1990672 | tf_op jit(solution)/shard_map/all_gather | solution.py:78
  78.2 70.7 %all-gather.1 = bf16[1152,288]{1,0:T(8,128)(2,1)S(1)} all-gather(bf16[144,288]{1,0:T(8,128)(2,1)S(1)} %bitcast.843), channel_id=3, replica_groups=mesh['blk'=8,'tp'=4] {'blk'}, dimensions={0}, use_global_device_ids=true | all-gather | bytes 746496 | tf_op jit(solution)/shard_map/all_gather | solution.py:78
  161.4 7.4 collective-permute-done.3
  173.5 28.9 %all-gather.22.cloned.1.call-done = bf16[1152,1076]{1,0:T(8,128)(2,1)} async-done(((bf16[144,1076]{1,0:T(8,128)(2,1)}), bf16[1152,1076]{1,0:T(8,128)(2,1)}) %all-gather.22.cloned.1.call-update) | async-done | bytes 2479120 | tf_op jit(solution)/shard_map/all_gather | solution.py:78
  223.6 7.5 all-to-all-done.1
  236.2 13.2 collective-permute-done.6
  250.7 37.7 %all-to-all-done.2 = bf16[8,2,144,448]{3,2,1,0:T(8,128)(2,1)S(1)} async-done(((bf16[8,2,144,448]{3,2,1,0:T(8,128)(2,1)}), bf16[8,2,144,448]{3,2,1,0:T(8,128)(2,1)S(1)}, u32[]{:S(2)}, u32[]{:S(2)}) %all-to-all-start.2) | async-done | bytes 2064416 | tf_op jit(solution)/shard_map/all_to_all | solution.py:37
  299.2 108.3 %all-gather.24.cloned.1.call-done = bf16[8192,448]{0,1:T(8,128)(2,1)} async-done(((bf16[1024,448]{0,1:T(8,128)(2,1)}), bf16[8192,448]{0,1:T(8,128)(2,1)}) %all-gather.24.cloned.1.call-update) | async-done | bytes 7340048 | tf_op jit(solution)/shard_map/all_gather | solution.py:78
  407.6 7.3 copy.687
  414.9 12.8 dot_general.212
  427.7 7.4 fusion.35
  447.0 5.8 collective-permute-done.9
  454.9 16.2 %all-to-all-done.5 = bf16[8,64,512]{2,1,0:T(8,128)(2,1)S(1)} async-done(((bf16[8,64,512]{2,1,0:T(8,128)(2,1)}), bf16[8,64,512]{2,1,0:T(8,128)(2,1)S(1)}, u32[]{:S(2)}, u32[]{:S(2)}) %all-to-all-start.5) | async-done | bytes 524320 | tf_op jit(solution)/shard_map/all_to_all | solution.py:37
  476.4 15.5 all-to-all-done.3
  495.9 17.1 %all-to-all-done.6 = bf16[8,64,576]{2,1,0:T(8,128)(2,1)S(1)} async-done(((bf16[8,64,576]{2,1,0:T(8,128)(2,1)}), bf16[8,64,576]{2,1,0:T(8,128)(2,1)S(1)}, u32[]{:S(2)}, u32[]{:S(2)}) %all-to-all-start.6) | async-done | bytes 589856 | tf_op jit(solution)/shard_map/all_to_all | solution.py:37
  517.9 15.0 all-to-all-done.4
  549.0 28.2 %all_to_all.136 = bf16[8,16,4096]{2,1,0:T(8,128)(2,1)S(1)} all-to-all(bf16[8,16,4096]{2,1,0:T(8,128)(2,1)S(1)} %broadcast_in_dim.71), channel_id=1, replica_groups=mesh['blk'=8,'tp'=4] {'blk'}, dimensions={0} | all-to-all | bytes 2097152 | tf_op jit(solution)/shard_map/all_to_all | solution.py:37
  578.7 22.1 %collective-permute-done.12 = bf16[8,16,4096]{2,1,0:T(8,128)(2,1)S(1)} collective-permute-done((bf16[8,16,4096]{2,1,0:T(8,128)(2,1)S(1)}, bf16[8,16,4096]{2,1,0:T(8,128)(2,1)S(1)}, u32[]{:S(2)}, u32[]{:S(2)}) %collective-permute-start.12) | collective-permute-done | bytes 1048608 | tf_op jit(solution)/shard_map/ppermute | solution.py:21
  623.5 23.7 %collective-permute-done.15 = bf16[8,16,4096]{2,1,0:T(8,128)(2,1)S(1)} collective-permute-done((bf16[8,16,4096]{2,1,0:T(8,128)(2,1)S(1)}, bf16[8,16,4096]{2,1,0:T(8,128)(2,1)S(1)}, u32[]{:S(2)}, u32[]{:S(2)}) %collective-permute-start.15) | collective-permute-done | bytes 1048608 | tf_op jit(solution)/shard_map/ppermute | solution.py:21
  647.6 29.6 %all_to_all.137 = bf16[8,16,4096]{2,1,0:T(8,128)(2,1)S(1)} all-to-all(bf16[8,16,4096]{2,1,0:T(8,128)(2,1)S(1)} %fusion.28), channel_id=1, replica_groups=mesh['blk'=8,'tp'=4] {'blk'}, dimensions={0} | all-to-all | bytes 2097152 | tf_op jit(solution)/shard_map/all_to_all | solution.py:37
  678.6 28.8 %all_to_all.138 = bf16[8,16,4096]{2,1,0:T(8,128)(2,1)S(1)} all-to-all(bf16[8,16,4096]{2,1,0:T(8,128)(2,1)S(1)} %broadcast_in_dim.73), channel_id=1, replica_groups=mesh['blk'=8,'tp'=4] {'blk'}, dimensions={0} | all-to-all | bytes 2097152 | tf_op jit(solution)/shard_map/all_to_all | solution.py:37
  708.9 22.1 %collective-permute-done.18 = bf16[8,16,4096]{2,1,0:T(8,128)(2,1)S(1)} collective-permute-done((bf16[8,16,4096]{2,1,0:T(8,128)(2,1)S(1)}, bf16[8,16,4096]{2,1,0:T(8,128)(2,1)S(1)}, u32[]{:S(2)}, u32[]{:S(2)}) %collective-permute-start.18) | collective-permute-done | bytes 1048608 | tf_op jit(solution)/shard_map/ppermute | solution.py:21
  739.5 8.1 fusion
  754.9 23.7 %collective-permute-done.21 = bf16[8,16,4096]{2,1,0:T(8,128)(2,1)S(1)} collective-permute-done((bf16[8,16,4096]{2,1,0:T(8,128)(2,1)S(1)}, bf16[8,16,4096]{2,1,0:T(8,128)(2,1)S(1)}, u32[]{:S(2)}, u32[]{:S(2)}) %collective-permute-start.21) | collective-permute-done | bytes 1048608 | tf_op jit(solution)/shard_map/ppermute | solution.py:21
  779.0 29.5 %all_to_all.139 = bf16[8,16,4096]{2,1,0:T(8,128)(2,1)S(1)} all-to-all(bf16[8,16,4096]{2,1,0:T(8,128)(2,1)S(1)} %fusion.27), channel_id=1, replica_groups=mesh['blk'=8,'tp'=4] {'blk'}, dimensions={0} | all-to-all | bytes 2097152 | tf_op jit(solution)/shard_map/all_to_all | solution.py:37
  825.9 15.5 %all-to-all-done.11 = bf16[32,32,192]{2,1,0:T(8,128)(2,1)S(1)} async-done(((bf16[32,32,192]{2,1,0:T(8,128)(2,1)}), bf16[32,32,192]{2,1,0:T(8,128)(2,1)S(1)}, u32[]{:S(2)}, u32[]{:S(2)}) %all-to-all-start.11) | async-done | bytes 393248 | tf_op jit(solution)/shard_map/all_to_all | solution.py:37
  842.0 20.8 %all_to_all.140 = bf16[8,5,32,192]{3,2,1,0:T(8,128)(2,1)S(1)} all-to-all(bf16[8,5,32,192]{3,2,1,0:T(8,128)(2,1)S(1)} %broadcast_in_dim.75), channel_id=1, replica_groups=mesh['blk'=8,'tp'=4] {'blk'}, dimensions={0} | all-to-all | bytes 983040 | tf_op jit(solution)/shard_map/all_to_all | solution.py:37
  866.4 5.2 collective-permute-done.24
  874.8 6.1 convert_bitcast_fusion
  887.9 182.0 %all-gather.6 = bf16[1024,288]{0,1:T(8,128)(2,1)} all-gather(bf16[128,288]{0,1:T(8,128)(2,1)S(1)} %copy-done.95), channel_id=8, replica_groups=mesh['blk'=8,'tp'=4] {'blk'}, dimensions={0}, use_global_device_ids=true | all-gather | bytes 663552 | tf_op jit(solution)/shard_map/all_gather | solution.py:78
  1071.1 33.9 %all_gather.82 = bf16[8,128,288]{1,2,0:T(8,128)(2,1)} all-gather(bf16[1,128,288]{1,2,0:T(8,128)(2,1)} %bitcast.811), channel_id=1, replica_groups=mesh['blk'=8,'tp'=4] {'blk'}, dimensions={0}, use_global_device_ids=true | all-gather | bytes 663552 | tf_op jit(solution)/shard_map/all_gather | solution.py:78
  1109.5 33.9 %all_gather.87 = bf16[8,64,384]{2,1,0:T(8,128)(2,1)} all-gather(bf16[1,64,384]{2,1,0:T(8,128)(2,1)S(1)} %all_gather_reshape.7), channel_id=1, replica_groups=mesh['blk'=8,'tp'=4] {'blk'}, dimensions={0}, use_global_device_ids=true | all-gather | bytes 442368 | tf_op jit(solution)/shard_map/all_gather | solution.py:78
  1144.6 6.7 fusion.83
  1151.4 32.6 %copy.574 = f32[4096,2,512]{2,1,0:T(2,128)} copy(f32[4096,2,512]{2,0,1:T(8,128)S(1)} %fusion.83) | data formatting | bytes 33554432
  1184.0 8.1 fusion.117
  1193.9 5.2 convert_reduce_fusion
  1209.7 31.7 %all-gather.7 = bf16[512,576]{1,0:T(8,128)(2,1)S(1)} all-gather(bf16[64,576]{1,0:T(8,128)(2,1)S(1)} %pad_maximum_fusion.9), channel_id=9, replica_groups=mesh['blk'=8,'tp'=4] {'blk'}, dimensions={0}, use_global_device_ids=true | all-gather | bytes 663552 | tf_op jit(solution)/shard_map/all_gather | solution.py:78
  1253.1 6.4 collective-permute-done.27
  1279.9 6.7 all-to-all-done.14
  1327.2 7.2 all-to-all-done.21
  1338.0 7.3 all-to-all-done.24
  1356.8 10.1 all-to-all-done.15
  1395.8 38.6 %all-to-all-done.22 = bf16[8,2,144,448]{3,2,1,0:T(8,128)(2,1)} async-done(((bf16[8,2,144,448]{3,2,1,0:T(8,128)(2,1)}), bf16[8,2,144,448]{3,2,1,0:T(8,128)(2,1)}, u32[]{:S(2)}, u32[]{:S(2)}) %all-to-all-start.22) | async-done | bytes 2064416 | tf_op jit(solution)/shard_map/all_to_all | solution.py:37
  1440.2 7.9 collective-permute-done.33
  1449.4 16.9 %all-to-all-done.20 = bf16[8,2,128,144]{2,3,1,0:T(8,128)(2,1)S(1)} async-done(((bf16[8,2,128,144]{2,3,1,0:T(8,128)(2,1)}), bf16[8,2,128,144]{2,3,1,0:T(8,128)(2,1)S(1)}, u32[]{:S(2)}, u32[]{:S(2)}) %all-to-all-start.20) | async-done | bytes 589856 | tf_op jit(solution)/shard_map/all_to_all | solution.py:37
  1481.7 6.0 all-to-all-start.19
  1487.7 10.3 fusion.251
  1505.2 7.0 reshape.1489
  (775 shorter events, 387.5 us)
Async XLA Ops:
  7.2 60.8 %all-gather.18.cloned.1.call-start = ((), (), s32[]{:S(2)}) async-start(), calls=%async_computation.26 | async-start | bytes 2985984 | tf_op jit(solution)/shard_map/all_gather | solution.py:78
  7.9 161.6 %all-gather.20.cloned.1.call-start = ((), (), s32[]{:S(2)}) async-start(), calls=%async_computation.27 | async-start | bytes 2985984 | tf_op jit(solution)/shard_map/all_gather | solution.py:78
  72.6 76.8 %all-to-all-start = ((bf16[8,2,128,288]{2,3,1,0:T(8,128)(2,1)}), bf16[8,2,128,288]{2,3,1,0:T(8,128)(2,1)}, u32[]{:S(2)}, u32[]{:S(2)}) async-start(bf16[8,2,128,288]{2,3,1,0:T(8,128)(2,1)} %broadcast_in_dim.66), calls=%async_computation | async-start | bytes 2359296 | tf_op jit(solution)/shard_map/all_to_all | solution.py:37
  76.9 125.6 %all-gather.22.cloned.1.call-start = ((), (), s32[]{:S(2)}) async-start(), calls=%async_computation.28 | async-start | bytes 2985984 | tf_op jit(solution)/shard_map/all_gather | solution.py:78
  159.7 9.1 collective-permute-start.3
  212.0 19.0 %all-to-all-start.1 = ((bf16[8,32,1152]{2,1,0:T(8,128)(2,1)}), bf16[8,32,1152]{2,1,0:T(8,128)(2,1)S(1)}, u32[]{:S(2)}, u32[]{:S(2)}) async-start(bf16[8,32,1152]{2,1,0:T(8,128)(2,1)} %broadcast_in_dim.68), calls=%async_computation.1 | async-start | bytes 1179648 | tf_op jit(solution)/shard_map/all_to_all | solution.py:37
  231.0 57.3 %all-to-all-start.2 = ((bf16[8,2,144,448]{3,2,1,0:T(8,128)(2,1)}), bf16[8,2,144,448]{3,2,1,0:T(8,128)(2,1)S(1)}, u32[]{:S(2)}, u32[]{:S(2)}) async-start(bf16[8,2,144,448]{3,2,1,0:T(8,128)(2,1)} %copy.493), calls=%async_computation.2 | async-start | bytes 4718592 | tf_op jit(solution)/shard_map/all_to_all | solution.py:37
  234.7 172.9 %all-gather.24.cloned.1.call-start = ((), (), s32[]{:S(2)}) async-start(), calls=%async_computation.29 | async-start | bytes 8257536 | tf_op jit(solution)/shard_map/all_gather | solution.py:78
  234.7 14.7 collective-permute-start.6
  250.7 39.0 %collective-permute-start.7 = (bf16[2,8,32,1152]{3,2,1,0:T(8,128)(2,1)}, bf16[2,8,32,1152]{3,2,1,0:T(8,128)(2,1)}, u32[]{:S(2)}, u32[]{:S(2)}) collective-permute-start(bf16[2,8,32,1152]{3,2,1,0:T(8,128)(2,1)} %maximum_select_fusion.6), channel_id=1, source_target_pairs={{0,1},{1,0},{2,3},{3,2},{4,5},{5,4},{6,7},{7,6},{8,9},{9,8},{10,11... | collective-permute-start | bytes 3538952 | tf_op jit(solution)/shard_map/ppermute | solution.py:17
  296.4 238.6 %all-gather.26.cloned.1.call-start = ((), (), s32[]{:S(2)}) async-start(), calls=%async_computation.30 | async-start | bytes 3538944 | tf_op jit(solution)/shard_map/all_gather | solution.py:78
  296.5 145.1 %collective-permute-start = (bf16[512,192]{0,1:T(8,128)(2,1)S(1)}, bf16[512,192]{0,1:T(8,128)(2,1)}, u32[]{:S(2)}, u32[]{:S(2)}) collective-permute-start(bf16[512,192]{0,1:T(8,128)(2,1)S(1)} %bitcast.746), channel_id=1, source_target_pairs={{0,2},{1,3},{2,0},{3,1},{4,6},{5,7},{6,4},{7,5},{8,10},{9,11},{10,... | collective-permute-start | bytes 589832 | tf_op jit(solution)/shard_map/ppermute | solution.py:21
  437.5 33.7 %all-to-all-start.5 = ((bf16[8,64,512]{2,1,0:T(8,128)(2,1)}), bf16[8,64,512]{2,1,0:T(8,128)(2,1)S(1)}, u32[]{:S(2)}, u32[]{:S(2)}) async-start(bf16[8,64,512]{2,1,0:T(8,128)(2,1)} %bitcast.768), calls=%async_computation.5 | async-start | bytes 1048576 | tf_op jit(solution)/shard_map/all_to_all | solution.py:37
  471.1 20.7 %all-to-all-start.3 = ((bf16[8,5,32,192]{3,2,1,0:T(8,128)(2,1)}), bf16[8,5,32,192]{3,2,1,0:T(8,128)(2,1)S(1)}, u32[]{:S(2)}, u32[]{:S(2)}) async-start(bf16[8,5,32,192]{3,2,1,0:T(8,128)(2,1)} %copy.502), calls=%async_computation.3 | async-start | bytes 1310720 | tf_op jit(solution)/shard_map/all_to_all | solution.py:37
  491.9 21.1 %all-to-all-start.6 = ((bf16[8,64,576]{2,1,0:T(8,128)(2,1)}), bf16[8,64,576]{2,1,0:T(8,128)(2,1)S(1)}, u32[]{:S(2)}, u32[]{:S(2)}) async-start(bf16[8,64,576]{2,1,0:T(8,128)(2,1)} %pad_maximum_fusion.4), calls=%async_computation.6 | async-start | bytes 1310720 | tf_op jit(solution)/shard_map/all_to_all | solution.py:37
  513.8 19.1 %all-to-all-start.4 = ((bf16[32,32,192]{2,1,0:T(8,128)(2,1)}), bf16[32,32,192]{2,1,0:T(8,128)(2,1)S(1)}, u32[]{:S(2)}, u32[]{:S(2)}) async-start(bf16[32,32,192]{2,1,0:T(8,128)(2,1)} %bitcast.62), calls=%async_computation.4 | async-start | bytes 1048576 | tf_op jit(solution)/shard_map/all_to_all | solution.py:37
  577.2 23.6 %collective-permute-start.12 = (bf16[8,16,4096]{2,1,0:T(8,128)(2,1)S(1)}, bf16[8,16,4096]{2,1,0:T(8,128)(2,1)S(1)}, u32[]{:S(2)}, u32[]{:S(2)}) collective-permute-start(bf16[8,16,4096]{2,1,0:T(8,128)(2,1)S(1)} %all_to_all.136), channel_id=1, source_target_pairs={{0,2},{1,3},{2,0},{3,1},{4,6},{5,7},{6,4},{7,5},{8,10},{9,11},{10,... | collective-permute-start | bytes 3145736 | tf_op jit(solution)/shard_map/ppermute | solution.py:21
  622.0 25.3 %collective-permute-start.15 = (bf16[8,16,4096]{2,1,0:T(8,128)(2,1)S(1)}, bf16[8,16,4096]{2,1,0:T(8,128)(2,1)S(1)}, u32[]{:S(2)}, u32[]{:S(2)}) collective-permute-start(bf16[8,16,4096]{2,1,0:T(8,128)(2,1)S(1)} %fusion.60), channel_id=1, source_target_pairs={{0,2},{1,3},{2,0},{3,1},{4,6},{5,7},{6,4},{7,5},{8,10},{9,11},{10,... | collective-permute-start | bytes 3145736 | tf_op jit(solution)/shard_map/ppermute | solution.py:21
  707.4 23.6 %collective-permute-start.18 = (bf16[8,16,4096]{2,1,0:T(8,128)(2,1)S(1)}, bf16[8,16,4096]{2,1,0:T(8,128)(2,1)S(1)}, u32[]{:S(2)}, u32[]{:S(2)}) collective-permute-start(bf16[8,16,4096]{2,1,0:T(8,128)(2,1)S(1)} %all_to_all.138), channel_id=1, source_target_pairs={{0,2},{1,3},{2,0},{3,1},{4,6},{5,7},{6,4},{7,5},{8,10},{9,11},{10,... | collective-permute-start | bytes 3145736 | tf_op jit(solution)/shard_map/ppermute | solution.py:21
  753.4 25.3 %collective-permute-start.21 = (bf16[8,16,4096]{2,1,0:T(8,128)(2,1)S(1)}, bf16[8,16,4096]{2,1,0:T(8,128)(2,1)S(1)}, u32[]{:S(2)}, u32[]{:S(2)}) collective-permute-start(bf16[8,16,4096]{2,1,0:T(8,128)(2,1)S(1)} %fusion.61), channel_id=1, source_target_pairs={{0,2},{1,3},{2,0},{3,1},{4,6},{5,7},{6,4},{7,5},{8,10},{9,11},{10,... | collective-permute-start | bytes 3145736 | tf_op jit(solution)/shard_map/ppermute | solution.py:21
  822.4 19.1 %all-to-all-start.11 = ((bf16[32,32,192]{2,1,0:T(8,128)(2,1)}), bf16[32,32,192]{2,1,0:T(8,128)(2,1)S(1)}, u32[]{:S(2)}, u32[]{:S(2)}) async-start(bf16[32,32,192]{2,1,0:T(8,128)(2,1)} %bitcast.139), calls=%async_computation.11 | async-start | bytes 1048576 | tf_op jit(solution)/shard_map/all_to_all | solution.py:37
  880.8 313.1 %all-to-all-start.13 = ((bf16[8,1024,448]{1,2,0:T(8,128)(2,1)}), bf16[8,1024,448]{1,2,0:T(8,128)(2,1)}, u32[]{:S(2)}, u32[]{:S(2)}) async-start(bf16[8,1024,448]{1,2,0:T(8,128)(2,1)} %convert_bitcast_fusion), calls=%async_computation.13 | async-start | bytes 14680064 | tf_op jit(solution)/shard_map/all_to_all | solution.py:37
  885.9 628.8 %all-gather.30.cloned.1.call-start = ((), (), s32[]{:S(2)}) async-start(), calls=%async_computation.32 | async-start | bytes 2488320 | tf_op jit(solution)/shard_map/all_gather | solution.py:78
  1192.1 15.6 %collective-permute-start.16 = (f32[16,4096]{1,0:T(8,128)S(1)}, f32[16,4096]{1,0:T(8,128)S(1)}, u32[]{:S(2)}, u32[]{:S(2)}) collective-permute-start(f32[16,4096]{1,0:T(8,128)S(1)} %copy-done.65), channel_id=1, source_target_pairs={{0,2},{1,3},{2,0},{3,1},{4,6},{5,7},{6,4},{7,5},{8,10},{9,11},{10,... | collective-permute-start | bytes 786440 | tf_op jit(solution)/shard_map/ppermute | solution.py:21
  1207.7 34.1 %collective-permute-start.26 = (bf16[2,8,32,1152]{3,2,1,0:T(8,128)(2,1)}, bf16[2,8,32,1152]{3,2,1,0:T(8,128)(2,1)}, u32[]{:S(2)}, u32[]{:S(2)}) collective-permute-start(bf16[2,8,32,1152]{3,2,1,0:T(8,128)(2,1)} %fusion.44), channel_id=1, source_target_pairs={{0,1},{1,0},{2,3},{3,2},{4,5},{5,4},{6,7},{7,6},{8,9},{9,8},{10,11... | collective-permute-start | bytes 3538952 | tf_op jit(solution)/shard_map/ppermute | solution.py:17
  1208.6 67.5 %collective-permute-start.17 = (f32[2,16,4096]{2,1,0:T(8,128)}, f32[2,16,4096]{2,1,0:T(8,128)}, u32[]{:S(2)}, u32[]{:S(2)}) collective-permute-start(f32[2,16,4096]{2,1,0:T(8,128)} %maximum_select_fusion.13), channel_id=1, source_target_pairs={{0,1},{1,0},{2,3},{3,2},{4,5},{5,4},{6,7},{7,6},{8,9},{9,8},{10,11... | collective-permute-start | bytes 1572872 | tf_op jit(solution)/shard_map/ppermute | solution.py:17
  1245.8 13.7 collective-permute-start.27
  1247.9 18.9 %all-to-all-start.16 = ((bf16[32,16,512]{2,1,0:T(8,128)(2,1)}), bf16[32,16,512]{2,1,0:T(8,128)(2,1)}, u32[]{:S(2)}, u32[]{:S(2)}) async-start(bf16[32,16,512]{2,1,0:T(8,128)(2,1)} %bitcast.773), calls=%async_computation.16 | async-start | bytes 1048576 | tf_op jit(solution)/shard_map/all_to_all | solution.py:37
  1266.8 19.9 %all-to-all-start.14 = ((bf16[8,32,1152]{2,1,0:T(8,128)(2,1)}), bf16[8,32,1152]{2,1,0:T(8,128)(2,1)S(1)}, u32[]{:S(2)}, u32[]{:S(2)}) async-start(bf16[8,32,1152]{2,1,0:T(8,128)(2,1)} %fusion.45), calls=%async_computation.14 | async-start | bytes 1179648 | tf_op jit(solution)/shard_map/all_to_all | solution.py:37
  1286.6 18.3 %all-to-all-start.25 = ((bf16[8,64,512]{2,1,0:T(8,128)(2,1)}), bf16[8,64,512]{2,1,0:T(8,128)(2,1)S(1)}, u32[]{:S(2)}, u32[]{:S(2)}) async-start(bf16[8,64,512]{2,1,0:T(8,128)(2,1)} %bitcast.696), calls=%async_computation.25 | async-start | bytes 1048576 | tf_op jit(solution)/shard_map/all_to_all | solution.py:37
  1296.2 11.1 collective-permute-start.34
  1303.3 10.2 collective-permute-start.30
  1308.1 163.3 %collective-permute-start.35 = (f32[2,16,4096]{2,1,0:T(8,128)}, f32[2,16,4096]{2,1,0:T(8,128)}, u32[]{:S(2)}, u32[]{:S(2)}) collective-permute-start(f32[2,16,4096]{2,1,0:T(8,128)} %maximum_select_fusion.17), channel_id=1, source_target_pairs={{0,1},{1,0},{2,3},{3,2},{4,5},{5,4},{6,7},{7,6},{8,9},{9,8},{10,11... | collective-permute-start | bytes 1572872 | tf_op jit(solution)/shard_map/ppermute | solution.py:17
  1309.1 11.8 all-to-all-start.23
  1314.6 9.8 collective-permute-start.31
  1320.9 13.5 all-to-all-start.21
  1335.1 10.1 all-to-all-start.24
  1346.2 20.8 %all-to-all-start.15 = ((bf16[8,128,304]{1,2,0:T(8,128)(2,1)}), bf16[8,128,304]{1,2,0:T(8,128)(2,1)S(1)}, u32[]{:S(2)}, u32[]{:S(2)}) async-start(bf16[8,128,304]{1,2,0:T(8,128)(2,1)} %broadcast_in_dim.78), calls=%async_computation.15 | async-start | bytes 1245184 | tf_op jit(solution)/shard_map/all_to_all | solution.py:37
  1367.8 66.7 %all-to-all-start.22 = ((bf16[8,2,144,448]{3,2,1,0:T(8,128)(2,1)}), bf16[8,2,144,448]{3,2,1,0:T(8,128)(2,1)}, u32[]{:S(2)}, u32[]{:S(2)}) async-start(bf16[8,2,144,448]{3,2,1,0:T(8,128)(2,1)} %copy.563), calls=%async_computation.22 | async-start | bytes 4718592 | tf_op jit(solution)/shard_map/all_to_all | solution.py:37
  1372.1 150.6 %all-gather.28.cloned.1.call-start = ((), (), s32[]{:S(2)}) async-start(), calls=%async_computation.31 | async-start | bytes 2488320 | tf_op jit(solution)/shard_map/all_gather | solution.py:78
  1374.7 13.8 collective-permute-start.36
  1388.0 50.1 %collective-permute-start.32 = (f32[128,1152]{1,0:T(8,128)}, f32[128,1152]{1,0:T(8,128)}, u32[]{:S(2)}, u32[]{:S(2)}) collective-permute-start(f32[128,1152]{1,0:T(8,128)} %convolution_add_fusion.2), channel_id=1, source_target_pairs={{0,1},{1,0},{2,3},{3,2},{4,5},{5,4},{6,7},{7,6},{8,9},{9,8},{10,11... | collective-permute-start | bytes 1769480 | tf_op jit(solution)/shard_map/ppermute | solution.py:17
  1390.4 86.8 %collective-permute-start.37 = (bf16[512,192]{0,1:T(8,128)(2,1)}, bf16[512,192]{0,1:T(8,128)(2,1)}, u32[]{:S(2)}, u32[]{:S(2)}) collective-permute-start(bf16[512,192]{0,1:T(8,128)(2,1)} %fusion.167), channel_id=1, source_target_pairs={{0,2},{1,3},{2,0},{3,1},{4,6},{5,7},{6,4},{7,5},{8,10},{9,11},{10,... | collective-permute-start | bytes 589832 | tf_op jit(solution)/shard_map/ppermute | solution.py:21
  1434.5 31.9 %all-to-all-start.20 = ((bf16[8,2,128,144]{2,3,1,0:T(8,128)(2,1)}), bf16[8,2,128,144]{2,3,1,0:T(8,128)(2,1)S(1)}, u32[]{:S(2)}, u32[]{:S(2)}) async-start(bf16[8,2,128,144]{2,3,1,0:T(8,128)(2,1)} %copy.557), calls=%async_computation.20 | async-start | bytes 1179648 | tf_op jit(solution)/shard_map/all_to_all | solution.py:37
  1439.4 8.7 collective-permute-start.33
  1467.2 13.0 all-to-all-start.17
  1481.7 46.2 %all-to-all-start.19 = ((bf16[8,3,128,288]{2,3,1,0:T(8,128)(2,1)}), bf16[8,3,128,288]{2,3,1,0:T(8,128)(2,1)S(1)}, u32[]{:S(2)}, u32[]{:S(2)}) async-start(bf16[8,3,128,288]{2,3,1,0:T(8,128)(2,1)} %broadcast_in_dim.83), calls=%async_computation.19 | async-start | bytes 3538944 | tf_op jit(solution)/shard_map/all_to_all | solution.py:37
  1527.9 13.5 all-to-all-start.18
  (199 other events, 3696.8 us)
Sparse Core Ops, SparseCore 0:
  10.2 57.7 all-gather.17
  70.1 76.6 all-gather.19
  149.0 53.4 all-gather.21
  296.5 111.0 all-gather.23
  410.2 67.7 all-gather.25
  1107.0 52.6 all-gather.29
  1391.6 77.5 all-gather.27

commit v2 on v1

--- a/solution.py
+++ b/solution.py
@@ -1,6 +1,9 @@
 import jax
 import jax.numpy as jnp
 from jax import lax
+from jax.experimental import pallas as pl
+from jax.experimental.layout import Layout, with_layout_constraint
+from jax.experimental.pallas import tpu as pltpu
 from jax.sharding import PartitionSpec as P
 
 HEADS = 16
@@ -86,14 +89,107 @@
     return sum_blk(sum_tp_quarter(partial))
 
 
-def sum_small(rows):
-    blk, tp = lax.axis_size("blk"), lax.axis_size("tp")
-    count = blk * tp
-    width = rows.shape[0]
-    unit = count * 128
-    padded = jnp.pad(rows, (0, (-width) % unit)).reshape(count, -1)
-    own = jnp.sum(exchange(padded, EVERY), axis=0)
-    return gather_direct(own, EVERY, count).reshape(-1)[:width]
+def ring_order():
+    count = lax.axis_size("blk")
+    return list(range(0, count, 2)) + list(range(count - 1, 0, -2))
+
+
+def ring_index(distance):
+    order = ring_order()
+    count = len(order)
+    after = [order[(order.index(i) + distance) % count] for i in range(count)]
+    return jnp.array(after, jnp.int32)[lax.axis_index("blk")]
+
+
+def pass_on(value, step):
+    order = ring_order()
+    count = len(order)
+    route = [(order[i], order[(i + step) % count]) for i in range(count)]
+    return lax.ppermute(value, "blk", route)
+
+
+def ring_gather(own):
+    count = lax.axis_size("blk")
+    half, rows = count // 2, own.shape[0] // 2
+    blocks = [own] + [None] * (count - 1)
+    ahead = behind = own
+    for k in range(1, half):
+        behind = pass_on(behind, 1)
+        ahead = pass_on(ahead, -1)
+        blocks[count - k], blocks[k] = behind, ahead
+    blocks[half] = jnp.concatenate(
+        [pass_on(behind[:rows], 1), pass_on(ahead[rows:], -1)], axis=0
+    )
+    return blocks
+
+
+def ring_sum(part):
+    count = lax.axis_size("blk")
+    half = count // 2
+    far = part(half)
+    rows = far.shape[0] // 2
+    low = far.astype(BF)
+    onward, back = pass_on(low[:rows], 1), pass_on(low[rows:], -1)
+    for k in range(half - 1, 0, -1):
+        one, two = part(k), part(count - k)
+        if k == half - 1:
+            blank = jnp.zeros_like(onward)
+            onward = jnp.concatenate([onward, blank], axis=0)
+            back = jnp.concatenate([blank, back], axis=0)
+        onward = pass_on((one + onward.astype(F32)).astype(BF), 1)
+        back = pass_on((two + back.astype(F32)).astype(BF), -1)
+    return part(0) + onward.astype(F32) + back.astype(F32)
+
+
+def place_blocks(blocks):
+    count = len(blocks)
+    places = jnp.stack([ring_index(k) for k in range(count)])
+
+    def kernel(places_ref, *refs):
+        for k in range(count):
+            refs[count][places_ref[k]] = refs[k][...]
+
+    return pl.pallas_call(
+        kernel,
+        out_shape=jax.ShapeDtypeStruct((count,) + blocks[0].shape, blocks[0].dtype),
+        in_specs=[pl.BlockSpec(memory_space=pltpu.SMEM)]
+        + [pl.BlockSpec(memory_space=pltpu.VMEM)] * count,
+        out_specs=pl.BlockSpec(memory_space=pltpu.VMEM),
+        compiler_params=pltpu.CompilerParams(vmem_limit_bytes=24 * 2**20),
+        name="place_blocks",
+    )(places, *blocks)
+
+
+def after(value, *others):
+    return lax.optimization_barrier((value,) + others)[0]
+
+
+def ring_groups():
+    count = lax.axis_size("blk")
+    half = count // 2
+    return [[0]] + [[k, count - k] for k in range(1, half)] + [[half]]
+
+
+def gather_rows_every(own):
+    blocks = ring_gather(own)
+    parts = []
+    for group in ring_groups():
+        parts.append(gather_tp(jnp.concatenate([blocks[k] for k in group], axis=0)))
+    return jnp.concatenate([part.reshape((-1,) + own.shape[1:]) for part in parts], axis=0)
+
+
+def sum_rows_every(partial, rows):
+    start, sums = 0, {}
+    pieces = []
+    for group in ring_groups():
+        size = 4 * len(group) * rows
+        pieces.append((group, partial[start : start + size]))
+        start += size
+    for group, piece in reversed(pieces):
+        total = sum_tp_quarter(piece.reshape((4, len(group) * rows) + partial.shape[1:]))
+        for place, k in enumerate(group):
+            sums[k] = total[place * rows : (place + 1) * rows]
+    return ring_sum(lambda k: sums[k])
 
 
 def layer_norm(values, gain, shift):
@@ -173,20 +269,68 @@
     qcols = res_q.shape[1]
     kvcols = RES_HEAD
 
-    qkv_shard = vis_qkv.transpose(1, 0, 2)
-    qkv_full = gather_blk_later(qkv_shard)
-    qkv_full = qkv_full.transpose(1, 0, 2, 3).reshape(3, wide, -1)
+    attn_shard = jnp.concatenate([vis_qkv.transpose(1, 0, 2), vis_out.T[None]], axis=0)
+    attn_ring = ring_gather(attn_shard)
+    attn_full = place_blocks(attn_ring)
+    attn_full = attn_full.transpose(1, 0, 2, 3).reshape(4, wide, -1)
+    qkv_full, out_full = attn_full[:3], attn_full[3]
     gu_chunks = proj_gate_up.reshape(wcol, 2, blk, unit).transpose(2, 1, 0, 3)
-    gu_own = exchange(gu_chunks, "blk").transpose(1, 0, 2, 3).reshape(2, wide, unit)
-    out_full = gather_blk_later(vis_out.T).reshape(wide, -1)
-    fc1_full = gather_blk_later(vis_fc1).reshape(wide, -1)
+    fc1_ring = ring_gather(after(vis_fc1, attn_ring[blk // 2]))
+    fc1_full = place_blocks(fc1_ring).reshape(wide, -1)
     fc2_full = gather_blk_later(vis_fc2.T).reshape(wide, -1)
-    rout_full = gather_blk_later(res_out.T).reshape(text, -1)
     rkv_own = res_kv.reshape(tcol, 2 * kvcols)
     rkv_quad = gather_tp(rkv_own)
 
     latent_in = latents.astype(F32)
     latent_low = rms_norm(latent_in, res_gains[1]).astype(BF)
+    all_images = stream_images(image_patches, span_order, tok)
+    own_images = lax.dynamic_slice_in_dim(all_images, b * tok, tok)
+    allowed_vis = own_images[:, None] == all_images[None, :]
+    inputs = patches.astype(F32)
+    normed_one, norm_one_pull = jax.vjp(layer_norm, inputs, vis_gains[0], vis_shifts[0])
+    attn_input = normed_one.astype(BF)
+    query_rows = (dot(attn_input, qkv_full[0], 1, 0) + vis_qv_bias[0]).astype(BF)
+    key_rows = dot(attn_input, qkv_full[1], 1, 0).astype(BF)
+    value_rows = (dot(attn_input, qkv_full[2], 1, 0) + vis_qv_bias[1]).astype(BF)
+    kv_all = jnp.stack(ring_gather(jnp.concatenate([key_rows, value_rows], axis=1)))
+    rout_full = gather_blk_later(after(res_out.T, attn_ring[blk // 2])).reshape(text, -1)
+    key_all = kv_all[:, :, : heads * HEAD_VIS].reshape(tokens, heads, HEAD_VIS)
+    value_all = kv_all[:, :, heads * HEAD_VIS :].reshape(tokens, heads, HEAD_VIS)
+    ring_images = jnp.stack(
+        [all_images.reshape(blk, tok)[ring_index(k)] for k in range(blk)]
+    ).reshape(-1)
+    allowed_ring = own_images[:, None] == ring_images[None, :]
+    query_heads = query_rows.reshape(tok, heads, HEAD_VIS)
+    key_heads = key_rows.reshape(tok, heads, HEAD_VIS)
+    value_heads = value_rows.reshape(tok, heads, HEAD_VIS)
+    vis_scale = HEAD_VIS ** (-0.5)
+    scores = mm("qhd,khd->hqk", query_heads, key_all) * vis_scale
+    scores = jnp.where(allowed_ring[None], scores, -jnp.inf)
+    row_top = jnp.max(scores, axis=-1)
+    weights = jnp.exp(scores - row_top[..., None])
+    weight_sum = jnp.sum(weights, axis=-1)
+    weighted = mm("hqk,khd->hqd", weights.astype(BF), value_all)
+    vis_lse = row_top + jnp.log(weight_sum)
+    vis_result = (weighted / weight_sum[..., None]).transpose(1, 0, 2)
+    attn_output = vis_result.astype(BF).reshape(tok, -1)
+
+    gate_own = exchange(after(gu_chunks[:, 0], kv_all), "blk").reshape(wide, unit)
+    up_own = exchange(after(gu_chunks[:, 1], gate_own), "blk").reshape(wide, unit)
+
+    hidden_one = inputs + sum_tp(dot(attn_output, out_full, 1, 1)) + vis_out_bias[0]
+    hidden_one, gate_own = lax.optimization_barrier((hidden_one, gate_own))
+    normed_two, norm_two_pull = jax.vjp(layer_norm, hidden_one, vis_gains[1], vis_shifts[1])
+    mlp_input = normed_two.astype(BF)
+    fc1_pre = dot(mlp_input, fc1_full, 1, 0) + vis_fc1_bias
+    fc1_act, gelu_pull = jax.vjp(gelu_tanh, fc1_pre)
+    fc1_low = fc1_act.astype(BF)
+    fc2_part = dot(fc1_low, fc2_full, 1, 1).reshape(4, sub, wide)
+    hidden_sub = lax.dynamic_slice_in_dim(hidden_one, t * sub, sub)
+    vision_sub = hidden_sub + sum_tp_quarter(fc2_part) + vis_out_bias[1]
+    vision_sub, up_own, rout_full = lax.optimization_barrier((vision_sub, up_own, rout_full))
+    vision_low = gather_every(vision_sub.astype(BF)).reshape(tokens, wide)
+
+    latent_low = after(latent_low, hidden_one)
     latent_cols = exchange(latent_low.reshape(lat, blk, tcol).transpose(1, 0, 2), "blk")
     latent_cols = latent_cols.reshape(lats, tcol)
     latent_qkv = sum_blk(
@@ -194,61 +338,25 @@
         .astype(BF)
         .reshape(blk, lat, qcols + 2 * kvcols)
     ).astype(BF)
+
+    vision_low, latent_qkv = lax.optimization_barrier((vision_low, latent_qkv))
     latent_query = latent_qkv[:, :qcols]
     latent_kv = latent_qkv[:, qcols:]
 
-    all_images = stream_images(image_patches, span_order, tok)
-    own_images = lax.dynamic_slice_in_dim(all_images, b * tok, tok)
-    allowed_vis = own_images[:, None] == all_images[None, :]
-    inputs = patches.astype(F32)
-    normed_one, norm_one_pull = jax.vjp(layer_norm, inputs, vis_gains[0], vis_shifts[0])
-    attn_input = normed_one.astype(BF)
-    attn_cols = exchange(attn_input.reshape(tok, blk, wcol).transpose(1, 0, 2), "blk")
-    attn_cols = attn_cols.reshape(tokens, wcol)
-    query_rows = (dot(attn_input, qkv_full[0], 1, 0) + vis_qv_bias[0]).astype(BF)
-    key_rows = dot(attn_input, qkv_full[1], 1, 0).astype(BF)
-    value_rows = (dot(attn_input, qkv_full[2], 1, 0) + vis_qv_bias[1]).astype(BF)
-    kv_all = gather_blk(jnp.stack([key_rows, value_rows]))
-    query_all = gather_blk_later(query_rows).reshape(tokens, heads, HEAD_VIS)
-    key_all = kv_all[:, 0].reshape(tokens, heads, HEAD_VIS)
-    value_all = kv_all[:, 1].reshape(tokens, heads, HEAD_VIS)
-    query_heads = query_rows.reshape(tok, heads, HEAD_VIS)
-    key_heads = key_rows.reshape(tok, heads, HEAD_VIS)
-    value_heads = value_rows.reshape(tok, heads, HEAD_VIS)
-    vis_scale = HEAD_VIS ** (-0.5)
-    scores = mm("qhd,khd->hqk", query_heads, key_all) * vis_scale
-    scores = jnp.where(allowed_vis[None], scores, -jnp.inf)
-    row_top = jnp.max(scores, axis=-1)
-    weights = jnp.exp(scores - row_top[..., None])
-    weight_sum = jnp.sum(weights, axis=-1)
-    weighted = mm("hqk,khd->hqd", weights.astype(BF), value_all)
-    vis_lse = row_top + jnp.log(weight_sum)
-    vis_result = (weighted / weight_sum[..., None]).transpose(1, 0, 2)
-    attn_output = vis_result.astype(BF).reshape(tok, -1)
-
-    hidden_one = inputs + sum_tp(dot(attn_output, out_full, 1, 1)) + vis_out_bias[0]
-    normed_two, norm_two_pull = jax.vjp(layer_norm, hidden_one, vis_gains[1], vis_shifts[1])
-    mlp_input = normed_two.astype(BF)
-    mlp_cols = exchange(mlp_input.reshape(tok, blk, wcol).transpose(1, 0, 2), "blk")
-    mlp_cols = mlp_cols.reshape(tokens, wcol)
-    fc1_pre = dot(mlp_input, fc1_full, 1, 0) + vis_fc1_bias
-    fc1_act, gelu_pull = jax.vjp(gelu_tanh, fc1_pre)
-    fc1_low = fc1_act.astype(BF)
-    fc2_part = dot(fc1_low, fc2_full, 1, 1).reshape(4, sub, wide)
-    hidden_sub = lax.dynamic_slice_in_dim(hidden_one, t * sub, sub)
-    vision_sub = hidden_sub + sum_tp_quarter(fc2_part) + vis_out_bias[1]
-    vision_low = gather_every(vision_sub.astype(BF)).reshape(tokens, wide)
-    attn_out_all = gather_blk_later(attn_output).reshape(tokens, -1)
-    fc1_low_all = gather_blk_later(fc1_low).reshape(tokens, -1)
-
-    gate = dot(vision_low, gu_own[0], 1, 0)
-    up = dot(vision_low, gu_own[1], 1, 0)
+    gate = dot(vision_low, gate_own, 1, 0)
+    up = dot(vision_low, up_own, 1, 0)
     proj_hidden, proj_pull = jax.vjp(swiglu, gate, up)
-    proj_all = gather_blk_later(proj_hidden.astype(BF))
+    proj_ring = ring_gather(proj_hidden.astype(BF))
     pdown = proj_down.reshape(blk, unit, tcol)
-    context_part = mm("bth,bhc->tc", proj_all, pdown)
+    pdown_ring = [lax.dynamic_index_in_dim(pdown, ring_index(k), 0, False) for k in range(blk)]
+    context_part = dot(proj_ring[0], pdown_ring[0], 1, 0)
+    for k in sorted(range(1, blk), key=lambda k: min(k, blk - k)):
+        context_part = context_part + dot(proj_ring[k], pdown_ring[k], 1, 0)
+    kept = jnp.concatenate([query_rows, attn_output, fc1_low], axis=1)
+    kept_all = gather_blk_later(after(kept, context_part)).reshape(tokens, -1)
     quarter = tokens // 4
     context = sum_tp_quarter(context_part.reshape(4, quarter, tcol))
+    gain_latent_own = lax.dynamic_slice_in_dim(res_gains[1], b * tcol, tcol)
     gain_context_own = lax.dynamic_slice_in_dim(res_gains[0], b * tcol, tcol)
     scaled_low = (context * gain_context_own).astype(BF)
     kv_part = mm("kc,tcj->tkj", scaled_low, rkv_quad)
@@ -291,28 +399,30 @@
         dot(result_low, rout_full, 1, 1).reshape(4, lsub, text)
     )
     post_normed, post_pull = jax.vjp(rms_norm, latent_one, res_gains[2])
-    post_all = gather_every(post_normed.astype(BF)).reshape(lats, text)
-    result_all = gather_blk_later(result_low).reshape(lats, qcols)
+    post_all = gather_rows_every(post_normed.astype(BF))
     gate_up_two = mm("td,dje->tje", post_all, res_gate_up)
     mlp_hidden, mlp_pull = jax.vjp(swiglu, gate_up_two[:, 0], gate_up_two[:, 1])
     mlp_low = mlp_hidden.astype(BF)
-    down_part = dot(mlp_low, res_down, 1, 0).reshape(4, blk, lsub, text)
-    latent_two = latent_one + sum_every(down_part)
+    latent_two = latent_one + sum_rows_every(dot(mlp_low, res_down, 1, 0), lsub)
+    latent_two, kept_all = lax.optimization_barrier((latent_two, kept_all))
+    width = heads * HEAD_VIS
+    query_all = kept_all[:, :width].reshape(tokens, heads, HEAD_VIS)
+    attn_out_all = kept_all[:, width : 2 * width]
+    fc1_low_all = kept_all[:, 2 * width :]
     final_normed, final_pull = jax.vjp(rms_norm, latent_two, res_gains[3])
     grad_sub = lax.dynamic_slice_in_dim(out_grad, t * lsub, lsub).astype(F32)
     dlatent_two, gain_final = final_pull(grad_sub)
     latents_out = gather_tp(final_normed).reshape(lat, text)
 
-    dmlp_all = gather_every(dlatent_two.astype(BF)).reshape(lats, text)
+    dmlp_all = gather_rows_every(dlatent_two.astype(BF))
     dgate_two, dup_two = mlp_pull(dot(dmlp_all, res_down, 1, 1))
     dgate_up_two = jnp.stack([dgate_two, dup_two], axis=1).astype(BF)
-    dpost_part = mm("tje,dje->td", dgate_up_two, res_gate_up).reshape(4, blk, lsub, text)
-    dpost = sum_every(dpost_part)
-    grad_res_down = dot(mlp_low, dmlp_all, 0, 0)
-    grad_res_gate_up = mm("td,tje->dje", post_all, dgate_up_two)
+    dpost = sum_rows_every(mm("tje,dje->td", dgate_up_two, res_gate_up), lsub)
     dlatent_part, gain_post = post_pull(dpost)
     dlatent_one = dlatent_two + dlatent_part
     dattn_low = gather_tp(dlatent_one.astype(BF)).reshape(lat, text)
+    gain_rows = jnp.stack([gain_post, gain_final]).reshape(2, 4, -1).transpose(1, 0, 2)
+    gain_rows = sum_tp_quarter(gain_rows)
 
     dresult = dot(dattn_low, rout_full, 1, 0).astype(BF)
     dresult_heads = dresult.reshape(lat, group, RES_HEAD)
@@ -352,27 +462,28 @@
     context_low = (unit_context * gain_context_own).astype(BF)
 
     dcontext_low = gather_tp(dcontext.astype(BF)).reshape(tokens, tcol)
-    dproj_part = mm("tc,bhc->bth", dcontext_low, pdown)
-    dproj = sum_blk(dproj_part)
-    dgate, dup = proj_pull(dproj)
-    dgate_low, dup_low = dgate.astype(BF), dup.astype(BF)
-    dvision_part = dot(dgate_low, gu_own[0], 1, 1) + dot(dup_low, gu_own[1], 1, 1)
-    dvision_sub = sum_every(dvision_part.reshape(4, blk, sub, wide))
-    dvision_out = gather_tp(dvision_sub).reshape(tok, wide)
-    grad_proj_down = mm("bth,tc->bhc", proj_all, dcontext_low).reshape(hidden, tcol)
-    grad_gu = jnp.stack([dot(vision_low, dgate_low, 0, 0), dot(vision_low, dup_low, 0, 0)])
-    grad_gu = exchange(grad_gu.astype(BF).reshape(2, blk, wcol, unit).transpose(1, 0, 2, 3), "blk")
-    grad_proj_gate_up = grad_gu.transpose(2, 1, 0, 3).reshape(wcol, 2, hidden).astype(F32)
-
-    dqkv_rows = gather_blk_later(jnp.concatenate([dquery_own, dlatent_kv], axis=1))
-    dqkv_rows = dqkv_rows.reshape(lats, qcols + 2 * kvcols)
-    dquery_all, dlkv_all = dqkv_rows[:, :qcols], dqkv_rows[:, qcols:]
+    dproj = ring_sum(lambda k: dot(dcontext_low, pdown_ring[k], 1, 1))
+    mlp_late, post_late = after(mlp_low, dcontext_low), after(post_all, dcontext_low)
+    grad_res_down = dot(mlp_late, dmlp_all, 0, 0)
+    grad_res_gate_up = mm("td,tje->dje", post_late, dgate_up_two)
+    grad_proj_down = jnp.zeros((blk, unit, tcol), F32)
+    for k in range(blk):
+        grad_proj_down = lax.dynamic_update_index_in_dim(
+            grad_proj_down, dot(proj_ring[k], dcontext_low, 0, 0), ring_index(k), 0
+        )
+    grad_proj_down = grad_proj_down.reshape(hidden, tcol)
+    res_rows = jnp.concatenate([dquery_own, dlatent_kv, result_low], axis=1)
+    res_rows = gather_blk(after(res_rows, dcontext_low))
+    res_rows = res_rows.reshape(lats, -1)
+    dquery_all, dlkv_all = res_rows[:, :qcols], res_rows[:, qcols : qcols + 2 * kvcols]
+    result_all = res_rows[:, qcols + 2 * kvcols :]
     grad_res_q = dot(latent_cols, dquery_all, 0, 0)
     grad_res_kv = dot(latent_cols, dlkv_all, 0, 0) + sum_tp_quarter(
         mm("kc,tkj->tcj", context_low, dpatch_quad)
     )
     grad_res_kv = grad_res_kv.reshape(tcol, 2, kvcols)
     dlatent_part = dot(dquery_all, res_q, 1, 1) + dot(dlkv_all, rkv_own, 1, 1)
+    gain_latent = jnp.sum(dlatent_part * latent_cols.astype(F32), axis=0) / gain_latent_own
     dlatent_rows = exchange(dlatent_part.astype(BF).reshape(4 * blk, lsub, tcol), EVERY)
     dlatent_normed = (
         jnp.sum(dlatent_rows.reshape(blk, 4, lsub, tcol).astype(F32), axis=1)
@@ -380,16 +491,24 @@
         .reshape(lsub, text)
     )
     latent_pull = jax.vjp(rms_norm, latent_sub, res_gains[1])[1]
-    dlatent_in, gain_latent = latent_pull(dlatent_normed)
+    dlatent_in, _ = latent_pull(dlatent_normed)
     latents_grad = gather_tp(dlatent_one + dlatent_in).reshape(lat, text)
     dattn_cols = exchange(dattn_low.reshape(lat, blk, tcol).transpose(1, 0, 2), "blk")
     grad_res_out = dot(result_all, dattn_cols.reshape(lats, tcol), 0, 0)
-    gain_context_full = lax.dynamic_update_slice_in_dim(
-        jnp.zeros((text,), F32), gain_context, b * tcol, 0
-    )
-    grad_res_gains = sum_small(
-        jnp.concatenate([gain_context_full, gain_latent, gain_post, gain_final])
-    ).reshape(4, text)
+    gain_cols = sum_tp(jnp.stack([gain_context, gain_latent]))
+    dproj, grad_res_down, grad_res_gate_up, grad_proj_down, latents_grad, grad_res_out = (
+        lax.optimization_barrier(
+            (dproj, grad_res_down, grad_res_gate_up, grad_proj_down, latents_grad, grad_res_out)
+        )
+    )
+    dgate, dup = proj_pull(dproj)
+    dgate_low, dup_low = dgate.astype(BF), dup.astype(BF)
+    dvision_part = dot(dgate_low, gate_own, 1, 1) + dot(dup_low, up_own, 1, 1)
+    dvision_sub = sum_every(dvision_part.reshape(4, blk, sub, wide))
+    dvision_out = gather_tp(dvision_sub).reshape(tok, wide)
+    vision_late = after(vision_low, dvision_sub)
+    grad_gu = jnp.stack([dot(vision_late, dgate_low, 0, 0), dot(vision_late, dup_low, 0, 0)])
+    grad_gu = exchange(grad_gu.astype(BF).reshape(2, blk, wcol, unit).transpose(1, 0, 2, 3), "blk")
 
     dfc2_low = dvision_out.astype(BF)
     bias_two = jnp.sum(dfc2_low.astype(F32), axis=0)
@@ -403,6 +522,15 @@
     dattn_total = dhidden_one.astype(BF)
     bias_one = jnp.sum(dattn_total.astype(F32), axis=0)
     dattn_output = dot(dattn_total, out_full, 1, 0).astype(BF)
+    grad_res_gate_up = with_layout_constraint(
+        grad_res_gate_up, Layout(major_to_minor=(0, 1, 2))
+    )
+    dattn_output, grad_gu, grad_res_gate_up = lax.optimization_barrier(
+        (dattn_output, grad_gu, grad_res_gate_up)
+    )
+    grad_proj_gate_up = grad_gu.transpose(2, 1, 0, 3).reshape(wcol, 2, hidden).astype(F32)
+    cols = after(jnp.stack([attn_input, mlp_input, dfc2_low, dattn_total]), dattn_output)
+    cols = exchange(cols.reshape(4, tok, blk, wcol).transpose(2, 0, 1, 3), "blk")
 
     dout_heads = dattn_output.reshape(tok, heads, HEAD_VIS)
     vis_delta = jnp.sum(dout_heads.astype(F32) * vis_result, axis=-1)
@@ -414,7 +542,6 @@
             axis=1,
         )
     ).reshape(tokens, -1)
-    width = heads * HEAD_VIS
     row_values = dout_all[:, width:].astype(F32).reshape(tokens, 2, 2, heads).sum(axis=2)
     delta_all, lse_all = row_values[:, 0].T, row_values[:, 1].T
     dout_all_heads = dout_all[:, :width].reshape(tokens, heads, HEAD_VIS)
@@ -436,10 +563,18 @@
             dvalue_home.reshape(tok, -1),
         ]
     ).astype(BF)
+    dqkv_low, cols = lax.optimization_barrier((dqkv_low, cols))
     bias_qv = jnp.stack(
         [jnp.sum(dqkv_low[0].astype(F32), axis=0), jnp.sum(dqkv_low[2].astype(F32), axis=0)]
     )
-    dqkv_all = gather_blk(dqkv_low)
+    attn_cols, mlp_cols, dfc2_cols, dattn_vis_cols = (
+        cols[:, j].reshape(tokens, wcol) for j in range(4)
+    )
+    dqkv_ring = ring_gather(jnp.concatenate(list(dqkv_low), axis=1))
+    dqkv_ring = jnp.concatenate(dqkv_ring, axis=0)
+    attn_cols_ring = jnp.concatenate(
+        [lax.dynamic_slice_in_dim(attn_cols, ring_index(k) * tok, tok) for k in range(blk)]
+    )
     dnormed_one = sum_tp(
         dot(dqkv_low[0], qkv_full[0], 1, 1)
         + dot(dqkv_low[1], qkv_full[1], 1, 1)
@@ -448,21 +583,10 @@
     dinput_part, gain_one, shift_one = norm_one_pull(dnormed_one)
     patches_grad = dhidden_one + dinput_part
 
-    dcols = exchange(
-        jnp.stack([dfc2_low, dattn_total]).reshape(2, tok, blk, wcol).transpose(2, 0, 1, 3), "blk"
-    )
-    dfc2_cols = dcols[:, 0].reshape(tokens, wcol)
-    dattn_vis_cols = dcols[:, 1].reshape(tokens, wcol)
     grad_vis_fc2 = dot(dfc2_cols, fc1_low_all, 0, 0).T
     grad_vis_out = dot(dattn_vis_cols, attn_out_all, 0, 0).T
     grad_vis_fc1 = dot(mlp_cols, dfc1_all, 0, 0)
-    grad_vis_qkv = jnp.stack(
-        [
-            dot(attn_cols, dqkv_all[:, j].reshape(tokens, -1), 0, 0)
-            for j in range(3)
-        ],
-        axis=1,
-    )
+    grad_vis_qkv = dot(attn_cols_ring, dqkv_ring, 0, 0).reshape(wcol, 3, -1)
     small = jnp.concatenate(
         [
             gain_one,
@@ -473,14 +597,21 @@
             bias_two,
             bias_qv.reshape(-1),
             bias_fc1,
+            gain_rows.reshape(-1),
+            gain_cols.reshape(-1),
         ]
     )
-    small = jnp.sum(gather_blk(small), axis=0)
+    small = gather_blk(small)
+    gain_cols = small[:, small.shape[1] - 2 * tcol :].reshape(blk, 2, tcol)
+    small = jnp.sum(small[:, : small.shape[1] - 2 * tcol], axis=0)
+    gain_rows = gather_tp(small[small.shape[0] - text // 2 :].reshape(2, text // 4))
+    gain_rows = gain_rows.transpose(1, 0, 2).reshape(2, text)
+    grad_res_gains = jnp.concatenate([gain_cols.transpose(1, 0, 2).reshape(2, text), gain_rows])
     grad_vis_gains = small[: 2 * wide].reshape(2, wide)
     grad_vis_shifts = small[2 * wide : 4 * wide].reshape(2, wide)
     grad_vis_out_bias = small[4 * wide : 6 * wide].reshape(2, wide)
     grad_vis_qv_bias = small[6 * wide : 6 * wide + 2 * width].reshape(2, width)
-    grad_vis_fc1_bias = small[6 * wide + 2 * width :]
+    grad_vis_fc1_bias = small[6 * wide + 2 * width : 6 * wide + 2 * width + bias_fc1.shape[0]]
     return (
         latents_out,
         patches_grad,

time: 1560 us -> 1180 us (0.76)
  blocking collectives: 489 us -> 43.6 us
  starting transfers between devices: 111 us -> 236 us
  waiting for transfers between devices: 596 us -> 482 us
  matrix products: 120 us -> 149 us
  between operations: 17.7 us -> 35.1 us
    all_gather x5 -> x0, blocking collectives: 352 us -> none  [gather_blk_later(): return lax.all_gather(value, 'blk', axis=0, tiled=False)]
    ppermute x0 -> x80, waiting for transfers between devices: none -> 242 us  [pass_on(): return lax.ppermute(value, 'blk', route)]
    all_gather x7 -> x4, waiting for transfers between devices: 190 us -> 2.14 us  [gather_blk_later(): return lax.all_gather(value, 'blk', axis=0, tiled=False)]
    ppermute x0 -> x80, starting transfers between devices: none -> 120 us  [pass_on(): return lax.ppermute(value, 'blk', route)]
    all_to_all x5 -> x2, blocking collectives: 137 us -> 43.6 us  [exchange(): return lax.all_to_all(chunks, axis, 0, 0, tiled=True)]
    all_to_all x21 -> x15, waiting for transfers between devices: 228 us -> 152 us  [exchange(): return lax.all_to_all(chunks, axis, 0, 0, tiled=True)]
    ppermute x19 -> x38, waiting for transfers between devices: 153 us -> 79.5 us  [swap_x(): lax.ppermute(value, 'tp', [(i, i ^ 2) for i in range(lax.axis_size('tp'))])]
    dot_general x36 -> x58, matrix products: 62.1 us -> 114 us  [dot(): lax.dot_general(left, right, (((on_left,), (on_right,)), ((), ())), prefe...]
  transfers between devices with their start and end apart: 66 -> 175, of which waited for: 45 -> 90; matrix products, arithmetic and copies ran while one was open for 17% -> 24% of each run, Pallas kernels for 0% -> 0%
where the time goes in v2:
time: 1180 us; the launch traced here: 1170 us
  waiting for transfers between devices  482 us (41%)
  starting transfers between devices  236 us (20%)
  matrix products  149 us (13%)
  local copies, waits for them, and re-layouts  143 us (12%)
  other arithmetic  75.7 us (6%)
  blocking collectives  43.6 us (4%)
  between operations  35.1 us (3%)
    ppermute x80, waiting for transfers between devices, pass_on(): return lax.ppermute(value, 'blk', route)  242 us
    all_to_all x15, waiting for transfers between devices, exchange(): return lax.all_to_all(chunks, axis, 0, 0, tiled=True)  152 us
    ppermute x80, starting transfers between devices, pass_on(): return lax.ppermute(value, 'blk', route)  120 us
    dot_general x58, matrix products, dot(): lax.dot_general(left, right, (((on_left,), (on_right,)), ((), ())), prefe...  114 us
    ppermute x38, waiting for transfers between devices, swap_x(): lax.ppermute(value, 'tp', [(i, i ^ 2) for i in range(lax.axis_size('tp'))])  79.5 us
    all_to_all x15, starting transfers between devices, exchange(): return lax.all_to_all(chunks, axis, 0, 0, tiled=True)  66.2 us
    all_to_all x2, blocking collectives, exchange(): return lax.all_to_all(chunks, axis, 0, 0, tiled=True)  43.6 us
    ppermute x38, starting transfers between devices, swap_x(): lax.ppermute(value, 'tp', [(i, i ^ 2) for i in range(lax.axis_size('tp'))])  43.3 us
  transfers between devices with their start and end apart: 175, of which 90 were waited for; matrix products, arithmetic and copies ran while one was open for 24% of the time, Pallas kernels for 0%

profile of v2, /device:TPU:0, one launch (start us, length us, event | category | flops | bytes accessed | tf_op | source)
XLA Modules:
  0.0 1166.4 jit_solution(6020789647549695290)
XLA Ops:
  39.0 15.1 %collective-permute-done.6.refs_6_ = bf16[4,144,288]{2,1,0:T(8,128)(2,1)S(1)} collective-permute-done((bf16[4,144,288]{2,1,0:T(8,128)(2,1)S(1)}, bf16[4,144,288]{2,1,0:T(8,128)(2,1)S(1)}, u32[]{:S(2)}, u32[]{:S(2)}) %collective-permute-start.6) | collective-permute-done | bytes 331808 | tf_op jit(solution)/shard_map/ppermute | solution.py:108
  54.1 7.2 collective-permute-start.7
  61.5 8.4 collective-permute-done.3.refs_2_
  69.9 5.8 collective-permute-done.7.refs_5_
  86.6 6.1 reshape.2078
  110.8 6.2 collective-permute-done.11
  125.9 6.1 collective-permute-done.17
  152.1 35.0 %collective-permute-done.25.refs_5_ = bf16[144,1076]{1,0:T(8,128)(2,1)S(1)} collective-permute-done((bf16[144,1076]{1,0:T(8,128)(2,1)S(1)}, bf16[144,1076]{1,0:T(8,128)(2,1)S(1)}, u32[]{:S(2)}, u32[]{:S(2)}) %collective-permute-start.25) | collective-permute-done | bytes 309920 | tf_op jit(solution)/shard_map/ppermute | solution.py:108
  187.1 11.6 collective-permute-start.26
  206.0 6.0 collective-permute-done.27
  227.3 5.1 all-to-all-start.1
  242.1 18.8 %all-to-all-done.1 = bf16[8,144,448]{2,1,0:T(8,128)(2,1)S(1)} async-done(((bf16[8,144,448]{2,1,0:T(8,128)(2,1)}), bf16[8,144,448]{2,1,0:T(8,128)(2,1)S(1)}, u32[]{:S(2)}, u32[]{:S(2)}) %all-to-all-start.1) | async-done | bytes 1032224 | tf_op jit(solution)/shard_map/all_to_all | solution.py:40
  266.6 15.0 %all-to-all-done.2 = bf16[8,32,1152]{2,1,0:T(8,128)(2,1)S(1)} async-done(((bf16[8,32,1152]{2,1,0:T(8,128)(2,1)}), bf16[8,32,1152]{2,1,0:T(8,128)(2,1)S(1)}, u32[]{:S(2)}, u32[]{:S(2)}) %all-to-all-start.2) | async-done | bytes 589856 | tf_op jit(solution)/shard_map/all_to_all | solution.py:40
  286.7 13.2 %all-to-all-done.3 = bf16[8,64,512]{2,1,0:T(8,128)(2,1)S(1)} async-done(((bf16[8,64,512]{2,1,0:T(8,128)(2,1)}), bf16[8,64,512]{2,1,0:T(8,128)(2,1)S(1)}, u32[]{:S(2)}, u32[]{:S(2)}) %all-to-all-start.3) | async-done | bytes 524320 | tf_op jit(solution)/shard_map/all_to_all | solution.py:40
  307.1 15.8 %all-to-all-done.4 = bf16[8,64,576]{2,1,0:T(8,128)(2,1)} async-done(((bf16[8,64,576]{2,1,0:T(8,128)(2,1)}), bf16[8,64,576]{2,1,0:T(8,128)(2,1)}, u32[]{:S(2)}, u32[]{:S(2)}) %all-to-all-start.4) | async-done | bytes 589856 | tf_op jit(solution)/shard_map/all_to_all | solution.py:40
  335.5 19.0 %collective-permute-done.33 = bf16[1024,448]{0,1:T(8,128)(2,1)S(1)} collective-permute-done((bf16[1024,448]{0,1:T(8,128)(2,1)S(1)}, bf16[1024,448]{0,1:T(8,128)(2,1)S(1)}, u32[]{:S(2)}, u32[]{:S(2)}) %collective-permute-start.33) | collective-permute-done | bytes 917536 | tf_op jit(solution)/shard_map/ppermute | solution.py:108
  356.5 18.5 %collective-permute-done.35 = bf16[1024,448]{0,1:T(8,128)(2,1)S(1)} collective-permute-done((bf16[1024,448]{0,1:T(8,128)(2,1)S(1)}, bf16[1024,448]{0,1:T(8,128)(2,1)S(1)}, u32[]{:S(2)}, u32[]{:S(2)}) %collective-permute-start.35) | collective-permute-done | bytes 917536 | tf_op jit(solution)/shard_map/ppermute | solution.py:108
  380.4 14.1 %collective-permute-done.37 = bf16[1024,448]{0,1:T(8,128)(2,1)S(1)} collective-permute-done((bf16[1024,448]{0,1:T(8,128)(2,1)S(1)}, bf16[1024,448]{0,1:T(8,128)(2,1)S(1)}, u32[]{:S(2)}, u32[]{:S(2)}) %collective-permute-start.37) | collective-permute-done | bytes 917536 | tf_op jit(solution)/shard_map/ppermute | solution.py:108
  399.2 6.7 collective-permute-done.38
  412.0 5.8 collective-permute-done
  421.0 7.0 collective-permute-done.41
  430.0 23.0 %all_to_all.89 = bf16[8,5,32,192]{3,2,1,0:T(8,128)(2,1)S(1)} all-to-all(bf16[8,5,32,192]{3,2,1,0:T(8,128)(2,1)S(1)} %copy.617), channel_id=1, replica_groups=mesh['blk'=8,'tp'=4] {'blk'}, dimensions={0} | all-to-all | bytes 983040 | tf_op jit(solution)/shard_map/all_to_all | solution.py:40
  458.7 14.4 %all-to-all-done.6 = bf16[32,32,192]{2,1,0:T(8,128)(2,1)S(1)} async-done(((bf16[32,32,192]{2,1,0:T(8,128)(2,1)}), bf16[32,32,192]{2,1,0:T(8,128)(2,1)S(1)}, u32[]{:S(2)}, u32[]{:S(2)}) %all-to-all-start.6) | async-done | bytes 393248 | tf_op jit(solution)/shard_map/all_to_all | solution.py:40
  493.9 5.8 collective-permute-done.46
  502.7 5.8 collective-permute-done.50
  523.9 5.0 collective-permute-done.60
  556.0 6.8 collective-permute-done.69
  612.6 5.1 collective-permute-done.98
  627.0 5.6 fusion.4
  647.5 6.7 collective-permute-done.107
  694.0 15.5 %all-to-all-done.7 = bf16[32,32,192]{2,1,0:T(8,128)(2,1)S(1)} async-done(((bf16[32,32,192]{2,1,0:T(8,128)(2,1)}), bf16[32,32,192]{2,1,0:T(8,128)(2,1)S(1)}, u32[]{:S(2)}, u32[]{:S(2)}) %all-to-all-start.7) | async-done | bytes 393248 | tf_op jit(solution)/shard_map/all_to_all | solution.py:40
  710.0 20.6 %all_to_all.90 = bf16[8,5,32,192]{3,2,1,0:T(8,128)(2,1)S(1)} all-to-all(bf16[8,5,32,192]{3,2,1,0:T(8,128)(2,1)S(1)} %broadcast_in_dim.167), channel_id=1, replica_groups=mesh['blk'=8,'tp'=4] {'blk'}, dimensions={0} | all-to-all | bytes 983040 | tf_op jit(solution)/shard_map/all_to_all | solution.py:40
  764.6 8.4 fusion.7
  791.1 6.0 collective-permute-start.123
  798.6 5.9 fusion.352
  829.0 6.5 all-to-all-start.10
  850.1 10.0 collective-permute-start.125
  877.8 16.4 %collective-permute-done.129 = bf16[1024,448]{0,1:T(8,128)(2,1)S(1)} collective-permute-done((bf16[1024,448]{0,1:T(8,128)(2,1)S(1)}, bf16[1024,448]{0,1:T(8,128)(2,1)S(1)}, u32[]{:S(2)}, u32[]{:S(2)}) %collective-permute-start.129) | collective-permute-done | bytes 917536 | tf_op jit(solution)/shard_map/ppermute | solution.py:108
  910.9 5.4 collective-permute-done.141
  917.8 10.6 collective-permute-done.133
  929.4 5.1 all-to-all-start.12
  939.3 10.8 all-to-all-done.12
  982.7 28.6 %copy.687 = f32[4096,2,512]{2,1,0:T(2,128)} copy(f32[4096,2,512]{2,0,1:T(8,128)} %fusion.7) | data formatting | bytes 33554432 | tf_op jit(solution)/shard_map/optimization_barrier | solution.py:500
  1013.4 9.9 all-to-all-done.13
  1039.2 6.0 all-to-all-done.14
  1056.9 7.2 reshape.2154
  1072.7 22.2 %all-to-all-done.15 = bf16[8,4,128,144]{2,3,1,0:T(8,128)(2,1)} async-done(((bf16[8,4,128,144]{2,3,1,0:T(8,128)(2,1)}), bf16[8,4,128,144]{2,3,1,0:T(8,128)(2,1)}, u32[]{:S(2)}, u32[]{:S(2)}) %all-to-all-start.15) | async-done | bytes 1179680 | tf_op jit(solution)/shard_map/all_to_all | solution.py:40
  1144.9 7.9 all-to-all-done.16
  (1167 shorter events, 603.9 us)
Async XLA Ops:
  7.2 225.2 %all-gather.9.cloned.1.call-start = ((), (), s32[]{:S(2)}) async-start(), calls=%async_computation.17 | async-start | bytes 2985984 | tf_op jit(solution)/shard_map/all_gather | solution.py:81
  8.4 27.4 %collective-permute-start.5 = (bf16[4,144,288]{2,1,0:T(8,128)(2,1)S(1)}, bf16[4,144,288]{2,1,0:T(8,128)(2,1)S(1)}, u32[]{:S(2)}, u32[]{:S(2)}) collective-permute-start(bf16[4,144,288]{2,1,0:T(8,128)(2,1)S(1)} %pad_maximum_fusion.5.refs_0_), channel_id=1, source_target_pairs={{0,8},{8,16},{16,24},{24,28},{28,20},{20,12},{12,4},{4,0},{1,9},{9... | collective-permute-start | bytes 995336 | tf_op jit(solution)/shard_map/ppermute | solution.py:108
  11.5 27.4 %collective-permute-start.2 = (bf16[4,144,288]{2,1,0:T(8,128)(2,1)S(1)}, bf16[4,144,288]{2,1,0:T(8,128)(2,1)S(1)}, u32[]{:S(2)}, u32[]{:S(2)}) collective-permute-start(bf16[4,144,288]{2,1,0:T(8,128)(2,1)S(1)} %pad_maximum_fusion.5.refs_0_), channel_id=1, source_target_pairs={{0,4},{8,0},{16,8},{24,16},{28,24},{20,28},{12,20},{4,12},{1,5},{9... | collective-permute-start | bytes 995336 | tf_op jit(solution)/shard_map/ppermute | solution.py:108
  39.0 30.9 %collective-permute-start.3 = (bf16[4,144,288]{2,1,0:T(8,128)(2,1)S(1)}, bf16[4,144,288]{2,1,0:T(8,128)(2,1)S(1)}, u32[]{:S(2)}, u32[]{:S(2)}) collective-permute-start(bf16[4,144,288]{2,1,0:T(8,128)(2,1)S(1)} %collective-permute-done.2.refs_1_), channel_id=1, source_target_pairs={{0,4},{8,0},{16,8},{24,16},{28,24},{20,28},{12,20},{4,12},{1,5},{9... | collective-permute-start | bytes 995336 | tf_op jit(solution)/shard_map/ppermute | solution.py:108
  54.1 21.6 %collective-permute-start.7 = (bf16[4,144,288]{2,1,0:T(8,128)(2,1)S(1)}, bf16[4,144,288]{2,1,0:T(8,128)(2,1)S(1)}, u32[]{:S(2)}, u32[]{:S(2)}) collective-permute-start(bf16[4,144,288]{2,1,0:T(8,128)(2,1)S(1)} %collective-permute-done.6.refs_6_), channel_id=1, source_target_pairs={{0,8},{8,16},{16,24},{24,28},{28,20},{20,12},{12,4},{4,0},{1,9},{9... | collective-permute-start | bytes 995336 | tf_op jit(solution)/shard_map/ppermute | solution.py:108
  76.4 20.7 %collective-permute-start.8 = (bf16[2,144,288]{2,1,0:T(8,128)(2,1)}, bf16[2,144,288]{2,1,0:T(8,128)(2,1)}, u32[]{:S(2)}, u32[]{:S(2)}) collective-permute-start(bf16[2,144,288]{2,1,0:T(8,128)(2,1)} %slice.752), channel_id=1, source_target_pairs={{0,8},{8,16},{16,24},{24,28},{28,20},{20,12},{12,4},{4,0},{1,9},{9... | collective-permute-start | bytes 497672 | tf_op jit(solution)/shard_map/ppermute | solution.py:108
  119.2 30.8 %collective-permute-start.24 = (bf16[144,1076]{1,0:T(8,128)(2,1)S(1)}, bf16[144,1076]{1,0:T(8,128)(2,1)S(1)}, u32[]{:S(2)}, u32[]{:S(2)}) collective-permute-start(bf16[144,1076]{1,0:T(8,128)(2,1)S(1)} %collective-permute-done.23.refs_7_), channel_id=1, source_target_pairs={{0,8},{8,16},{16,24},{24,28},{28,20},{20,12},{12,4},{4,0},{1,9},{9... | collective-permute-start | bytes 929672 | tf_op jit(solution)/shard_map/ppermute | solution.py:108
  121.0 30.9 %collective-permute-start.21 = (bf16[144,1076]{1,0:T(8,128)(2,1)S(1)}, bf16[144,1076]{1,0:T(8,128)(2,1)S(1)}, u32[]{:S(2)}, u32[]{:S(2)}) collective-permute-start(bf16[144,1076]{1,0:T(8,128)(2,1)S(1)} %collective-permute-done.20.refs_1_), channel_id=1, source_target_pairs={{0,4},{8,0},{16,8},{24,16},{28,24},{20,28},{12,20},{4,12},{1,5},{9... | collective-permute-start | bytes 929672 | tf_op jit(solution)/shard_map/ppermute | solution.py:108
  143.7 55.1 %collective-permute-start.18 = (f32[128,1152]{1,0:T(8,128)}, f32[128,1152]{1,0:T(8,128)S(1)}, u32[]{:S(2)}, u32[]{:S(2)}) collective-permute-start(f32[128,1152]{1,0:T(8,128)} %fusion.349), channel_id=1, source_target_pairs={{0,1},{1,0},{2,3},{3,2},{4,5},{5,4},{6,7},{7,6},{8,9},{9,8},{10,11... | collective-permute-start | bytes 1769480 | tf_op jit(solution)/shard_map/ppermute | solution.py:20
  145.3 76.2 %all-to-all-start = ((bf16[8,144,448]{2,1,0:T(8,128)(2,1)}), bf16[8,144,448]{2,1,0:T(8,128)(2,1)}, u32[]{:S(2)}, u32[]{:S(2)}) async-start(bf16[8,144,448]{2,1,0:T(8,128)(2,1)} %get-tuple-element.51), calls=%async_computation | async-start | bytes 2359296 | tf_op jit(solution)/shard_map/all_to_all | solution.py:40
  149.9 111.0 %all-gather.11.cloned.1.call-start = ((), (), s32[]{:S(2)}) async-start(), calls=%async_computation.18 | async-start | bytes 3538944 | tf_op jit(solution)/shard_map/all_gather | solution.py:81
  150.0 37.1 %collective-permute-start.25 = (bf16[144,1076]{1,0:T(8,128)(2,1)S(1)}, bf16[144,1076]{1,0:T(8,128)(2,1)S(1)}, u32[]{:S(2)}, u32[]{:S(2)}) collective-permute-start(bf16[144,1076]{1,0:T(8,128)(2,1)S(1)} %collective-permute-done.24.refs_6_), channel_id=1, source_target_pairs={{0,8},{8,16},{16,24},{24,28},{28,20},{20,12},{12,4},{4,0},{1,9},{9... | collective-permute-start | bytes 929672 | tf_op jit(solution)/shard_map/ppermute | solution.py:108
  151.9 46.8 %collective-permute-start.22 = (bf16[144,1076]{1,0:T(8,128)(2,1)S(1)}, bf16[144,1076]{1,0:T(8,128)(2,1)S(1)}, u32[]{:S(2)}, u32[]{:S(2)}) collective-permute-start(bf16[144,1076]{1,0:T(8,128)(2,1)S(1)} %collective-permute-done.21.refs_2_), channel_id=1, source_target_pairs={{0,4},{8,0},{16,8},{24,16},{28,24},{20,28},{12,20},{4,12},{1,5},{9... | collective-permute-start | bytes 929672 | tf_op jit(solution)/shard_map/ppermute | solution.py:108
  227.3 33.6 %all-to-all-start.1 = ((bf16[8,144,448]{2,1,0:T(8,128)(2,1)}), bf16[8,144,448]{2,1,0:T(8,128)(2,1)S(1)}, u32[]{:S(2)}, u32[]{:S(2)}) async-start(bf16[8,144,448]{2,1,0:T(8,128)(2,1)} %get-tuple-element.54), calls=%async_computation.1 | async-start | bytes 2359296 | tf_op jit(solution)/shard_map/all_to_all | solution.py:40
  261.8 19.8 %all-to-all-start.2 = ((bf16[8,32,1152]{2,1,0:T(8,128)(2,1)}), bf16[8,32,1152]{2,1,0:T(8,128)(2,1)S(1)}, u32[]{:S(2)}, u32[]{:S(2)}) async-start(bf16[8,32,1152]{2,1,0:T(8,128)(2,1)} %broadcast_in_dim.89), calls=%async_computation.2 | async-start | bytes 1179648 | tf_op jit(solution)/shard_map/all_to_all | solution.py:40
  285.3 20.6 %collective-permute-start.30 = (bf16[8,32,1152]{2,1,0:T(8,128)(2,1)S(1)}, bf16[8,32,1152]{2,1,0:T(8,128)(2,1)S(1)}, u32[]{:S(2)}, u32[]{:S(2)}) collective-permute-start(bf16[8,32,1152]{2,1,0:T(8,128)(2,1)S(1)} %all-to-all-done.2), channel_id=1, source_target_pairs={{0,2},{1,3},{2,0},{3,1},{4,6},{5,7},{6,4},{7,5},{8,10},{9,11},{10,... | collective-permute-start | bytes 1769480 | tf_op jit(solution)/shard_map/ppermute | solution.py:24
  301.6 21.2 %all-to-all-start.4 = ((bf16[8,64,576]{2,1,0:T(8,128)(2,1)}), bf16[8,64,576]{2,1,0:T(8,128)(2,1)}, u32[]{:S(2)}, u32[]{:S(2)}) async-start(bf16[8,64,576]{2,1,0:T(8,128)(2,1)} %pad_maximum_fusion.4), calls=%async_computation.4 | async-start | bytes 1310720 | tf_op jit(solution)/shard_map/all_to_all | solution.py:40
  333.5 21.0 %collective-permute-start.33 = (bf16[1024,448]{0,1:T(8,128)(2,1)S(1)}, bf16[1024,448]{0,1:T(8,128)(2,1)S(1)}, u32[]{:S(2)}, u32[]{:S(2)}) collective-permute-start(bf16[1024,448]{0,1:T(8,128)(2,1)S(1)} %get-tuple-element.356), channel_id=1, source_target_pairs={{0,8},{8,16},{16,24},{24,28},{28,20},{20,12},{12,4},{4,0},{1,9},{9... | collective-permute-start | bytes 2752520 | tf_op jit(solution)/shard_map/ppermute | solution.py:108
  334.0 20.4 %collective-permute-start.32 = (bf16[1024,448]{0,1:T(8,128)(2,1)S(1)}, bf16[1024,448]{0,1:T(8,128)(2,1)S(1)}, u32[]{:S(2)}, u32[]{:S(2)}) collective-permute-start(bf16[1024,448]{0,1:T(8,128)(2,1)S(1)} %get-tuple-element.356), channel_id=1, source_target_pairs={{0,4},{8,0},{16,8},{24,16},{28,24},{20,28},{12,20},{4,12},{1,5},{9... | collective-permute-start | bytes 2752520 | tf_op jit(solution)/shard_map/ppermute | solution.py:108
  354.5 20.5 %collective-permute-start.35 = (bf16[1024,448]{0,1:T(8,128)(2,1)S(1)}, bf16[1024,448]{0,1:T(8,128)(2,1)S(1)}, u32[]{:S(2)}, u32[]{:S(2)}) collective-permute-start(bf16[1024,448]{0,1:T(8,128)(2,1)S(1)} %collective-permute-done.33), channel_id=1, source_target_pairs={{0,8},{8,16},{16,24},{24,28},{28,20},{20,12},{12,4},{4,0},{1,9},{9... | collective-permute-start | bytes 2752520 | tf_op jit(solution)/shard_map/ppermute | solution.py:108
  354.5 20.5 %collective-permute-start.34 = (bf16[1024,448]{0,1:T(8,128)(2,1)S(1)}, bf16[1024,448]{0,1:T(8,128)(2,1)S(1)}, u32[]{:S(2)}, u32[]{:S(2)}) collective-permute-start(bf16[1024,448]{0,1:T(8,128)(2,1)S(1)} %collective-permute-done.32), channel_id=1, source_target_pairs={{0,4},{8,0},{16,8},{24,16},{28,24},{20,28},{12,20},{4,12},{1,5},{9... | collective-permute-start | bytes 2752520 | tf_op jit(solution)/shard_map/ppermute | solution.py:108
  375.0 19.5 %collective-permute-start.37 = (bf16[1024,448]{0,1:T(8,128)(2,1)S(1)}, bf16[1024,448]{0,1:T(8,128)(2,1)S(1)}, u32[]{:S(2)}, u32[]{:S(2)}) collective-permute-start(bf16[1024,448]{0,1:T(8,128)(2,1)S(1)} %collective-permute-done.35), channel_id=1, source_target_pairs={{0,8},{8,16},{16,24},{24,28},{28,20},{20,12},{12,4},{4,0},{1,9},{9... | collective-permute-start | bytes 2752520 | tf_op jit(solution)/shard_map/ppermute | solution.py:108
  375.0 20.9 %collective-permute-start.36 = (bf16[1024,448]{0,1:T(8,128)(2,1)S(1)}, bf16[1024,448]{0,1:T(8,128)(2,1)S(1)}, u32[]{:S(2)}, u32[]{:S(2)}) collective-permute-start(bf16[1024,448]{0,1:T(8,128)(2,1)S(1)} %collective-permute-done.34), channel_id=1, source_target_pairs={{0,4},{8,0},{16,8},{24,16},{28,24},{20,28},{12,20},{4,12},{1,5},{9... | collective-permute-start | bytes 2752520 | tf_op jit(solution)/shard_map/ppermute | solution.py:108
  457.5 126.0 %all-gather.13.cloned.1.call-start = ((), (), s32[]{:S(2)}) async-start(), calls=%async_computation.19 | async-start | bytes 3815424 | tf_op jit(solution)/shard_map/all_gather | solution.py:81
  499.8 18.9 %collective-permute-start.48 = (bf16[32,4096]{1,0:T(8,128)(2,1)S(1)}, bf16[32,4096]{1,0:T(8,128)(2,1)S(1)}, u32[]{:S(2)}, u32[]{:S(2)}) collective-permute-start(bf16[32,4096]{1,0:T(8,128)(2,1)S(1)} %constant_dynamic-update-slice_fusion.4), channel_id=1, source_target_pairs={{0,2},{1,3},{2,0},{3,1},{4,6},{5,7},{6,4},{7,5},{8,10},{9,11},{10,... | collective-permute-start | bytes 786440 | tf_op jit(solution)/shard_map/ppermute | solution.py:24
  500.5 20.0 %collective-permute-start.45 = (bf16[2,16,4096]{2,1,0:T(8,128)(2,1)S(1)}, bf16[2,16,4096]{2,1,0:T(8,128)(2,1)S(1)}, u32[]{:S(2)}, u32[]{:S(2)}) collective-permute-start(bf16[2,16,4096]{2,1,0:T(8,128)(2,1)S(1)} %maximum_select_fusion.38), channel_id=1, source_target_pairs={{0,1},{1,0},{2,3},{3,2},{4,5},{5,4},{6,7},{7,6},{8,9},{9,8},{10,11... | collective-permute-start | bytes 786440 | tf_op jit(solution)/shard_map/ppermute | solution.py:20
  545.8 33.8 %collective-permute-start.63 = (bf16[16,4096]{1,0:T(8,128)(2,1)S(1)}, bf16[16,4096]{1,0:T(8,128)(2,1)S(1)}, u32[]{:S(2)}, u32[]{:S(2)}) collective-permute-start(bf16[16,4096]{1,0:T(8,128)(2,1)S(1)} %fusion.245), channel_id=1, source_target_pairs={{0,2},{1,3},{2,0},{3,1},{4,6},{5,7},{6,4},{7,5},{8,10},{9,11},{10,... | collective-permute-start | bytes 393224 | tf_op jit(solution)/shard_map/ppermute | solution.py:24
  637.0 32.3 %collective-permute-start.101 = (bf16[16,4096]{1,0:T(8,128)(2,1)S(1)}, bf16[16,4096]{1,0:T(8,128)(2,1)S(1)}, u32[]{:S(2)}, u32[]{:S(2)}) collective-permute-start(bf16[16,4096]{1,0:T(8,128)(2,1)S(1)} %fusion.247), channel_id=1, source_target_pairs={{0,2},{1,3},{2,0},{3,1},{4,6},{5,7},{6,4},{7,5},{8,10},{9,11},{10,... | collective-permute-start | bytes 393224 | tf_op jit(solution)/shard_map/ppermute | solution.py:24
  753.8 50.7 %all-to-all-start.9 = ((bf16[8,64,960]{2,1,0:T(8,128)(2,1)}), bf16[8,64,960]{2,1,0:T(8,128)(2,1)}, u32[]{:S(2)}, u32[]{:S(2)}) async-start(bf16[8,64,960]{2,1,0:T(8,128)(2,1)} %broadcast_in_dim.177), calls=%async_computation.9 | async-start | bytes 2097152 | tf_op jit(solution)/shard_map/all_to_all | solution.py:40
  775.8 33.4 %collective-permute-start.126 = (bf16[512,448]{0,1:T(8,128)(2,1)}, bf16[512,448]{0,1:T(8,128)(2,1)}, u32[]{:S(2)}, u32[]{:S(2)}) collective-permute-start(bf16[512,448]{0,1:T(8,128)(2,1)} %get-tuple-element.293), channel_id=1, source_target_pairs={{0,4},{8,0},{16,8},{24,16},{28,24},{20,28},{12,20},{4,12},{1,5},{9... | collective-permute-start | bytes 1376264 | tf_op jit(solution)/shard_map/ppermute | solution.py:108
  791.1 27.0 %collective-permute-start.123 = (bf16[1024,448]{0,1:T(8,128)(2,1)}, bf16[1024,448]{0,1:T(8,128)(2,1)}, u32[]{:S(2)}, u32[]{:S(2)}) collective-permute-start(bf16[1024,448]{0,1:T(8,128)(2,1)} %add_convert_fusion.5), channel_id=1, source_target_pairs={{0,8},{8,16},{16,24},{24,28},{28,20},{20,12},{12,4},{4,0},{1,9},{9... | collective-permute-start | bytes 2752520 | tf_op jit(solution)/shard_map/ppermute | solution.py:108
  804.5 24.5 %all-to-all-start.11 = ((bf16[8,64,512]{2,1,0:T(8,128)(2,1)}), bf16[8,64,512]{2,1,0:T(8,128)(2,1)S(1)}, u32[]{:S(2)}, u32[]{:S(2)}) async-start(bf16[8,64,512]{2,1,0:T(8,128)(2,1)} %copy.679), calls=%async_computation.11 | async-start | bytes 1048576 | tf_op jit(solution)/shard_map/all_to_all | solution.py:40
  812.4 28.5 %collective-permute-start.127 = (bf16[1024,448]{0,1:T(8,128)(2,1)}, bf16[1024,448]{0,1:T(8,128)(2,1)}, u32[]{:S(2)}, u32[]{:S(2)}) collective-permute-start(bf16[1024,448]{0,1:T(8,128)(2,1)} %add_convert_fusion.2), channel_id=1, source_target_pairs={{0,4},{8,0},{16,8},{24,16},{28,24},{20,28},{12,20},{4,12},{1,5},{9... | collective-permute-start | bytes 2752520 | tf_op jit(solution)/shard_map/ppermute | solution.py:108
  821.1 26.1 %collective-permute-start.124 = (bf16[1024,448]{0,1:T(8,128)(2,1)}, bf16[1024,448]{0,1:T(8,128)(2,1)}, u32[]{:S(2)}, u32[]{:S(2)}) collective-permute-start(bf16[1024,448]{0,1:T(8,128)(2,1)} %add_convert_fusion.4), channel_id=1, source_target_pairs={{0,8},{8,16},{16,24},{24,28},{28,20},{20,12},{12,4},{4,0},{1,9},{9... | collective-permute-start | bytes 2752520 | tf_op jit(solution)/shard_map/ppermute | solution.py:108
  829.0 33.9 %all-to-all-start.10 = ((bf16[32,16,512]{2,1,0:T(8,128)(2,1)}), bf16[32,16,512]{2,1,0:T(8,128)(2,1)S(1)}, u32[]{:S(2)}, u32[]{:S(2)}) async-start(bf16[32,16,512]{2,1,0:T(8,128)(2,1)} %bitcast.267), calls=%async_computation.10 | async-start | bytes 1048576 | tf_op jit(solution)/shard_map/all_to_all | solution.py:40
  844.2 25.1 %collective-permute-start.128 = (bf16[1024,448]{0,1:T(8,128)(2,1)}, bf16[1024,448]{0,1:T(8,128)(2,1)}, u32[]{:S(2)}, u32[]{:S(2)}) collective-permute-start(bf16[1024,448]{0,1:T(8,128)(2,1)} %add_convert_fusion.1), channel_id=1, source_target_pairs={{0,4},{8,0},{16,8},{24,16},{28,24},{20,28},{12,20},{4,12},{1,5},{9... | collective-permute-start | bytes 2752520 | tf_op jit(solution)/shard_map/ppermute | solution.py:108
  850.1 27.7 %collective-permute-start.125 = (bf16[1024,448]{0,1:T(8,128)(2,1)}, bf16[1024,448]{0,1:T(8,128)(2,1)}, u32[]{:S(2)}, u32[]{:S(2)}) collective-permute-start(bf16[1024,448]{0,1:T(8,128)(2,1)} %add_convert_fusion.3), channel_id=1, source_target_pairs={{0,8},{8,16},{16,24},{24,28},{28,20},{20,12},{12,4},{4,0},{1,9},{9... | collective-permute-start | bytes 2752520 | tf_op jit(solution)/shard_map/ppermute | solution.py:108
  871.7 22.5 %collective-permute-start.129 = (bf16[1024,448]{0,1:T(8,128)(2,1)S(1)}, bf16[1024,448]{0,1:T(8,128)(2,1)S(1)}, u32[]{:S(2)}, u32[]{:S(2)}) collective-permute-start(bf16[1024,448]{0,1:T(8,128)(2,1)S(1)} %add_convert_fusion), channel_id=1, source_target_pairs={{0,4},{8,0},{16,8},{24,16},{28,24},{20,28},{12,20},{4,12},{1,5},{9... | collective-permute-start | bytes 2752520 | tf_op jit(solution)/shard_map/ppermute | solution.py:108
  873.6 22.3 %collective-permute-start.131 = (f32[2,16,4096]{2,1,0:T(8,128)S(1)}, f32[2,16,4096]{2,1,0:T(8,128)S(1)}, u32[]{:S(2)}, u32[]{:S(2)}) collective-permute-start(f32[2,16,4096]{2,1,0:T(8,128)S(1)} %maximum_select_fusion.33), channel_id=1, source_target_pairs={{0,1},{1,0},{2,3},{3,2},{4,5},{5,4},{6,7},{7,6},{8,9},{9,8},{10,11... | collective-permute-start | bytes 1572872 | tf_op jit(solution)/shard_map/ppermute | solution.py:20
  929.4 20.7 %all-to-all-start.12 = ((bf16[8,32,1152]{2,1,0:T(8,128)(2,1)}), bf16[8,32,1152]{2,1,0:T(8,128)(2,1)S(1)}, u32[]{:S(2)}, u32[]{:S(2)}) async-start(bf16[8,32,1152]{2,1,0:T(8,128)(2,1)} %fusion.44), calls=%async_computation.12 | async-start | bytes 1179648 | tf_op jit(solution)/shard_map/all_to_all | solution.py:40
  939.3 36.7 %collective-permute-start.154 = (bf16[2,512,192]{1,2,0:T(8,128)(2,1)}, bf16[2,512,192]{1,2,0:T(8,128)(2,1)}, u32[]{:S(2)}, u32[]{:S(2)}) collective-permute-start(bf16[2,512,192]{1,2,0:T(8,128)(2,1)} %fusion.169), channel_id=1, source_target_pairs={{0,1},{1,0},{2,3},{3,2},{4,5},{5,4},{6,7},{7,6},{8,9},{9,8},{10,11... | collective-permute-start | bytes 1179656 | tf_op jit(solution)/shard_map/ppermute | solution.py:20
  963.7 59.6 %all-to-all-start.13 = ((bf16[8,2,144,448]{3,2,1,0:T(8,128)(2,1)}), bf16[8,2,144,448]{3,2,1,0:T(8,128)(2,1)}, u32[]{:S(2)}, u32[]{:S(2)}) async-start(bf16[8,2,144,448]{3,2,1,0:T(8,128)(2,1)} %copy.686), calls=%async_computation.13 | async-start | bytes 4718592 | tf_op jit(solution)/shard_map/all_to_all | solution.py:40
  978.0 52.8 %collective-permute-start.155 = (bf16[512,192]{0,1:T(8,128)(2,1)}, bf16[512,192]{0,1:T(8,128)(2,1)}, u32[]{:S(2)}, u32[]{:S(2)}) collective-permute-start(bf16[512,192]{0,1:T(8,128)(2,1)} %fusion.239), channel_id=1, source_target_pairs={{0,2},{1,3},{2,0},{3,1},{4,6},{5,7},{6,4},{7,5},{8,10},{9,11},{10,... | collective-permute-start | bytes 589832 | tf_op jit(solution)/shard_map/ppermute | solution.py:24
  978.9 32.4 %collective-permute-start.137 = (bf16[128,1152]{1,0:T(8,128)(2,1)S(1)}, bf16[128,1152]{1,0:T(8,128)(2,1)S(1)}, u32[]{:S(2)}, u32[]{:S(2)}) collective-permute-start(bf16[128,1152]{1,0:T(8,128)(2,1)S(1)} %add_convert_fusion.7), channel_id=1, source_target_pairs={{0,2},{1,3},{2,0},{3,1},{4,6},{5,7},{6,4},{7,5},{8,10},{9,11},{10,... | collective-permute-start | bytes 884744 | tf_op jit(solution)/shard_map/ppermute | solution.py:24
  980.2 49.6 %collective-permute-start.142 = (f32[2,512]{1,0:T(2,128)S(1)}, f32[2,512]{1,0:T(2,128)S(1)}, u32[]{:S(2)}, u32[]{:S(2)}) collective-permute-start(f32[2,512]{1,0:T(2,128)S(1)} %pad_maximum_fusion.17), channel_id=1, source_target_pairs={{0,1},{1,0},{2,3},{3,2},{4,5},{5,4},{6,7},{7,6},{8,9},{9,8},{10,11... | collective-permute-start | bytes 12296 | tf_op jit(solution)/shard_map/ppermute | solution.py:20
  1024.3 20.9 %all-to-all-start.14 = ((bf16[8,128,304]{1,2,0:T(8,128)(2,1)}), bf16[8,128,304]{1,2,0:T(8,128)(2,1)}, u32[]{:S(2)}, u32[]{:S(2)}) async-start(bf16[8,128,304]{1,2,0:T(8,128)(2,1)} %broadcast_in_dim.182), calls=%async_computation.14 | async-start | bytes 1245184 | tf_op jit(solution)/shard_map/all_to_all | solution.py:40
  1028.5 77.5 %all-gather.15.cloned.1.call-start = ((), (), s32[]{:S(2)}) async-start(), calls=%async_computation.20 | async-start | bytes 2488320 | tf_op jit(solution)/shard_map/all_gather | solution.py:81
  1045.2 49.7 %all-to-all-start.15 = ((bf16[8,4,128,144]{2,3,1,0:T(8,128)(2,1)}), bf16[8,4,128,144]{2,3,1,0:T(8,128)(2,1)}, u32[]{:S(2)}, u32[]{:S(2)}) async-start(bf16[8,4,128,144]{2,3,1,0:T(8,128)(2,1)} %copy.690), calls=%async_computation.15 | async-start | bytes 2359296 | tf_op jit(solution)/shard_map/all_to_all | solution.py:40
  (319 other events, 4526.4 us)
Sparse Core Ops, SparseCore 0:
  11.7 66.2 all-gather.8
  152.8 79.7 all-gather.10
  485.3 70.8 all-gather.12
  1034.2 71.7 all-gather.14

commit v3 on v2

--- a/solution.py
+++ b/solution.py
@@ -123,7 +123,7 @@
     return blocks
 
 
-def ring_sum(part):
+def ring_sum(part, arrivals=None):
     count = lax.axis_size("blk")
     half = count // 2
     far = part(half)
@@ -136,6 +136,8 @@
             blank = jnp.zeros_like(onward)
             onward = jnp.concatenate([onward, blank], axis=0)
             back = jnp.concatenate([blank, back], axis=0)
+        if arrivals is not None:
+            arrivals.append(onward)
         onward = pass_on((one + onward.astype(F32)).astype(BF), 1)
         back = pass_on((two + back.astype(F32)).astype(BF), -1)
     return part(0) + onward.astype(F32) + back.astype(F32)
@@ -158,6 +160,12 @@
         compiler_params=pltpu.CompilerParams(vmem_limit_bytes=24 * 2**20),
         name="place_blocks",
     )(places, *blocks)
+
+
+def share_columns(rows):
+    parts, own, count, width = rows.shape
+    got = gather_tp(exchange(rows.transpose(2, 0, 1, 3), "blk"))
+    return got.transpose(2, 1, 0, 3, 4).reshape(parts, count * 4 * own, width)
 
 
 def after(value, *others):
@@ -275,14 +283,11 @@
     attn_full = attn_full.transpose(1, 0, 2, 3).reshape(4, wide, -1)
     qkv_full, out_full = attn_full[:3], attn_full[3]
     gu_chunks = proj_gate_up.reshape(wcol, 2, blk, unit).transpose(2, 1, 0, 3)
-    fc1_ring = ring_gather(after(vis_fc1, attn_ring[blk // 2]))
-    fc1_full = place_blocks(fc1_ring).reshape(wide, -1)
+    fc1_full = gather_blk_later(vis_fc1).reshape(wide, -1)
     fc2_full = gather_blk_later(vis_fc2.T).reshape(wide, -1)
     rkv_own = res_kv.reshape(tcol, 2 * kvcols)
     rkv_quad = gather_tp(rkv_own)
 
-    latent_in = latents.astype(F32)
-    latent_low = rms_norm(latent_in, res_gains[1]).astype(BF)
     all_images = stream_images(image_patches, span_order, tok)
     own_images = lax.dynamic_slice_in_dim(all_images, b * tok, tok)
     allowed_vis = own_images[:, None] == all_images[None, :]
@@ -293,7 +298,6 @@
     key_rows = dot(attn_input, qkv_full[1], 1, 0).astype(BF)
     value_rows = (dot(attn_input, qkv_full[2], 1, 0) + vis_qv_bias[1]).astype(BF)
     kv_all = jnp.stack(ring_gather(jnp.concatenate([key_rows, value_rows], axis=1)))
-    rout_full = gather_blk_later(after(res_out.T, attn_ring[blk // 2])).reshape(text, -1)
     key_all = kv_all[:, :, : heads * HEAD_VIS].reshape(tokens, heads, HEAD_VIS)
     value_all = kv_all[:, :, heads * HEAD_VIS :].reshape(tokens, heads, HEAD_VIS)
     ring_images = jnp.stack(
@@ -327,21 +331,17 @@
     fc2_part = dot(fc1_low, fc2_full, 1, 1).reshape(4, sub, wide)
     hidden_sub = lax.dynamic_slice_in_dim(hidden_one, t * sub, sub)
     vision_sub = hidden_sub + sum_tp_quarter(fc2_part) + vis_out_bias[1]
-    vision_sub, up_own, rout_full = lax.optimization_barrier((vision_sub, up_own, rout_full))
-    vision_low = gather_every(vision_sub.astype(BF)).reshape(tokens, wide)
-
-    latent_low = after(latent_low, hidden_one)
-    latent_cols = exchange(latent_low.reshape(lat, blk, tcol).transpose(1, 0, 2), "blk")
-    latent_cols = latent_cols.reshape(lats, tcol)
-    latent_qkv = sum_blk(
-        jnp.concatenate([dot(latent_cols, res_q, 1, 0), dot(latent_cols, rkv_own, 1, 0)], axis=1)
-        .astype(BF)
-        .reshape(blk, lat, qcols + 2 * kvcols)
-    ).astype(BF)
-
-    vision_low, latent_qkv = lax.optimization_barrier((vision_low, latent_qkv))
-    latent_query = latent_qkv[:, :qcols]
-    latent_kv = latent_qkv[:, qcols:]
+    vision_sub, up_own = lax.optimization_barrier((vision_sub, up_own))
+    latent_in = latents.astype(F32)
+    latent_low = rms_norm(latent_in, res_gains[1]).astype(BF)
+    latent_quarter = lax.dynamic_slice_in_dim(latent_low, t * lsub, lsub)
+    latent_quarter = after(latent_quarter, hidden_one)
+    latent_cols = share_columns(latent_quarter.reshape(1, lsub, blk, tcol))[0]
+    vision_low = place_blocks(ring_gather(vision_sub.astype(BF)))
+    vision_low = gather_tp(vision_low).reshape(tokens, wide)
+    latent_part = jnp.concatenate(
+        [dot(latent_cols, res_q, 1, 0), dot(latent_cols, rkv_own, 1, 0)], axis=1
+    )
 
     gate = dot(vision_low, gate_own, 1, 0)
     up = dot(vision_low, up_own, 1, 0)
@@ -352,8 +352,7 @@
     context_part = dot(proj_ring[0], pdown_ring[0], 1, 0)
     for k in sorted(range(1, blk), key=lambda k: min(k, blk - k)):
         context_part = context_part + dot(proj_ring[k], pdown_ring[k], 1, 0)
-    kept = jnp.concatenate([query_rows, attn_output, fc1_low], axis=1)
-    kept_all = gather_blk_later(after(kept, context_part)).reshape(tokens, -1)
+    rout_full = gather_blk_later(after(res_out.T, context_part)).reshape(text, -1)
     quarter = tokens // 4
     context = sum_tp_quarter(context_part.reshape(4, quarter, tcol))
     gain_latent_own = lax.dynamic_slice_in_dim(res_gains[1], b * tcol, tcol)
@@ -363,12 +362,18 @@
     square_part = jnp.sum(context * context, axis=-1)
     high, low = halves(square_part)
     stats = jnp.pad(jnp.stack([high, low], axis=1), ((0, 0), (0, 2 * kvcols - 2)))
-    kv_sums = sum_blk(
+    kv_terms = (
         jnp.concatenate([kv_part, stats[None]], axis=0)
-        .astype(BF)
         .reshape(5, blk, sub, 2 * kvcols)
-        .transpose(1, 0, 2, 3)
-    )
+        .transpose(1, 2, 0, 3)
+        .reshape(blk, sub, -1)
+    )
+    terms = jnp.concatenate([kv_terms, latent_part.reshape(blk, sub, -1)], axis=2)
+    sums = ring_sum(lambda k: lax.dynamic_index_in_dim(terms, ring_index(k), 0, False))
+    kv_sums = sums[:, : 10 * kvcols].reshape(sub, 5, 2 * kvcols).transpose(1, 0, 2)
+    latent_qkv = sums[:, 10 * kvcols :].reshape(lat, qcols + 2 * kvcols).astype(BF)
+    latent_query = latent_qkv[:, :qcols]
+    latent_kv = latent_qkv[:, qcols:]
     scale_sub = lax.rsqrt((kv_sums[4, :, 0] + kv_sums[4, :, 1]) / text + EPSILON)
     patch_kv = (kv_sums[:4] * scale_sub[None, :, None]).astype(BF)
     patch_all = exchange(
@@ -398,17 +403,16 @@
     latent_one = latent_sub + sum_tp_quarter(
         dot(result_low, rout_full, 1, 1).reshape(4, lsub, text)
     )
+    kept = jnp.concatenate(
+        [query_rows, attn_output, result_low.reshape(tok, -1), fc1_low], axis=1
+    )
+    kept_all = gather_blk_later(after(kept, latent_one)).reshape(tokens, -1)
     post_normed, post_pull = jax.vjp(rms_norm, latent_one, res_gains[2])
     post_all = gather_rows_every(post_normed.astype(BF))
     gate_up_two = mm("td,dje->tje", post_all, res_gate_up)
     mlp_hidden, mlp_pull = jax.vjp(swiglu, gate_up_two[:, 0], gate_up_two[:, 1])
     mlp_low = mlp_hidden.astype(BF)
     latent_two = latent_one + sum_rows_every(dot(mlp_low, res_down, 1, 0), lsub)
-    latent_two, kept_all = lax.optimization_barrier((latent_two, kept_all))
-    width = heads * HEAD_VIS
-    query_all = kept_all[:, :width].reshape(tokens, heads, HEAD_VIS)
-    attn_out_all = kept_all[:, width : 2 * width]
-    fc1_low_all = kept_all[:, 2 * width :]
     final_normed, final_pull = jax.vjp(rms_norm, latent_two, res_gains[3])
     grad_sub = lax.dynamic_slice_in_dim(out_grad, t * lsub, lsub).astype(F32)
     dlatent_two, gain_final = final_pull(grad_sub)
@@ -420,10 +424,17 @@
     dpost = sum_rows_every(mm("tje,dje->td", dgate_up_two, res_gate_up), lsub)
     dlatent_part, gain_post = post_pull(dpost)
     dlatent_one = dlatent_two + dlatent_part
+    dlatent_one, kept_all = lax.optimization_barrier((dlatent_one, kept_all))
+    width, each = heads * HEAD_VIS, lat * qcols // tok
+    query_all = kept_all[:, :width].reshape(tokens, heads, HEAD_VIS)
+    attn_out_all = kept_all[:, width : 2 * width]
+    result_all = kept_all[:, 2 * width : 2 * width + each].reshape(lats, qcols)
+    fc1_low_all = kept_all[:, 2 * width + each :]
     dattn_low = gather_tp(dlatent_one.astype(BF)).reshape(lat, text)
-    gain_rows = jnp.stack([gain_post, gain_final]).reshape(2, 4, -1).transpose(1, 0, 2)
-    gain_rows = sum_tp_quarter(gain_rows)
-
+
+    mlp_late, post_late = after(mlp_low, dattn_low), after(post_all, dattn_low)
+    grad_res_down = dot(mlp_late, dmlp_all, 0, 0)
+    grad_res_gate_up = mm("td,tje->dje", post_late, dgate_up_two)
     dresult = dot(dattn_low, rout_full, 1, 0).astype(BF)
     dresult_heads = dresult.reshape(lat, group, RES_HEAD)
     res_delta = jnp.sum(dresult_heads.astype(F32) * res_result, axis=-1).T
@@ -442,6 +453,12 @@
         .astype(F32),
         axis=0,
     )
+    dpatch_sub, grad_res_down, grad_res_gate_up = lax.optimization_barrier(
+        (dpatch_sub, grad_res_down, grad_res_gate_up)
+    )
+    grad_res_gate_up = with_layout_constraint(
+        grad_res_gate_up, Layout(major_to_minor=(0, 1, 2))
+    )
     along = jnp.sum(dpatch_sub * patch_kv.astype(F32), axis=(0, 2)) / text
     a_high, a_low = halves(along)
     s_high, s_low = halves(scale_sub)
@@ -449,6 +466,7 @@
         jnp.stack([a_high, a_low, s_high, s_low], axis=1), ((0, 0), (0, 2 * kvcols - 4))
     )
     dpatch_rows = gather_blk(jnp.concatenate([dpatch_sub, row_stats[None]], axis=0).astype(BF))
+    dpatch_rows, grad_res_gate_up = lax.optimization_barrier((dpatch_rows, grad_res_gate_up))
     dpatch_rows = dpatch_rows.transpose(1, 0, 2, 3).reshape(5, quarter, 2 * kvcols)
     dpatch_quad = dpatch_rows[:4]
     along_rows = dpatch_rows[4, :, 0].astype(F32) + dpatch_rows[4, :, 1].astype(F32)
@@ -462,86 +480,98 @@
     context_low = (unit_context * gain_context_own).astype(BF)
 
     dcontext_low = gather_tp(dcontext.astype(BF)).reshape(tokens, tcol)
-    dproj = ring_sum(lambda k: dot(dcontext_low, pdown_ring[k], 1, 1))
-    mlp_late, post_late = after(mlp_low, dcontext_low), after(post_all, dcontext_low)
-    grad_res_down = dot(mlp_late, dmlp_all, 0, 0)
-    grad_res_gate_up = mm("td,tje->dje", post_late, dgate_up_two)
+    arrivals = []
+    dproj = ring_sum(lambda k: dot(dcontext_low, pdown_ring[k], 1, 1), arrivals)
     grad_proj_down = jnp.zeros((blk, unit, tcol), F32)
     for k in range(blk):
+        block = after(proj_ring[k], arrivals[min(2 * k // blk, len(arrivals) - 1)])
         grad_proj_down = lax.dynamic_update_index_in_dim(
-            grad_proj_down, dot(proj_ring[k], dcontext_low, 0, 0), ring_index(k), 0
+            grad_proj_down, dot(block, dcontext_low, 0, 0), ring_index(k), 0
         )
     grad_proj_down = grad_proj_down.reshape(hidden, tcol)
-    res_rows = jnp.concatenate([dquery_own, dlatent_kv, result_low], axis=1)
-    res_rows = gather_blk(after(res_rows, dcontext_low))
+    res_rows = jnp.concatenate([dquery_own, dlatent_kv], axis=1)
+    res_rows = gather_blk(after(res_rows, arrivals[0]))
     res_rows = res_rows.reshape(lats, -1)
-    dquery_all, dlkv_all = res_rows[:, :qcols], res_rows[:, qcols : qcols + 2 * kvcols]
-    result_all = res_rows[:, qcols + 2 * kvcols :]
-    grad_res_q = dot(latent_cols, dquery_all, 0, 0)
-    grad_res_kv = dot(latent_cols, dlkv_all, 0, 0) + sum_tp_quarter(
-        mm("kc,tkj->tcj", context_low, dpatch_quad)
-    )
-    grad_res_kv = grad_res_kv.reshape(tcol, 2, kvcols)
-    dlatent_part = dot(dquery_all, res_q, 1, 1) + dot(dlkv_all, rkv_own, 1, 1)
-    gain_latent = jnp.sum(dlatent_part * latent_cols.astype(F32), axis=0) / gain_latent_own
-    dlatent_rows = exchange(dlatent_part.astype(BF).reshape(4 * blk, lsub, tcol), EVERY)
-    dlatent_normed = (
-        jnp.sum(dlatent_rows.reshape(blk, 4, lsub, tcol).astype(F32), axis=1)
-        .transpose(1, 0, 2)
-        .reshape(lsub, text)
-    )
-    latent_pull = jax.vjp(rms_norm, latent_sub, res_gains[1])[1]
-    dlatent_in, _ = latent_pull(dlatent_normed)
-    latents_grad = gather_tp(dlatent_one + dlatent_in).reshape(lat, text)
-    dattn_cols = exchange(dattn_low.reshape(lat, blk, tcol).transpose(1, 0, 2), "blk")
-    grad_res_out = dot(result_all, dattn_cols.reshape(lats, tcol), 0, 0)
-    gain_cols = sum_tp(jnp.stack([gain_context, gain_latent]))
-    dproj, grad_res_down, grad_res_gate_up, grad_proj_down, latents_grad, grad_res_out = (
-        lax.optimization_barrier(
-            (dproj, grad_res_down, grad_res_gate_up, grad_proj_down, latents_grad, grad_res_out)
-        )
+    dquery_all, dlkv_all = res_rows[:, :qcols], res_rows[:, qcols:]
+    dattn_quarter = after(dlatent_one.astype(BF), arrivals[min(1, len(arrivals) - 1)])
+    dattn_cols = share_columns(dattn_quarter.reshape(1, lsub, blk, tcol))[0]
+    grad_res_out = dot(result_all, dattn_cols, 0, 0)
+    dproj, grad_proj_down, grad_res_out, dquery_all, dlkv_all = lax.optimization_barrier(
+        (dproj, grad_proj_down, grad_res_out, dquery_all, dlkv_all)
     )
     dgate, dup = proj_pull(dproj)
     dgate_low, dup_low = dgate.astype(BF), dup.astype(BF)
     dvision_part = dot(dgate_low, gate_own, 1, 1) + dot(dup_low, up_own, 1, 1)
     dvision_sub = sum_every(dvision_part.reshape(4, blk, sub, wide))
+    grad_gate = dot(vision_low, dgate_low, 0, 0).astype(BF).reshape(blk, wcol, unit)
+    grad_up = dot(vision_low, dup_low, 0, 0).astype(BF).reshape(blk, wcol, unit)
+    dvision_sub, grad_gate, grad_up = lax.optimization_barrier((dvision_sub, grad_gate, grad_up))
     dvision_out = gather_tp(dvision_sub).reshape(tok, wide)
-    vision_late = after(vision_low, dvision_sub)
-    grad_gu = jnp.stack([dot(vision_late, dgate_low, 0, 0), dot(vision_late, dup_low, 0, 0)])
-    grad_gu = exchange(grad_gu.astype(BF).reshape(2, blk, wcol, unit).transpose(1, 0, 2, 3), "blk")
-
+    grad_gate = exchange(grad_gate, "blk")
+
+    grad_res_q = dot(latent_cols, dquery_all, 0, 0)
+    grad_res_kv = dot(latent_cols, dlkv_all, 0, 0) + sum_tp_quarter(
+        mm("kc,tkj->tcj", context_low, dpatch_quad)
+    )
+    grad_res_kv = grad_res_kv.reshape(tcol, 2, kvcols)
+    dlatent_part = dot(dquery_all, res_q, 1, 1) + dot(dlkv_all, rkv_own, 1, 1)
+    gain_latent = jnp.sum(dlatent_part * latent_cols.astype(F32), axis=0) / gain_latent_own
+    gain_cols = sum_tp(jnp.stack([gain_context, gain_latent]))
+
+    gain_rows = jnp.stack([gain_post, gain_final]).reshape(2, 4, -1).transpose(1, 0, 2)
+    gain_rows = sum_tp_quarter(after(gain_rows, dvision_out))
     dfc2_low = dvision_out.astype(BF)
     bias_two = jnp.sum(dfc2_low.astype(F32), axis=0)
     (dfc1_pre,) = gelu_pull(dot(dfc2_low, fc2_full, 1, 0))
     dfc1_low = dfc1_pre.astype(BF)
     bias_fc1 = jnp.sum(dfc1_low.astype(F32), axis=0)
-    dfc1_all = gather_blk_later(dfc1_low).reshape(tokens, -1)
     dnormed_two = sum_tp(dot(dfc1_low, fc1_full, 1, 1))
     dhidden_part, gain_two, shift_two = norm_two_pull(dnormed_two)
     dhidden_one = dvision_out + dhidden_part
     dattn_total = dhidden_one.astype(BF)
     bias_one = jnp.sum(dattn_total.astype(F32), axis=0)
     dattn_output = dot(dattn_total, out_full, 1, 0).astype(BF)
-    grad_res_gate_up = with_layout_constraint(
-        grad_res_gate_up, Layout(major_to_minor=(0, 1, 2))
-    )
-    dattn_output, grad_gu, grad_res_gate_up = lax.optimization_barrier(
-        (dattn_output, grad_gu, grad_res_gate_up)
-    )
-    grad_proj_gate_up = grad_gu.transpose(2, 1, 0, 3).reshape(wcol, 2, hidden).astype(F32)
-    cols = after(jnp.stack([attn_input, mlp_input, dfc2_low, dattn_total]), dattn_output)
-    cols = exchange(cols.reshape(4, tok, blk, wcol).transpose(2, 0, 1, 3), "blk")
-
+    dattn_output, grad_gate = lax.optimization_barrier((dattn_output, grad_gate))
     dout_heads = dattn_output.reshape(tok, heads, HEAD_VIS)
     vis_delta = jnp.sum(dout_heads.astype(F32) * vis_result, axis=-1)
     d_high, d_low = halves(vis_delta)
     l_high, l_low = halves(vis_lse.T)
-    dout_all = gather_blk(
+    dout_low = jnp.concatenate(
+        [dattn_output, jnp.concatenate([d_high, d_low, l_high, l_low], axis=1).astype(BF)], axis=1
+    )
+    cols = jnp.stack([attn_input, mlp_input, dfc2_low, dattn_total])
+    cols = lax.dynamic_slice_in_dim(cols, t * sub, sub, 1)
+    cols = cols.reshape(tok, blk, wcol).transpose(1, 0, 2)
+    dout_width = dout_low.shape[1]
+    dlatent_home = sum_tp_quarter(
+        dlatent_part.reshape(blk, 4, lsub, tcol).transpose(1, 0, 2, 3)
+    ).astype(BF)
+    arrived = exchange(
         jnp.concatenate(
-            [dattn_output, jnp.concatenate([d_high, d_low, l_high, l_low], axis=1).astype(BF)],
-            axis=1,
-        )
-    ).reshape(tokens, -1)
+            [
+                jnp.broadcast_to(dout_low[None], (blk,) + dout_low.shape),
+                cols,
+                dlatent_home.reshape(blk, tok, -1),
+            ],
+            axis=2,
+        ),
+        "blk",
+    )
+    dout_all = arrived[:, :, :dout_width].reshape(tokens, -1)
+    cols = arrived[:, :, dout_width : dout_width + wcol].reshape(blk, 4, sub, wcol)
+    cols = gather_tp(cols).transpose(2, 1, 0, 3, 4).reshape(4, tokens, wcol)
+    grad_up = exchange(after(grad_up, dout_all), "blk")
+    dfc1_all = gather_blk_later(after(dfc1_low, dout_all)).reshape(tokens, -1)
+    dlatent_normed = (
+        arrived[:, :, dout_width + wcol :]
+        .reshape(blk, lsub, tcol)
+        .transpose(1, 0, 2)
+        .reshape(lsub, text)
+        .astype(F32)
+    )
+    latent_pull = jax.vjp(rms_norm, latent_sub, res_gains[1])[1]
+    dlatent_in, _ = latent_pull(dlatent_normed)
+    latents_grad = gather_tp(dlatent_one + dlatent_in).reshape(lat, text)
     row_values = dout_all[:, width:].astype(F32).reshape(tokens, 2, 2, heads).sum(axis=2)
     delta_all, lse_all = row_values[:, 0].T, row_values[:, 1].T
     dout_all_heads = dout_all[:, :width].reshape(tokens, heads, HEAD_VIS)
@@ -563,13 +593,11 @@
             dvalue_home.reshape(tok, -1),
         ]
     ).astype(BF)
-    dqkv_low, cols = lax.optimization_barrier((dqkv_low, cols))
+    dqkv_low, grad_up = lax.optimization_barrier((dqkv_low, grad_up))
     bias_qv = jnp.stack(
         [jnp.sum(dqkv_low[0].astype(F32), axis=0), jnp.sum(dqkv_low[2].astype(F32), axis=0)]
     )
-    attn_cols, mlp_cols, dfc2_cols, dattn_vis_cols = (
-        cols[:, j].reshape(tokens, wcol) for j in range(4)
-    )
+    attn_cols, mlp_cols, dfc2_cols, dattn_vis_cols = (cols[j] for j in range(4))
     dqkv_ring = ring_gather(jnp.concatenate(list(dqkv_low), axis=1))
     dqkv_ring = jnp.concatenate(dqkv_ring, axis=0)
     attn_cols_ring = jnp.concatenate(
@@ -583,6 +611,9 @@
     dinput_part, gain_one, shift_one = norm_one_pull(dnormed_one)
     patches_grad = dhidden_one + dinput_part
 
+    grad_proj_gate_up = (
+        jnp.stack([grad_gate, grad_up]).transpose(2, 0, 1, 3).reshape(wcol, 2, hidden).astype(F32)
+    )
     grad_vis_fc2 = dot(dfc2_cols, fc1_low_all, 0, 0).T
     grad_vis_out = dot(dattn_vis_cols, attn_out_all, 0, 0).T
     grad_vis_fc1 = dot(mlp_cols, dfc1_all, 0, 0)

time: 1180 us -> 1120 us (0.949)
  blocking collectives: 43.6 us -> 0 us
  waiting for transfers between devices: 482 us -> 457 us
    all_to_all x2 -> x0, blocking collectives: 43.6 us -> none  [exchange(): return lax.all_to_all(chunks, axis, 0, 0, tiled=True)]
    all_to_all x15 -> x13, waiting for transfers between devices: 152 us -> 113 us  [exchange(): return lax.all_to_all(chunks, axis, 0, 0, tiled=True)]
    ppermute x38 -> x42, waiting for transfers between devices: 79.5 us -> 113 us  [swap_x(): lax.ppermute(value, 'tp', [(i, i ^ 2) for i in range(lax.axis_size('tp'))])]
    ppermute x80 -> x88, waiting for transfers between devices: 242 us -> 219 us  [pass_on(): return lax.ppermute(value, 'blk', route)]
    ppermute x38 -> x42, starting transfers between devices: 43.3 us -> 37.1 us  [swap_x(): lax.ppermute(value, 'tp', [(i, i ^ 2) for i in range(lax.axis_size('tp'))])]
    ppermute x80 -> x88, starting transfers between devices: 120 us -> 116 us  [pass_on(): return lax.ppermute(value, 'blk', route)]
    all_to_all x15 -> x13, starting transfers between devices: 66.2 us -> 68.6 us  [exchange(): return lax.all_to_all(chunks, axis, 0, 0, tiled=True)]
    optimization_barrier x3 -> x1, local copies, waits for them, and re-layouts: 30.2 us -> 28.6 us  [per_device(): lax.optimization_barrier((dpatch_sub, grad_res_down, grad_res_gate_up))]
  transfers between devices with their start and end apart: 175 -> 190, of which waited for: 90 -> 103; matrix products, arithmetic and copies ran while one was open for 24% -> 30% of each run, Pallas kernels for 0% -> 0%
where the time goes in v3:
time: 1120 us; the launch traced here: 1110 us
  waiting for transfers between devices  457 us (41%)
  starting transfers between devices  229 us (20%)
  matrix products  158 us (14%)
  local copies, waits for them, and re-layouts  149 us (13%)
  other arithmetic  82.1 us (7%)
  between operations  35.2 us (3%)
    ppermute x88, waiting for transfers between devices, pass_on(): return lax.ppermute(value, 'blk', route)  219 us
    dot_general x58, matrix products, dot(): lax.dot_general(left, right, (((on_left,), (on_right,)), ((), ())), prefe...  117 us
    ppermute x88, starting transfers between devices, pass_on(): return lax.ppermute(value, 'blk', route)  116 us
    all_to_all x13, waiting for transfers between devices, exchange(): return lax.all_to_all(chunks, axis, 0, 0, tiled=True)  113 us
    ppermute x42, waiting for transfers between devices, swap_x(): lax.ppermute(value, 'tp', [(i, i ^ 2) for i in range(lax.axis_size('tp'))])  113 us
    all_to_all x13, starting transfers between devices, exchange(): return lax.all_to_all(chunks, axis, 0, 0, tiled=True)  68.6 us
    dot_general x18, matrix products, mm(): return jnp.einsum(spec, left, right, preferred_element_type=F32)  40.7 us
    unnamed x427, local copies, waits for them, and re-layouts  38 us
  transfers between devices with their start and end apart: 190, of which 103 were waited for; matrix products, arithmetic and copies ran while one was open for 30% of the time, Pallas kernels for 0%

profile of v3, /device:TPU:0, one launch (start us, length us, event | category | flops | bytes accessed | tf_op | source)
XLA Modules:
  0.0 1111.7 jit_solution(11901230345337936087)
XLA Ops:
  38.9 16.9 %collective-permute-done.6.refs_6_ = bf16[4,144,288]{2,1,0:T(8,128)(2,1)S(1)} collective-permute-done((bf16[4,144,288]{2,1,0:T(8,128)(2,1)S(1)}, bf16[4,144,288]{2,1,0:T(8,128)(2,1)S(1)}, u32[]{:S(2)}, u32[]{:S(2)}) %collective-permute-start.6) | collective-permute-done | bytes 331808 | tf_op jit(solution)/shard_map/ppermute | solution.py:108
  55.8 9.2 collective-permute-start.7
  65.1 4.7 collective-permute-done.3.refs_2_
  70.7 8.3 collective-permute-done.7.refs_5_
  87.8 6.1 reshape.2545
  121.6 7.7 collective-permute-done.12
  134.7 6.7 collective-permute-done.17
  151.2 6.5 all-to-all-start
  157.9 9.0 collective-permute-done.19
  167.9 18.9 %all-to-all-done = bf16[8,144,448]{2,1,0:T(8,128)(2,1)S(1)} async-done(((bf16[8,144,448]{2,1,0:T(8,128)(2,1)}), bf16[8,144,448]{2,1,0:T(8,128)(2,1)S(1)}, u32[]{:S(2)}, u32[]{:S(2)}) %all-to-all-start) | async-done | bytes 1032224 | tf_op jit(solution)/shard_map/all_to_all | solution.py:40
  206.8 13.4 %all-to-all-done.1 = bf16[8,144,448]{2,1,0:T(8,128)(2,1)S(1)} async-done(((bf16[8,144,448]{2,1,0:T(8,128)(2,1)}), bf16[8,144,448]{2,1,0:T(8,128)(2,1)S(1)}, u32[]{:S(2)}, u32[]{:S(2)}) %all-to-all-start.1) | async-done | bytes 1032224 | tf_op jit(solution)/shard_map/all_to_all | solution.py:40
  238.9 9.9 collective-permute-done.30
  259.9 20.7 %collective-permute-done.33 = bf16[1024,448]{0,1:T(8,128)(2,1)} collective-permute-done((bf16[1024,448]{0,1:T(8,128)(2,1)}, bf16[1024,448]{0,1:T(8,128)(2,1)}, u32[]{:S(2)}, u32[]{:S(2)}) %collective-permute-start.33) | collective-permute-done | bytes 917536 | tf_op jit(solution)/shard_map/ppermute | solution.py:108
  289.4 18.2 %all-to-all-done.2 = bf16[8,1,16,512]{3,2,1,0:T(8,128)(2,1)S(1)} async-done(((bf16[8,1,16,512]{3,2,1,0:T(8,128)(2,1)}), bf16[8,1,16,512]{3,2,1,0:T(8,128)(2,1)S(1)}, u32[]{:S(2)}, u32[]{:S(2)}) %all-to-all-start.2) | async-done | bytes 131104 | tf_op jit(solution)/shard_map/all_to_all | solution.py:40
  322.7 12.9 %collective-permute-done.37 = bf16[1024,448]{0,1:T(8,128)(2,1)S(1)} collective-permute-done((bf16[1024,448]{0,1:T(8,128)(2,1)}, bf16[1024,448]{0,1:T(8,128)(2,1)S(1)}, u32[]{:S(2)}, u32[]{:S(2)}) %collective-permute-start.37) | collective-permute-done | bytes 917536 | tf_op jit(solution)/shard_map/ppermute | solution.py:108
  340.5 7.3 collective-permute-done.38
  393.9 6.5 collective-permute-done.47
  411.8 21.5 %all-to-all-done.3 = bf16[32,32,192]{2,1,0:T(8,128)(2,1)S(1)} async-done(((bf16[32,32,192]{2,1,0:T(8,128)(2,1)}), bf16[32,32,192]{2,1,0:T(8,128)(2,1)S(1)}, u32[]{:S(2)}, u32[]{:S(2)}) %all-to-all-start.3) | async-done | bytes 393248 | tf_op jit(solution)/shard_map/all_to_all | solution.py:40
  505.9 6.7 collective-permute-done.79
  549.4 8.2 collective-permute-done.98
  560.5 5.1 collective-permute-done.103
  589.5 5.6 fusion.4
  609.6 6.7 collective-permute-done.117
  654.2 12.8 %fusion.7 = f32[4096,2,512]{2,0,1:T(8,128)} fusion(bf16[512,4096]{1,0:T(8,128)(2,1)} %copy-done.128, bf16[512,1,512]{2,0,1:T(8,128)(2,1)} %get-tuple-element.303, bf16[512,1,512]{2,0,1:T(8,128)(2,1)S(1)} %copy-done.186), kind=kOutput, calls=%fused_computation.23 | convolution fusion | flops 4297064448 | bytes 22020096 | tf_op jit(solution)/shard_map/td,tje->dje/dot_general | solution.py:222
  667.0 5.8 fusion.363
  674.3 6.3 all-to-all-start.5
  684.8 28.6 %copy.755 = f32[4096,2,512]{2,1,0:T(2,128)} copy(f32[4096,2,512]{2,0,1:T(8,128)} %fusion.7) | data formatting | bytes 33554432 | tf_op jit(solution)/shard_map/optimization_barrier | solution.py:456
  717.8 5.9 collective-permute-done.130
  737.8 8.1 collective-permute-done.132
  770.0 5.7 all-to-all-start.6
  788.1 6.1 all-to-all-start.7
  798.0 4.7 collective-permute-done.134
  805.7 5.6 collective-permute-start.135
  817.7 4.8 all-to-all-done.7
  829.0 5.0 collective-permute-done.139
  852.6 11.6 %collective-permute-done.143 = bf16[8,32,1152]{2,1,0:T(8,128)(2,1)S(1)} collective-permute-done((bf16[8,32,1152]{2,1,0:T(8,128)(2,1)S(1)}, bf16[8,32,1152]{2,1,0:T(8,128)(2,1)S(1)}, u32[]{:S(2)}, u32[]{:S(2)}) %collective-permute-start.143) | collective-permute-done | bytes 589856 | tf_op jit(solution)/shard_map/ppermute | solution.py:24
  865.3 7.4 all-to-all-start.8
  909.0 6.1 all-to-all-start.9
  923.8 19.7 %all-to-all-done.9 = bf16[8,144,448]{2,1,0:T(8,128)(2,1)} async-done(((bf16[8,144,448]{2,1,0:T(8,128)(2,1)}), bf16[8,144,448]{2,1,0:T(8,128)(2,1)}, u32[]{:S(2)}, u32[]{:S(2)}) %all-to-all-start.9) | async-done | bytes 1032224 | tf_op jit(solution)/shard_map/all_to_all | solution.py:40
  946.2 4.8 all-to-all-start.10
  953.1 5.2 collective-permute-done.171
  967.7 8.9 all-to-all-done.10
  995.7 8.3 collective-permute-done.152
  1034.0 8.2 collective-permute-done.161
  1049.4 4.9 copy.803
  1054.4 7.0 reshape.2628
  1080.4 6.0 all-to-all-start.12
  1088.6 6.8 all-to-all-done.12
  (1234 shorter events, 635.6 us)
Async XLA Ops:
  7.2 184.7 %all-gather.11.cloned.1.call-start = ((), (), s32[]{:S(2)}) async-start(), calls=%async_computation.13 | async-start | bytes 2985984 | tf_op jit(solution)/shard_map/all_gather | solution.py:81
  8.0 188.0 %all-gather.13.cloned.1.call-start = ((), (), s32[]{:S(2)}) async-start(), calls=%async_computation.14 | async-start | bytes 2985984 | tf_op jit(solution)/shard_map/all_gather | solution.py:81
  9.1 27.4 %collective-permute-start.5 = (bf16[4,144,288]{2,1,0:T(8,128)(2,1)S(1)}, bf16[4,144,288]{2,1,0:T(8,128)(2,1)S(1)}, u32[]{:S(2)}, u32[]{:S(2)}) collective-permute-start(bf16[4,144,288]{2,1,0:T(8,128)(2,1)S(1)} %pad_maximum_fusion.6.refs_0_), channel_id=1, source_target_pairs={{0,8},{8,16},{16,24},{24,28},{28,20},{20,12},{12,4},{4,0},{1,9},{9... | collective-permute-start | bytes 995336 | tf_op jit(solution)/shard_map/ppermute | solution.py:108
  12.2 26.4 %collective-permute-start.2 = (bf16[4,144,288]{2,1,0:T(8,128)(2,1)S(1)}, bf16[4,144,288]{2,1,0:T(8,128)(2,1)S(1)}, u32[]{:S(2)}, u32[]{:S(2)}) collective-permute-start(bf16[4,144,288]{2,1,0:T(8,128)(2,1)S(1)} %pad_maximum_fusion.6.refs_0_), channel_id=1, source_target_pairs={{0,4},{8,0},{16,8},{24,16},{28,24},{20,28},{12,20},{4,12},{1,5},{9... | collective-permute-start | bytes 995336 | tf_op jit(solution)/shard_map/ppermute | solution.py:108
  36.5 19.3 %collective-permute-start.6 = (bf16[4,144,288]{2,1,0:T(8,128)(2,1)S(1)}, bf16[4,144,288]{2,1,0:T(8,128)(2,1)S(1)}, u32[]{:S(2)}, u32[]{:S(2)}) collective-permute-start(bf16[4,144,288]{2,1,0:T(8,128)(2,1)S(1)} %collective-permute-done.5.refs_7_), channel_id=1, source_target_pairs={{0,8},{8,16},{16,24},{24,28},{28,20},{20,12},{12,4},{4,0},{1,9},{9... | collective-permute-start | bytes 995336 | tf_op jit(solution)/shard_map/ppermute | solution.py:108
  38.6 31.1 %collective-permute-start.3 = (bf16[4,144,288]{2,1,0:T(8,128)(2,1)S(1)}, bf16[4,144,288]{2,1,0:T(8,128)(2,1)S(1)}, u32[]{:S(2)}, u32[]{:S(2)}) collective-permute-start(bf16[4,144,288]{2,1,0:T(8,128)(2,1)S(1)} %collective-permute-done.2.refs_1_), channel_id=1, source_target_pairs={{0,4},{8,0},{16,8},{24,16},{28,24},{20,28},{12,20},{4,12},{1,5},{9... | collective-permute-start | bytes 995336 | tf_op jit(solution)/shard_map/ppermute | solution.py:108
  55.8 23.2 %collective-permute-start.7 = (bf16[4,144,288]{2,1,0:T(8,128)(2,1)S(1)}, bf16[4,144,288]{2,1,0:T(8,128)(2,1)S(1)}, u32[]{:S(2)}, u32[]{:S(2)}) collective-permute-start(bf16[4,144,288]{2,1,0:T(8,128)(2,1)S(1)} %collective-permute-done.6.refs_6_), channel_id=1, source_target_pairs={{0,8},{8,16},{16,24},{24,28},{28,20},{20,12},{12,4},{4,0},{1,9},{9... | collective-permute-start | bytes 995336 | tf_op jit(solution)/shard_map/ppermute | solution.py:108
  79.7 19.3 %collective-permute-start.8 = (bf16[2,144,288]{2,1,0:T(8,128)(2,1)}, bf16[2,144,288]{2,1,0:T(8,128)(2,1)}, u32[]{:S(2)}, u32[]{:S(2)}) collective-permute-start(bf16[2,144,288]{2,1,0:T(8,128)(2,1)} %slice.813), channel_id=1, source_target_pairs={{0,8},{8,16},{16,24},{24,28},{28,20},{20,12},{12,4},{4,0},{1,9},{9... | collective-permute-start | bytes 497672 | tf_op jit(solution)/shard_map/ppermute | solution.py:108
  151.2 35.6 %all-to-all-start = ((bf16[8,144,448]{2,1,0:T(8,128)(2,1)}), bf16[8,144,448]{2,1,0:T(8,128)(2,1)S(1)}, u32[]{:S(2)}, u32[]{:S(2)}) async-start(bf16[8,144,448]{2,1,0:T(8,128)(2,1)} %get-tuple-element.63), calls=%async_computation | async-start | bytes 2359296 | tf_op jit(solution)/shard_map/all_to_all | solution.py:40
  187.9 32.4 %all-to-all-start.1 = ((bf16[8,144,448]{2,1,0:T(8,128)(2,1)}), bf16[8,144,448]{2,1,0:T(8,128)(2,1)S(1)}, u32[]{:S(2)}, u32[]{:S(2)}) async-start(bf16[8,144,448]{2,1,0:T(8,128)(2,1)} %get-tuple-element.65), calls=%async_computation.1 | async-start | bytes 2359296 | tf_op jit(solution)/shard_map/all_to_all | solution.py:40
  257.7 22.9 %collective-permute-start.33 = (bf16[1024,448]{0,1:T(8,128)(2,1)}, bf16[1024,448]{0,1:T(8,128)(2,1)}, u32[]{:S(2)}, u32[]{:S(2)}) collective-permute-start(bf16[1024,448]{0,1:T(8,128)(2,1)} %get-tuple-element.78), channel_id=1, source_target_pairs={{0,8},{8,16},{16,24},{24,28},{28,20},{20,12},{12,4},{4,0},{1,9},{9... | collective-permute-start | bytes 2752520 | tf_op jit(solution)/shard_map/ppermute | solution.py:108
  259.4 22.7 %collective-permute-start.32 = (bf16[1024,448]{0,1:T(8,128)(2,1)}, bf16[1024,448]{0,1:T(8,128)(2,1)}, u32[]{:S(2)}, u32[]{:S(2)}) collective-permute-start(bf16[1024,448]{0,1:T(8,128)(2,1)} %get-tuple-element.78), channel_id=1, source_target_pairs={{0,4},{8,0},{16,8},{24,16},{28,24},{20,28},{12,20},{4,12},{1,5},{9... | collective-permute-start | bytes 2752520 | tf_op jit(solution)/shard_map/ppermute | solution.py:108
  280.6 32.1 %collective-permute-start.35 = (bf16[1024,448]{0,1:T(8,128)(2,1)}, bf16[1024,448]{0,1:T(8,128)(2,1)}, u32[]{:S(2)}, u32[]{:S(2)}) collective-permute-start(bf16[1024,448]{0,1:T(8,128)(2,1)} %collective-permute-done.33), channel_id=1, source_target_pairs={{0,8},{8,16},{16,24},{24,28},{28,20},{20,12},{12,4},{4,0},{1,9},{9... | collective-permute-start | bytes 2752520 | tf_op jit(solution)/shard_map/ppermute | solution.py:108
  282.1 31.1 %collective-permute-start.34 = (bf16[1024,448]{0,1:T(8,128)(2,1)}, bf16[1024,448]{0,1:T(8,128)(2,1)}, u32[]{:S(2)}, u32[]{:S(2)}) collective-permute-start(bf16[1024,448]{0,1:T(8,128)(2,1)} %collective-permute-done.32), channel_id=1, source_target_pairs={{0,4},{8,0},{16,8},{24,16},{28,24},{20,28},{12,20},{4,12},{1,5},{9... | collective-permute-start | bytes 2752520 | tf_op jit(solution)/shard_map/ppermute | solution.py:108
  283.5 24.1 %all-to-all-start.2 = ((bf16[8,1,16,512]{3,2,1,0:T(8,128)(2,1)}), bf16[8,1,16,512]{3,2,1,0:T(8,128)(2,1)S(1)}, u32[]{:S(2)}, u32[]{:S(2)}) async-start(bf16[8,1,16,512]{3,2,1,0:T(8,128)(2,1)} %bitcast.1154), calls=%async_computation.2 | async-start | bytes 262144 | tf_op jit(solution)/shard_map/all_to_all | solution.py:40
  288.0 148.5 %all-gather.15.cloned.1.call-start = ((), (), s32[]{:S(2)}) async-start(), calls=%async_computation.15 | async-start | bytes 3538944 | tf_op jit(solution)/shard_map/all_gather | solution.py:81
  288.1 19.8 %collective-permute-start = (bf16[512,192]{0,1:T(8,128)(2,1)S(1)}, bf16[512,192]{0,1:T(8,128)(2,1)S(1)}, u32[]{:S(2)}, u32[]{:S(2)}) collective-permute-start(bf16[512,192]{0,1:T(8,128)(2,1)S(1)} %bitcast.1257), channel_id=1, source_target_pairs={{0,2},{1,3},{2,0},{3,1},{4,6},{5,7},{6,4},{7,5},{8,10},{9,11},{10,... | collective-permute-start | bytes 589832 | tf_op jit(solution)/shard_map/ppermute | solution.py:24
  307.9 43.2 %collective-permute-start.1 = (bf16[2,512,192]{1,2,0:T(8,128)(2,1)S(1)}, bf16[2,512,192]{1,2,0:T(8,128)(2,1)S(1)}, u32[]{:S(2)}, u32[]{:S(2)}) collective-permute-start(bf16[2,512,192]{1,2,0:T(8,128)(2,1)S(1)} %maximum_select_fusion.39), channel_id=1, source_target_pairs={{0,1},{1,0},{2,3},{3,2},{4,5},{5,4},{6,7},{7,6},{8,9},{9,8},{10,11... | collective-permute-start | bytes 1179656 | tf_op jit(solution)/shard_map/ppermute | solution.py:20
  312.6 39.6 %collective-permute-start.43 = (bf16[2,8,1,16,512]{4,3,1,2,0:T(8,128)(2,1)S(1)}, bf16[2,8,1,16,512]{4,3,1,2,0:T(8,128)(2,1)S(1)}, u32[]{:S(2)}, u32[]{:S(2)}) collective-permute-start(bf16[2,8,1,16,512]{4,3,1,2,0:T(8,128)(2,1)S(1)} %maximum_select_fusion.43), channel_id=1, source_target_pairs={{0,1},{1,0},{2,3},{3,2},{4,5},{5,4},{6,7},{7,6},{8,9},{9,8},{10,11... | collective-permute-start | bytes 786440 | tf_op jit(solution)/shard_map/ppermute | solution.py:20
  312.6 23.0 %collective-permute-start.37 = (bf16[1024,448]{0,1:T(8,128)(2,1)}, bf16[1024,448]{0,1:T(8,128)(2,1)S(1)}, u32[]{:S(2)}, u32[]{:S(2)}) collective-permute-start(bf16[1024,448]{0,1:T(8,128)(2,1)} %collective-permute-done.35), channel_id=1, source_target_pairs={{0,8},{8,16},{16,24},{24,28},{28,20},{20,12},{12,4},{4,0},{1,9},{9... | collective-permute-start | bytes 2752520 | tf_op jit(solution)/shard_map/ppermute | solution.py:108
  313.2 23.0 %collective-permute-start.36 = (bf16[1024,448]{0,1:T(8,128)(2,1)}, bf16[1024,448]{0,1:T(8,128)(2,1)S(1)}, u32[]{:S(2)}, u32[]{:S(2)}) collective-permute-start(bf16[1024,448]{0,1:T(8,128)(2,1)} %collective-permute-done.34), channel_id=1, source_target_pairs={{0,4},{8,0},{16,8},{24,16},{28,24},{20,28},{12,20},{4,12},{1,5},{9... | collective-permute-start | bytes 2752520 | tf_op jit(solution)/shard_map/ppermute | solution.py:108
  406.9 26.4 %all-to-all-start.3 = ((bf16[32,32,192]{2,1,0:T(8,128)(2,1)}), bf16[32,32,192]{2,1,0:T(8,128)(2,1)S(1)}, u32[]{:S(2)}, u32[]{:S(2)}) async-start(bf16[32,32,192]{2,1,0:T(8,128)(2,1)} %bitcast.101), calls=%async_computation.3 | async-start | bytes 1048576 | tf_op jit(solution)/shard_map/all_to_all | solution.py:40
  410.6 228.7 %all-gather.17.cloned.1.call-start = ((), (), s32[]{:S(2)}) async-start(), calls=%async_computation.16 | async-start | bytes 4257792 | tf_op jit(solution)/shard_map/all_gather | solution.py:81
  496.6 32.5 %collective-permute-start.73 = (bf16[16,4096]{1,0:T(8,128)(2,1)}, bf16[16,4096]{1,0:T(8,128)(2,1)}, u32[]{:S(2)}, u32[]{:S(2)}) collective-permute-start(bf16[16,4096]{1,0:T(8,128)(2,1)} %fusion.263), channel_id=1, source_target_pairs={{0,2},{1,3},{2,0},{3,1},{4,6},{5,7},{6,4},{7,5},{8,10},{9,11},{10,... | collective-permute-start | bytes 393224 | tf_op jit(solution)/shard_map/ppermute | solution.py:24
  545.9 22.5 %collective-permute-start.96 = (bf16[32,4096]{1,0:T(8,128)(2,1)S(1)}, bf16[32,4096]{1,0:T(8,128)(2,1)S(1)}, u32[]{:S(2)}, u32[]{:S(2)}) collective-permute-start(bf16[32,4096]{1,0:T(8,128)(2,1)S(1)} %constant_dynamic-update-slice_fusion.15), channel_id=1, source_target_pairs={{0,2},{1,3},{2,0},{3,1},{4,6},{5,7},{6,4},{7,5},{8,10},{9,11},{10,... | collective-permute-start | bytes 786440 | tf_op jit(solution)/shard_map/ppermute | solution.py:24
  547.1 22.5 %collective-permute-start.93 = (bf16[2,16,4096]{2,1,0:T(8,128)(2,1)S(1)}, bf16[2,16,4096]{2,1,0:T(8,128)(2,1)S(1)}, u32[]{:S(2)}, u32[]{:S(2)}) collective-permute-start(bf16[2,16,4096]{2,1,0:T(8,128)(2,1)S(1)} %maximum_select_fusion.46), channel_id=1, source_target_pairs={{0,1},{1,0},{2,3},{3,2},{4,5},{5,4},{6,7},{7,6},{8,9},{9,8},{10,11... | collective-permute-start | bytes 786440 | tf_op jit(solution)/shard_map/ppermute | solution.py:20
  599.5 33.9 %collective-permute-start.111 = (bf16[16,4096]{1,0:T(8,128)(2,1)S(1)}, bf16[16,4096]{1,0:T(8,128)(2,1)S(1)}, u32[]{:S(2)}, u32[]{:S(2)}) collective-permute-start(bf16[16,4096]{1,0:T(8,128)(2,1)S(1)} %fusion.265), channel_id=1, source_target_pairs={{0,2},{1,3},{2,0},{3,1},{4,6},{5,7},{6,4},{7,5},{8,10},{9,11},{10,... | collective-permute-start | bytes 393224 | tf_op jit(solution)/shard_map/ppermute | solution.py:24
  650.6 22.3 %all-to-all-start.4 = ((bf16[32,32,192]{2,1,0:T(8,128)(2,1)}), bf16[32,32,192]{2,1,0:T(8,128)(2,1)S(1)}, u32[]{:S(2)}, u32[]{:S(2)}) async-start(bf16[32,32,192]{2,1,0:T(8,128)(2,1)} %bitcast.259), calls=%async_computation.4 | async-start | bytes 1048576 | tf_op jit(solution)/shard_map/all_to_all | solution.py:40
  674.3 39.1 %all-to-all-start.5 = ((bf16[8,5,32,192]{3,2,1,0:T(8,128)(2,1)}), bf16[8,5,32,192]{3,2,1,0:T(8,128)(2,1)S(1)}, u32[]{:S(2)}, u32[]{:S(2)}) async-start(bf16[8,5,32,192]{3,2,1,0:T(8,128)(2,1)} %broadcast_in_dim.161), calls=%async_computation.5 | async-start | bytes 1310720 | tf_op jit(solution)/shard_map/all_to_all | solution.py:40
  725.2 116.0 %collective-permute-start.154 = (bf16[2,2,1024]{2,1,0:T(2,128)(2,1)}, bf16[2,2,1024]{2,1,0:T(2,128)(2,1)}, u32[]{:S(2)}, u32[]{:S(2)}) collective-permute-start(bf16[2,2,1024]{2,1,0:T(2,128)(2,1)} %fusion.303), channel_id=1, source_target_pairs={{0,1},{1,0},{2,3},{3,2},{4,5},{5,4},{6,7},{7,6},{8,9},{9,8},{10,11... | collective-permute-start | bytes 24584 | tf_op jit(solution)/shard_map/ppermute | solution.py:20
  725.7 120.9 %collective-permute-start.90 = (f32[16,4096]{1,0:T(8,128)}, f32[16,4096]{1,0:T(8,128)}, u32[]{:S(2)}, u32[]{:S(2)}) collective-permute-start(f32[16,4096]{1,0:T(8,128)} %get-tuple-element.338), channel_id=1, source_target_pairs={{0,2},{1,3},{2,0},{3,1},{4,6},{5,7},{6,4},{7,5},{8,10},{9,11},{10,... | collective-permute-start | bytes 786440 | tf_op jit(solution)/shard_map/ppermute | solution.py:24
  747.8 21.1 %collective-permute-start.133 = (bf16[1024,448]{0,1:T(8,128)(2,1)S(1)}, bf16[1024,448]{0,1:T(8,128)(2,1)S(1)}, u32[]{:S(2)}, u32[]{:S(2)}) collective-permute-start(bf16[1024,448]{0,1:T(8,128)(2,1)S(1)} %add_convert_fusion.5), channel_id=1, source_target_pairs={{0,8},{8,16},{16,24},{24,28},{28,20},{20,12},{12,4},{4,0},{1,9},{9... | collective-permute-start | bytes 2752520 | tf_op jit(solution)/shard_map/ppermute | solution.py:108
  752.2 28.8 %collective-permute-start.137 = (bf16[1024,448]{0,1:T(8,128)(2,1)}, bf16[1024,448]{0,1:T(8,128)(2,1)}, u32[]{:S(2)}, u32[]{:S(2)}) collective-permute-start(bf16[1024,448]{0,1:T(8,128)(2,1)} %add_convert_fusion.2), channel_id=1, source_target_pairs={{0,4},{8,0},{16,8},{24,16},{28,24},{20,28},{12,20},{4,12},{1,5},{9... | collective-permute-start | bytes 2752520 | tf_op jit(solution)/shard_map/ppermute | solution.py:108
  770.0 17.3 %all-to-all-start.6 = ((bf16[8,1,16,512]{3,2,1,0:T(8,128)(2,1)}), bf16[8,1,16,512]{3,2,1,0:T(8,128)(2,1)S(1)}, u32[]{:S(2)}, u32[]{:S(2)}) async-start(bf16[8,1,16,512]{3,2,1,0:T(8,128)(2,1)} %bitcast.1153), calls=%async_computation.6 | async-start | bytes 262144 | tf_op jit(solution)/shard_map/all_to_all | solution.py:40
  779.0 23.7 %collective-permute-start.134 = (bf16[1024,448]{0,1:T(8,128)(2,1)}, bf16[1024,448]{0,1:T(8,128)(2,1)}, u32[]{:S(2)}, u32[]{:S(2)}) collective-permute-start(bf16[1024,448]{0,1:T(8,128)(2,1)} %add_convert_fusion.4), channel_id=1, source_target_pairs={{0,8},{8,16},{16,24},{24,28},{28,20},{20,12},{12,4},{4,0},{1,9},{9... | collective-permute-start | bytes 2752520 | tf_op jit(solution)/shard_map/ppermute | solution.py:108
  784.0 27.3 %collective-permute-start.138 = (bf16[1024,448]{0,1:T(8,128)(2,1)}, bf16[1024,448]{0,1:T(8,128)(2,1)}, u32[]{:S(2)}, u32[]{:S(2)}) collective-permute-start(bf16[1024,448]{0,1:T(8,128)(2,1)} %add_convert_fusion.1), channel_id=1, source_target_pairs={{0,4},{8,0},{16,8},{24,16},{28,24},{20,28},{12,20},{4,12},{1,5},{9... | collective-permute-start | bytes 2752520 | tf_op jit(solution)/shard_map/ppermute | solution.py:108
  788.1 34.4 %all-to-all-start.7 = ((bf16[8,64,576]{2,1,0:T(8,128)(2,1)}), bf16[8,64,576]{2,1,0:T(8,128)(2,1)}, u32[]{:S(2)}, u32[]{:S(2)}) async-start(bf16[8,64,576]{2,1,0:T(8,128)(2,1)} %broadcast_in_dim.171), calls=%async_computation.7 | async-start | bytes 1310720 | tf_op jit(solution)/shard_map/all_to_all | solution.py:40
  805.7 23.3 %collective-permute-start.135 = (bf16[1024,448]{0,1:T(8,128)(2,1)}, bf16[1024,448]{0,1:T(8,128)(2,1)}, u32[]{:S(2)}, u32[]{:S(2)}) collective-permute-start(bf16[1024,448]{0,1:T(8,128)(2,1)} %add_convert_fusion.3), channel_id=1, source_target_pairs={{0,8},{8,16},{16,24},{24,28},{28,20},{20,12},{12,4},{4,0},{1,9},{9... | collective-permute-start | bytes 2752520 | tf_op jit(solution)/shard_map/ppermute | solution.py:108
  814.2 19.7 %collective-permute-start.139 = (bf16[1024,448]{0,1:T(8,128)(2,1)}, bf16[1024,448]{0,1:T(8,128)(2,1)}, u32[]{:S(2)}, u32[]{:S(2)}) collective-permute-start(bf16[1024,448]{0,1:T(8,128)(2,1)} %add_convert_fusion), channel_id=1, source_target_pairs={{0,4},{8,0},{16,8},{24,16},{28,24},{20,28},{12,20},{4,12},{1,5},{9... | collective-permute-start | bytes 2752520 | tf_op jit(solution)/shard_map/ppermute | solution.py:108
  865.3 23.2 %all-to-all-start.8 = ((bf16[8,32,1152]{2,1,0:T(8,128)(2,1)}), bf16[8,32,1152]{2,1,0:T(8,128)(2,1)}, u32[]{:S(2)}, u32[]{:S(2)}) async-start(bf16[8,32,1152]{2,1,0:T(8,128)(2,1)} %fusion.43), calls=%async_computation.8 | async-start | bytes 1179648 | tf_op jit(solution)/shard_map/all_to_all | solution.py:40
  909.0 34.5 %all-to-all-start.9 = ((bf16[8,144,448]{2,1,0:T(8,128)(2,1)}), bf16[8,144,448]{2,1,0:T(8,128)(2,1)}, u32[]{:S(2)}, u32[]{:S(2)}) async-start(bf16[8,144,448]{2,1,0:T(8,128)(2,1)} %bitcast.1203), calls=%async_computation.9 | async-start | bytes 2359296 | tf_op jit(solution)/shard_map/all_to_all | solution.py:40
  946.2 30.3 %all-to-all-start.10 = ((bf16[8,128,512]{2,1,0:T(8,128)(2,1)}), bf16[8,128,512]{2,1,0:T(8,128)(2,1)}, u32[]{:S(2)}, u32[]{:S(2)}) async-start(bf16[8,128,512]{2,1,0:T(8,128)(2,1)} %pad_maximum_fusion.2), calls=%async_computation.10 | async-start | bytes 2097152 | tf_op jit(solution)/shard_map/all_to_all | solution.py:40
  977.9 41.4 %all-to-all-start.11 = ((bf16[8,144,448]{2,1,0:T(8,128)(2,1)}), bf16[8,144,448]{2,1,0:T(8,128)(2,1)}, u32[]{:S(2)}, u32[]{:S(2)}) async-start(bf16[8,144,448]{2,1,0:T(8,128)(2,1)} %bitcast.1202), calls=%async_computation.11 | async-start | bytes 2359296 | tf_op jit(solution)/shard_map/all_to_all | solution.py:40
  982.2 119.3 %all-gather.19.cloned.1.call-start = ((), (), s32[]{:S(2)}) async-start(), calls=%async_computation.17 | async-start | bytes 2488320 | tf_op jit(solution)/shard_map/all_gather | solution.py:81
  985.5 20.9 %collective-permute-start.158 = (bf16[8,4,32,144]{3,2,1,0:T(8,128)(2,1)}, bf16[8,4,32,144]{3,2,1,0:T(8,128)(2,1)}, u32[]{:S(2)}, u32[]{:S(2)}) collective-permute-start(bf16[8,4,32,144]{3,2,1,0:T(8,128)(2,1)} %bitcast.371), channel_id=1, source_target_pairs={{0,2},{1,3},{2,0},{3,1},{4,6},{5,7},{6,4},{7,5},{8,10},{9,11},{10,... | collective-permute-start | bytes 884744 | tf_op jit(solution)/shard_map/ppermute | solution.py:24
  1022.8 42.7 %collective-permute-start.150 = (f32[128,1152]{1,0:T(8,128)S(1)}, f32[128,1152]{1,0:T(8,128)S(1)}, u32[]{:S(2)}, u32[]{:S(2)}) collective-permute-start(f32[128,1152]{1,0:T(8,128)S(1)} %convolution_add_fusion.2), channel_id=1, source_target_pairs={{0,1},{1,0},{2,3},{3,2},{4,5},{5,4},{6,7},{7,6},{8,9},{9,8},{10,11... | collective-permute-start | bytes 1769480 | tf_op jit(solution)/shard_map/ppermute | solution.py:20
  1042.1 19.3 %collective-permute-start.162 = (bf16[128,864]{0,1:T(8,128)(2,1)S(1)}, bf16[128,864]{0,1:T(8,128)(2,1)S(1)}, u32[]{:S(2)}, u32[]{:S(2)}) collective-permute-start(bf16[128,864]{0,1:T(8,128)(2,1)S(1)} %collective-permute-done.161), channel_id=1, source_target_pairs={{0,4},{8,0},{16,8},{24,16},{28,24},{20,28},{12,20},{4,12},{1,5},{9... | collective-permute-start | bytes 663560 | tf_op jit(solution)/shard_map/ppermute | solution.py:108
  1044.6 17.0 %collective-permute-start.165 = (bf16[128,864]{0,1:T(8,128)(2,1)S(1)}, bf16[128,864]{0,1:T(8,128)(2,1)S(1)}, u32[]{:S(2)}, u32[]{:S(2)}) collective-permute-start(bf16[128,864]{0,1:T(8,128)(2,1)S(1)} %collective-permute-done.164), channel_id=1, source_target_pairs={{0,8},{8,16},{16,24},{24,28},{28,20},{20,12},{12,4},{4,0},{1,9},{9... | collective-permute-start | bytes 663560 | tf_op jit(solution)/shard_map/ppermute | solution.py:108
  (334 other events, 3421.3 us)
Sparse Core Ops, SparseCore 0:
  10.2 67.1 all-gather.10
  79.6 63.5 all-gather.12
  357.4 74.3 all-gather.14
  541.0 75.9 all-gather.16
  986.2 68.7 all-gather.18

commit v4 on v3

--- a/solution.py
+++ b/solution.py
@@ -2,7 +2,6 @@
 import jax.numpy as jnp
 from jax import lax
 from jax.experimental import pallas as pl
-from jax.experimental.layout import Layout, with_layout_constraint
 from jax.experimental.pallas import tpu as pltpu
 from jax.sharding import PartitionSpec as P
 
@@ -145,7 +144,11 @@
 
 def place_blocks(blocks):
     count = len(blocks)
-    places = jnp.stack([ring_index(k) for k in range(count)])
+    order = ring_order()
+    table = [[order[(order.index(i) + k) % count] for k in range(count)] for i in range(count)]
+    places = lax.dynamic_index_in_dim(
+        jnp.array(table, jnp.int32), lax.axis_index("blk"), 0, False
+    )
 
     def kernel(places_ref, *refs):
         for k in range(count):
@@ -238,6 +241,36 @@
     rows = span_order[:, None] * tok_rows + jnp.arange(tok_rows, dtype=jnp.int32)[None, :]
     stream = rows.reshape(-1)
     return jnp.sum((stream[:, None] >= bounds[None, :]).astype(jnp.int32), axis=1)
+
+
+def wide_gradient(left, gate, up):
+    rows, wide = left.shape
+    cols = gate.shape[1]
+    tile = 512
+
+    def kernel(left_ref, gate_ref, up_ref, out_ref):
+        part = left_ref[...]
+        out_ref[:, 0, :] = dot(part, gate_ref[...], 0, 0)
+        out_ref[:, 1, :] = dot(part, up_ref[...], 0, 0)
+
+    return pl.pallas_call(
+        kernel,
+        grid=(wide // tile,),
+        out_shape=jax.ShapeDtypeStruct((wide, 2, cols), F32),
+        in_specs=[
+            pl.BlockSpec((rows, tile), lambda i: (0, i)),
+            pl.BlockSpec((rows, cols), lambda i: (0, 0)),
+            pl.BlockSpec((rows, cols), lambda i: (0, 0)),
+        ],
+        out_specs=pl.BlockSpec((tile, 2, cols), lambda i: (i, 0, 0)),
+        compiler_params=pltpu.CompilerParams(vmem_limit_bytes=40 * 2**20),
+        cost_estimate=pl.CostEstimate(
+            flops=4 * rows * wide * cols,
+            bytes_accessed=2 * rows * (wide + 2 * cols) + 8 * wide * cols,
+            transcendentals=0,
+        ),
+        name="wide_gradient",
+    )(left, gate, up)
 
 
 def per_device(
@@ -280,9 +313,13 @@
     attn_shard = jnp.concatenate([vis_qkv.transpose(1, 0, 2), vis_out.T[None]], axis=0)
     attn_ring = ring_gather(attn_shard)
     attn_full = place_blocks(attn_ring)
+    gu_chunks = proj_gate_up.reshape(wcol, 2, blk, unit).transpose(2, 1, 0, 3)
+    gate_chunks, up_chunks = gu_chunks[:, 0], gu_chunks[:, 1]
+    attn_full, gate_chunks, up_chunks = lax.optimization_barrier(
+        (attn_full, gate_chunks, up_chunks)
+    )
     attn_full = attn_full.transpose(1, 0, 2, 3).reshape(4, wide, -1)
     qkv_full, out_full = attn_full[:3], attn_full[3]
-    gu_chunks = proj_gate_up.reshape(wcol, 2, blk, unit).transpose(2, 1, 0, 3)
     fc1_full = gather_blk_later(vis_fc1).reshape(wide, -1)
     fc2_full = gather_blk_later(vis_fc2.T).reshape(wide, -1)
     rkv_own = res_kv.reshape(tcol, 2 * kvcols)
@@ -318,8 +355,8 @@
     vis_result = (weighted / weight_sum[..., None]).transpose(1, 0, 2)
     attn_output = vis_result.astype(BF).reshape(tok, -1)
 
-    gate_own = exchange(after(gu_chunks[:, 0], kv_all), "blk").reshape(wide, unit)
-    up_own = exchange(after(gu_chunks[:, 1], gate_own), "blk").reshape(wide, unit)
+    gate_own = exchange(after(gate_chunks, kv_all), "blk").reshape(wide, unit)
+    up_own = exchange(after(up_chunks, gate_own), "blk").reshape(wide, unit)
 
     hidden_one = inputs + sum_tp(dot(attn_output, out_full, 1, 1)) + vis_out_bias[0]
     hidden_one, gate_own = lax.optimization_barrier((hidden_one, gate_own))
@@ -434,7 +471,7 @@
 
     mlp_late, post_late = after(mlp_low, dattn_low), after(post_all, dattn_low)
     grad_res_down = dot(mlp_late, dmlp_all, 0, 0)
-    grad_res_gate_up = mm("td,tje->dje", post_late, dgate_up_two)
+    grad_res_gate_up = wide_gradient(post_late, dgate_up_two[:, 0], dgate_up_two[:, 1])
     dresult = dot(dattn_low, rout_full, 1, 0).astype(BF)
     dresult_heads = dresult.reshape(lat, group, RES_HEAD)
     res_delta = jnp.sum(dresult_heads.astype(F32) * res_result, axis=-1).T
@@ -453,12 +490,7 @@
         .astype(F32),
         axis=0,
     )
-    dpatch_sub, grad_res_down, grad_res_gate_up = lax.optimization_barrier(
-        (dpatch_sub, grad_res_down, grad_res_gate_up)
-    )
-    grad_res_gate_up = with_layout_constraint(
-        grad_res_gate_up, Layout(major_to_minor=(0, 1, 2))
-    )
+    dpatch_sub, grad_res_gate_up = lax.optimization_barrier((dpatch_sub, grad_res_gate_up))
     along = jnp.sum(dpatch_sub * patch_kv.astype(F32), axis=(0, 2)) / text
     a_high, a_low = halves(along)
     s_high, s_low = halves(scale_sub)
@@ -466,7 +498,7 @@
         jnp.stack([a_high, a_low, s_high, s_low], axis=1), ((0, 0), (0, 2 * kvcols - 4))
     )
     dpatch_rows = gather_blk(jnp.concatenate([dpatch_sub, row_stats[None]], axis=0).astype(BF))
-    dpatch_rows, grad_res_gate_up = lax.optimization_barrier((dpatch_rows, grad_res_gate_up))
+    dpatch_rows, grad_res_down = lax.optimization_barrier((dpatch_rows, grad_res_down))
     dpatch_rows = dpatch_rows.transpose(1, 0, 2, 3).reshape(5, quarter, 2 * kvcols)
     dpatch_quad = dpatch_rows[:4]
     along_rows = dpatch_rows[4, :, 0].astype(F32) + dpatch_rows[4, :, 1].astype(F32)

time: 1120 us -> 1090 us (0.973)
  local copies, waits for them, and re-layouts: 149 us -> 113 us
  starting transfers between devices: 229 us -> 246 us
  matrix products: 158 us -> 143 us
    optimization_barrier x1 -> x0, local copies, waits for them, and re-layouts: 28.6 us -> none  [per_device(): lax.optimization_barrier((dpatch_sub, grad_res_down, grad_res_gate_up))]
    dot_general x18 -> x17, matrix products: 40.7 us -> 25.1 us  [mm(): return jnp.einsum(spec, left, right, preferred_element_type=F32)]
    unnamed x427 -> x433, local copies, waits for them, and re-layouts: 38 us -> 38.9 us
  transfers between devices with their start and end apart: 190 -> 190, of which waited for: 103 -> 106; matrix products, arithmetic and copies ran while one was open for 30% -> 25% of each run, Pallas kernels for 0% -> 1%
where the time goes in v4:
time: 1090 us; the launch traced here: 1080 us
  waiting for transfers between devices  452 us (41%)
  starting transfers between devices  246 us (23%)
  matrix products  143 us (13%)
  local copies, waits for them, and re-layouts  113 us (10%)
  other arithmetic  76.9 us (7%)
  between operations  35.8 us (3%)
  Pallas kernels  11.1 us (1%)
    ppermute x88, waiting for transfers between devices, pass_on(): return lax.ppermute(value, 'blk', route)  212 us
    all_to_all x13, waiting for transfers between devices, exchange(): return lax.all_to_all(chunks, axis, 0, 0, tiled=True)  122 us
    ppermute x88, starting transfers between devices, pass_on(): return lax.ppermute(value, 'blk', route)  118 us
    dot_general x58, matrix products, dot(): lax.dot_general(left, right, (((on_left,), (on_right,)), ((), ())), prefe...  118 us
    ppermute x42, waiting for transfers between devices, swap_x(): lax.ppermute(value, 'tp', [(i, i ^ 2) for i in range(lax.axis_size('tp'))])  108 us
    all_to_all x13, starting transfers between devices, exchange(): return lax.all_to_all(chunks, axis, 0, 0, tiled=True)  74.4 us
    ppermute x42, starting transfers between devices, swap_x(): lax.ppermute(value, 'tp', [(i, i ^ 2) for i in range(lax.axis_size('tp'))])  44.3 us
    unnamed x433, local copies, waits for them, and re-layouts  38.9 us
  transfers between devices with their start and end apart: 190, of which 106 were waited for; matrix products, arithmetic and copies ran while one was open for 25% of the time, Pallas kernels for 1%

profile of v4, /device:TPU:0, one launch (start us, length us, event | category | flops | bytes accessed | tf_op | source)
XLA Modules:
  0.0 1078.5 jit_solution(6012315549210513032)
XLA Ops:
  40.3 16.9 %collective-permute-done.6.refs_6_ = bf16[4,144,288]{2,1,0:T(8,128)(2,1)S(1)} collective-permute-done((bf16[4,144,288]{2,1,0:T(8,128)(2,1)S(1)}, bf16[4,144,288]{2,1,0:T(8,128)(2,1)S(1)}, u32[]{:S(2)}, u32[]{:S(2)}) %collective-permute-start.6) | collective-permute-done | bytes 331808 | tf_op jit(solution)/shard_map/ppermute | solution.py:107
  57.2 9.8 collective-permute-start.7
  67.0 4.5 collective-permute-done.3.refs_2_
  72.1 6.1 reshape.2543
  98.8 6.3 collective-permute-done.10
  121.0 7.6 collective-permute-done.17
  135.4 14.8 %all-to-all-start = ((bf16[8,144,448]{2,1,0:T(8,128)(2,1)}), bf16[8,144,448]{2,1,0:T(8,128)(2,1)S(1)}, u32[]{:S(2)}, u32[]{:S(2)}) async-start(bf16[8,144,448]{2,1,0:T(8,128)(2,1)} %get-tuple-element.67), calls=%async_computation | async-start | bytes 2359296 | tf_op jit(solution)/shard_map/all_to_all | solution.py:39
  151.8 7.7 collective-permute-done.19
  160.5 18.9 %all-to-all-done = bf16[8,144,448]{2,1,0:T(8,128)(2,1)S(1)} async-done(((bf16[8,144,448]{2,1,0:T(8,128)(2,1)}), bf16[8,144,448]{2,1,0:T(8,128)(2,1)S(1)}, u32[]{:S(2)}, u32[]{:S(2)}) %all-to-all-start) | async-done | bytes 1032224 | tf_op jit(solution)/shard_map/all_to_all | solution.py:39
  198.8 14.1 %all-to-all-done.1 = bf16[8,144,448]{2,1,0:T(8,128)(2,1)S(1)} async-done(((bf16[8,144,448]{2,1,0:T(8,128)(2,1)}), bf16[8,144,448]{2,1,0:T(8,128)(2,1)S(1)}, u32[]{:S(2)}, u32[]{:S(2)}) %all-to-all-start.1) | async-done | bytes 1032224 | tf_op jit(solution)/shard_map/all_to_all | solution.py:39
  232.8 8.5 collective-permute-done.30
  252.6 20.7 %collective-permute-done.33 = bf16[1024,448]{0,1:T(8,128)(2,1)} collective-permute-done((bf16[1024,448]{0,1:T(8,128)(2,1)}, bf16[1024,448]{0,1:T(8,128)(2,1)}, u32[]{:S(2)}, u32[]{:S(2)}) %collective-permute-start.33) | collective-permute-done | bytes 917536 | tf_op jit(solution)/shard_map/ppermute | solution.py:107
  276.1 4.6 all-to-all-start.2
  283.1 17.1 %all-to-all-done.2 = bf16[8,1,16,512]{3,2,1,0:T(8,128)(2,1)S(1)} async-done(((bf16[8,1,16,512]{3,2,1,0:T(8,128)(2,1)}), bf16[8,1,16,512]{3,2,1,0:T(8,128)(2,1)S(1)}, u32[]{:S(2)}, u32[]{:S(2)}) %all-to-all-start.2) | async-done | bytes 131104 | tf_op jit(solution)/shard_map/all_to_all | solution.py:39
  315.4 12.9 %collective-permute-done.37 = bf16[1024,448]{0,1:T(8,128)(2,1)S(1)} collective-permute-done((bf16[1024,448]{0,1:T(8,128)(2,1)}, bf16[1024,448]{0,1:T(8,128)(2,1)S(1)}, u32[]{:S(2)}, u32[]{:S(2)}) %collective-permute-start.37) | collective-permute-done | bytes 917536 | tf_op jit(solution)/shard_map/ppermute | solution.py:107
  333.1 7.3 collective-permute-done.38
  386.4 6.6 collective-permute-done.47
  404.0 21.7 %all-to-all-done.3 = bf16[32,32,192]{2,1,0:T(8,128)(2,1)S(1)} async-done(((bf16[32,32,192]{2,1,0:T(8,128)(2,1)}), bf16[32,32,192]{2,1,0:T(8,128)(2,1)S(1)}, u32[]{:S(2)}, u32[]{:S(2)}) %all-to-all-start.3) | async-done | bytes 393248 | tf_op jit(solution)/shard_map/all_to_all | solution.py:39
  497.4 6.7 collective-permute-done.79
  538.6 7.8 collective-permute-done.98
  548.9 4.6 collective-permute-done.103
  577.6 4.5 fusion.4
  599.4 6.7 collective-permute-done.117
  638.9 5.1 all-to-all-start.4
  646.2 9.7 wide_gradient.1
  668.8 8.0 fusion.362
  676.8 5.2 all-to-all-done.5
  686.2 5.3 collective-permute-done.130
  705.7 8.1 collective-permute-done.132
  754.5 5.9 all-to-all-start.7
  764.1 5.0 collective-permute-done.134
  772.1 5.6 collective-permute-start.135
  784.3 4.6 all-to-all-done.7
  795.2 5.1 collective-permute-done.139
  818.7 11.8 %collective-permute-done.143 = bf16[8,32,1152]{2,1,0:T(8,128)(2,1)S(1)} collective-permute-done((bf16[8,32,1152]{2,1,0:T(8,128)(2,1)S(1)}, bf16[8,32,1152]{2,1,0:T(8,128)(2,1)S(1)}, u32[]{:S(2)}, u32[]{:S(2)}) %collective-permute-start.143) | collective-permute-done | bytes 589856 | tf_op jit(solution)/shard_map/ppermute | solution.py:23
  831.5 7.4 all-to-all-start.8
  875.2 6.0 all-to-all-start.9
  890.0 19.7 %all-to-all-done.9 = bf16[8,144,448]{2,1,0:T(8,128)(2,1)} async-done(((bf16[8,144,448]{2,1,0:T(8,128)(2,1)}), bf16[8,144,448]{2,1,0:T(8,128)(2,1)}, u32[]{:S(2)}, u32[]{:S(2)}) %all-to-all-start.9) | async-done | bytes 1032224 | tf_op jit(solution)/shard_map/all_to_all | solution.py:39
  912.4 4.8 all-to-all-start.10
  919.2 5.3 collective-permute-done.171
  933.9 8.9 all-to-all-done.10
  961.9 8.3 collective-permute-done.152
  992.0 5.1 collective-permute-done.160
  1000.7 7.6 collective-permute-done.161
  1016.3 4.9 copy.773
  1021.2 7.0 reshape.2632
  1047.2 6.1 all-to-all-start.12
  1055.6 6.8 all-to-all-done.12
  (1239 shorter events, 628.8 us)
Async XLA Ops:
  7.2 177.3 %all-gather.11.cloned.1.call-start = ((), (), s32[]{:S(2)}) async-start(), calls=%async_computation.13 | async-start | bytes 2985984 | tf_op jit(solution)/shard_map/all_gather | solution.py:80
  8.0 180.6 %all-gather.13.cloned.1.call-start = ((), (), s32[]{:S(2)}) async-start(), calls=%async_computation.14 | async-start | bytes 2985984 | tf_op jit(solution)/shard_map/all_gather | solution.py:80
  9.1 28.1 %collective-permute-start.5 = (bf16[4,144,288]{2,1,0:T(8,128)(2,1)S(1)}, bf16[4,144,288]{2,1,0:T(8,128)(2,1)S(1)}, u32[]{:S(2)}, u32[]{:S(2)}) collective-permute-start(bf16[4,144,288]{2,1,0:T(8,128)(2,1)S(1)} %pad_maximum_fusion.3.refs_0_), channel_id=1, source_target_pairs={{0,8},{8,16},{16,24},{24,28},{28,20},{20,12},{12,4},{4,0},{1,9},{9... | collective-permute-start | bytes 995336 | tf_op jit(solution)/shard_map/ppermute | solution.py:107
  12.2 27.1 %collective-permute-start.2 = (bf16[4,144,288]{2,1,0:T(8,128)(2,1)S(1)}, bf16[4,144,288]{2,1,0:T(8,128)(2,1)S(1)}, u32[]{:S(2)}, u32[]{:S(2)}) collective-permute-start(bf16[4,144,288]{2,1,0:T(8,128)(2,1)S(1)} %pad_maximum_fusion.3.refs_0_), channel_id=1, source_target_pairs={{0,4},{8,0},{16,8},{24,16},{28,24},{20,28},{12,20},{4,12},{1,5},{9... | collective-permute-start | bytes 995336 | tf_op jit(solution)/shard_map/ppermute | solution.py:107
  37.2 20.0 %collective-permute-start.6 = (bf16[4,144,288]{2,1,0:T(8,128)(2,1)S(1)}, bf16[4,144,288]{2,1,0:T(8,128)(2,1)S(1)}, u32[]{:S(2)}, u32[]{:S(2)}) collective-permute-start(bf16[4,144,288]{2,1,0:T(8,128)(2,1)S(1)} %collective-permute-done.5.refs_7_), channel_id=1, source_target_pairs={{0,8},{8,16},{16,24},{24,28},{28,20},{20,12},{12,4},{4,0},{1,9},{9... | collective-permute-start | bytes 995336 | tf_op jit(solution)/shard_map/ppermute | solution.py:107
  39.3 32.2 %collective-permute-start.3 = (bf16[4,144,288]{2,1,0:T(8,128)(2,1)S(1)}, bf16[4,144,288]{2,1,0:T(8,128)(2,1)S(1)}, u32[]{:S(2)}, u32[]{:S(2)}) collective-permute-start(bf16[4,144,288]{2,1,0:T(8,128)(2,1)S(1)} %collective-permute-done.2.refs_1_), channel_id=1, source_target_pairs={{0,4},{8,0},{16,8},{24,16},{28,24},{20,28},{12,20},{4,12},{1,5},{9... | collective-permute-start | bytes 995336 | tf_op jit(solution)/shard_map/ppermute | solution.py:107
  57.2 25.6 %collective-permute-start.7 = (bf16[4,144,288]{2,1,0:T(8,128)(2,1)S(1)}, bf16[4,144,288]{2,1,0:T(8,128)(2,1)S(1)}, u32[]{:S(2)}, u32[]{:S(2)}) collective-permute-start(bf16[4,144,288]{2,1,0:T(8,128)(2,1)S(1)} %collective-permute-done.6.refs_6_), channel_id=1, source_target_pairs={{0,8},{8,16},{16,24},{24,28},{28,20},{20,12},{12,4},{4,0},{1,9},{9... | collective-permute-start | bytes 995336 | tf_op jit(solution)/shard_map/ppermute | solution.py:107
  135.4 44.0 %all-to-all-start = ((bf16[8,144,448]{2,1,0:T(8,128)(2,1)}), bf16[8,144,448]{2,1,0:T(8,128)(2,1)S(1)}, u32[]{:S(2)}, u32[]{:S(2)}) async-start(bf16[8,144,448]{2,1,0:T(8,128)(2,1)} %get-tuple-element.67), calls=%async_computation | async-start | bytes 2359296 | tf_op jit(solution)/shard_map/all_to_all | solution.py:39
  180.4 32.4 %all-to-all-start.1 = ((bf16[8,144,448]{2,1,0:T(8,128)(2,1)}), bf16[8,144,448]{2,1,0:T(8,128)(2,1)S(1)}, u32[]{:S(2)}, u32[]{:S(2)}) async-start(bf16[8,144,448]{2,1,0:T(8,128)(2,1)} %get-tuple-element.70), calls=%async_computation.1 | async-start | bytes 2359296 | tf_op jit(solution)/shard_map/all_to_all | solution.py:39
  250.3 22.9 %collective-permute-start.33 = (bf16[1024,448]{0,1:T(8,128)(2,1)}, bf16[1024,448]{0,1:T(8,128)(2,1)}, u32[]{:S(2)}, u32[]{:S(2)}) collective-permute-start(bf16[1024,448]{0,1:T(8,128)(2,1)} %get-tuple-element.82), channel_id=1, source_target_pairs={{0,8},{8,16},{16,24},{24,28},{28,20},{20,12},{12,4},{4,0},{1,9},{9... | collective-permute-start | bytes 2752520 | tf_op jit(solution)/shard_map/ppermute | solution.py:107
  252.0 22.7 %collective-permute-start.32 = (bf16[1024,448]{0,1:T(8,128)(2,1)}, bf16[1024,448]{0,1:T(8,128)(2,1)}, u32[]{:S(2)}, u32[]{:S(2)}) collective-permute-start(bf16[1024,448]{0,1:T(8,128)(2,1)} %get-tuple-element.82), channel_id=1, source_target_pairs={{0,4},{8,0},{16,8},{24,16},{28,24},{20,28},{12,20},{4,12},{1,5},{9... | collective-permute-start | bytes 2752520 | tf_op jit(solution)/shard_map/ppermute | solution.py:107
  273.2 32.1 %collective-permute-start.35 = (bf16[1024,448]{0,1:T(8,128)(2,1)}, bf16[1024,448]{0,1:T(8,128)(2,1)}, u32[]{:S(2)}, u32[]{:S(2)}) collective-permute-start(bf16[1024,448]{0,1:T(8,128)(2,1)} %collective-permute-done.33), channel_id=1, source_target_pairs={{0,8},{8,16},{16,24},{24,28},{28,20},{20,12},{12,4},{4,0},{1,9},{9... | collective-permute-start | bytes 2752520 | tf_op jit(solution)/shard_map/ppermute | solution.py:107
  274.7 31.1 %collective-permute-start.34 = (bf16[1024,448]{0,1:T(8,128)(2,1)}, bf16[1024,448]{0,1:T(8,128)(2,1)}, u32[]{:S(2)}, u32[]{:S(2)}) collective-permute-start(bf16[1024,448]{0,1:T(8,128)(2,1)} %collective-permute-done.32), channel_id=1, source_target_pairs={{0,4},{8,0},{16,8},{24,16},{28,24},{20,28},{12,20},{4,12},{1,5},{9... | collective-permute-start | bytes 2752520 | tf_op jit(solution)/shard_map/ppermute | solution.py:107
  276.1 24.1 %all-to-all-start.2 = ((bf16[8,1,16,512]{3,2,1,0:T(8,128)(2,1)}), bf16[8,1,16,512]{3,2,1,0:T(8,128)(2,1)S(1)}, u32[]{:S(2)}, u32[]{:S(2)}) async-start(bf16[8,1,16,512]{3,2,1,0:T(8,128)(2,1)} %bitcast.1145), calls=%async_computation.2 | async-start | bytes 262144 | tf_op jit(solution)/shard_map/all_to_all | solution.py:39
  280.7 147.2 %all-gather.15.cloned.1.call-start = ((), (), s32[]{:S(2)}) async-start(), calls=%async_computation.15 | async-start | bytes 3538944 | tf_op jit(solution)/shard_map/all_gather | solution.py:80
  280.7 20.8 %collective-permute-start = (bf16[512,192]{0,1:T(8,128)(2,1)S(1)}, bf16[512,192]{0,1:T(8,128)(2,1)S(1)}, u32[]{:S(2)}, u32[]{:S(2)}) collective-permute-start(bf16[512,192]{0,1:T(8,128)(2,1)S(1)} %bitcast.1250), channel_id=1, source_target_pairs={{0,2},{1,3},{2,0},{3,1},{4,6},{5,7},{6,4},{7,5},{8,10},{9,11},{10,... | collective-permute-start | bytes 589832 | tf_op jit(solution)/shard_map/ppermute | solution.py:23
  301.6 42.2 %collective-permute-start.1 = (bf16[2,512,192]{1,2,0:T(8,128)(2,1)S(1)}, bf16[2,512,192]{1,2,0:T(8,128)(2,1)S(1)}, u32[]{:S(2)}, u32[]{:S(2)}) collective-permute-start(bf16[2,512,192]{1,2,0:T(8,128)(2,1)S(1)} %maximum_select_fusion.39), channel_id=1, source_target_pairs={{0,1},{1,0},{2,3},{3,2},{4,5},{5,4},{6,7},{7,6},{8,9},{9,8},{10,11... | collective-permute-start | bytes 1179656 | tf_op jit(solution)/shard_map/ppermute | solution.py:19
  305.2 39.6 %collective-permute-start.43 = (bf16[2,8,1,16,512]{4,3,1,2,0:T(8,128)(2,1)S(1)}, bf16[2,8,1,16,512]{4,3,1,2,0:T(8,128)(2,1)S(1)}, u32[]{:S(2)}, u32[]{:S(2)}) collective-permute-start(bf16[2,8,1,16,512]{4,3,1,2,0:T(8,128)(2,1)S(1)} %maximum_select_fusion.43), channel_id=1, source_target_pairs={{0,1},{1,0},{2,3},{3,2},{4,5},{5,4},{6,7},{7,6},{8,9},{9,8},{10,11... | collective-permute-start | bytes 786440 | tf_op jit(solution)/shard_map/ppermute | solution.py:19
  305.3 23.0 %collective-permute-start.37 = (bf16[1024,448]{0,1:T(8,128)(2,1)}, bf16[1024,448]{0,1:T(8,128)(2,1)S(1)}, u32[]{:S(2)}, u32[]{:S(2)}) collective-permute-start(bf16[1024,448]{0,1:T(8,128)(2,1)} %collective-permute-done.35), channel_id=1, source_target_pairs={{0,8},{8,16},{16,24},{24,28},{28,20},{20,12},{12,4},{4,0},{1,9},{9... | collective-permute-start | bytes 2752520 | tf_op jit(solution)/shard_map/ppermute | solution.py:107
  305.8 23.0 %collective-permute-start.36 = (bf16[1024,448]{0,1:T(8,128)(2,1)}, bf16[1024,448]{0,1:T(8,128)(2,1)S(1)}, u32[]{:S(2)}, u32[]{:S(2)}) collective-permute-start(bf16[1024,448]{0,1:T(8,128)(2,1)} %collective-permute-done.34), channel_id=1, source_target_pairs={{0,4},{8,0},{16,8},{24,16},{28,24},{20,28},{12,20},{4,12},{1,5},{9... | collective-permute-start | bytes 2752520 | tf_op jit(solution)/shard_map/ppermute | solution.py:107
  399.3 26.4 %all-to-all-start.3 = ((bf16[32,32,192]{2,1,0:T(8,128)(2,1)}), bf16[32,32,192]{2,1,0:T(8,128)(2,1)S(1)}, u32[]{:S(2)}, u32[]{:S(2)}) async-start(bf16[32,32,192]{2,1,0:T(8,128)(2,1)} %bitcast.101), calls=%async_computation.3 | async-start | bytes 1048576 | tf_op jit(solution)/shard_map/all_to_all | solution.py:39
  403.3 224.2 %all-gather.17.cloned.1.call-start = ((), (), s32[]{:S(2)}) async-start(), calls=%async_computation.16 | async-start | bytes 4257792 | tf_op jit(solution)/shard_map/all_gather | solution.py:80
  445.5 16.7 %collective-permute-start.58 = (bf16[32,4096]{1,0:T(8,128)(2,1)S(1)}, bf16[32,4096]{1,0:T(8,128)(2,1)S(1)}, u32[]{:S(2)}, u32[]{:S(2)}) collective-permute-start(bf16[32,4096]{1,0:T(8,128)(2,1)S(1)} %constant_dynamic-update-slice_fusion.2), channel_id=1, source_target_pairs={{0,2},{1,3},{2,0},{3,1},{4,6},{5,7},{6,4},{7,5},{8,10},{9,11},{10,... | collective-permute-start | bytes 786440 | tf_op jit(solution)/shard_map/ppermute | solution.py:23
  488.2 30.9 %collective-permute-start.73 = (bf16[16,4096]{1,0:T(8,128)(2,1)}, bf16[16,4096]{1,0:T(8,128)(2,1)}, u32[]{:S(2)}, u32[]{:S(2)}) collective-permute-start(bf16[16,4096]{1,0:T(8,128)(2,1)} %fusion.262), channel_id=1, source_target_pairs={{0,2},{1,3},{2,0},{3,1},{4,6},{5,7},{6,4},{7,5},{8,10},{9,11},{10,... | collective-permute-start | bytes 393224 | tf_op jit(solution)/shard_map/ppermute | solution.py:23
  534.6 22.5 %collective-permute-start.96 = (bf16[32,4096]{1,0:T(8,128)(2,1)S(1)}, bf16[32,4096]{1,0:T(8,128)(2,1)S(1)}, u32[]{:S(2)}, u32[]{:S(2)}) collective-permute-start(bf16[32,4096]{1,0:T(8,128)(2,1)S(1)} %constant_dynamic-update-slice_fusion.15), channel_id=1, source_target_pairs={{0,2},{1,3},{2,0},{3,1},{4,6},{5,7},{6,4},{7,5},{8,10},{9,11},{10,... | collective-permute-start | bytes 786440 | tf_op jit(solution)/shard_map/ppermute | solution.py:23
  536.4 22.1 %collective-permute-start.93 = (bf16[2,16,4096]{2,1,0:T(8,128)(2,1)S(1)}, bf16[2,16,4096]{2,1,0:T(8,128)(2,1)S(1)}, u32[]{:S(2)}, u32[]{:S(2)}) collective-permute-start(bf16[2,16,4096]{2,1,0:T(8,128)(2,1)S(1)} %maximum_select_fusion.46), channel_id=1, source_target_pairs={{0,1},{1,0},{2,3},{3,2},{4,5},{5,4},{6,7},{7,6},{8,9},{9,8},{10,11... | collective-permute-start | bytes 786440 | tf_op jit(solution)/shard_map/ppermute | solution.py:19
  586.3 35.8 %collective-permute-start.111 = (bf16[16,4096]{1,0:T(8,128)(2,1)S(1)}, bf16[16,4096]{1,0:T(8,128)(2,1)S(1)}, u32[]{:S(2)}, u32[]{:S(2)}) collective-permute-start(bf16[16,4096]{1,0:T(8,128)(2,1)S(1)} %fusion.264), channel_id=1, source_target_pairs={{0,2},{1,3},{2,0},{3,1},{4,6},{5,7},{6,4},{7,5},{8,10},{9,11},{10,... | collective-permute-start | bytes 393224 | tf_op jit(solution)/shard_map/ppermute | solution.py:23
  638.9 20.7 %all-to-all-start.4 = ((bf16[32,32,192]{2,1,0:T(8,128)(2,1)}), bf16[32,32,192]{2,1,0:T(8,128)(2,1)S(1)}, u32[]{:S(2)}, u32[]{:S(2)}) async-start(bf16[32,32,192]{2,1,0:T(8,128)(2,1)} %bitcast.259), calls=%async_computation.4 | async-start | bytes 1048576 | tf_op jit(solution)/shard_map/all_to_all | solution.py:39
  660.9 21.1 %all-to-all-start.5 = ((bf16[8,5,32,192]{3,2,1,0:T(8,128)(2,1)}), bf16[8,5,32,192]{3,2,1,0:T(8,128)(2,1)S(1)}, u32[]{:S(2)}, u32[]{:S(2)}) async-start(bf16[8,5,32,192]{3,2,1,0:T(8,128)(2,1)} %broadcast_in_dim.161), calls=%async_computation.5 | async-start | bytes 1310720 | tf_op jit(solution)/shard_map/all_to_all | solution.py:39
  692.9 114.7 %collective-permute-start.154 = (bf16[2,2,1024]{2,1,0:T(2,128)(2,1)}, bf16[2,2,1024]{2,1,0:T(2,128)(2,1)}, u32[]{:S(2)}, u32[]{:S(2)}) collective-permute-start(bf16[2,2,1024]{2,1,0:T(2,128)(2,1)} %fusion.302), channel_id=1, source_target_pairs={{0,1},{1,0},{2,3},{3,2},{4,5},{5,4},{6,7},{7,6},{8,9},{9,8},{10,11... | collective-permute-start | bytes 24584 | tf_op jit(solution)/shard_map/ppermute | solution.py:19
  693.4 119.6 %collective-permute-start.90 = (f32[16,4096]{1,0:T(8,128)S(1)}, f32[16,4096]{1,0:T(8,128)}, u32[]{:S(2)}, u32[]{:S(2)}) collective-permute-start(f32[16,4096]{1,0:T(8,128)S(1)} %copy-done.62), channel_id=1, source_target_pairs={{0,2},{1,3},{2,0},{3,1},{4,6},{5,7},{6,4},{7,5},{8,10},{9,11},{10,... | collective-permute-start | bytes 786440 | tf_op jit(solution)/shard_map/ppermute | solution.py:23
  715.7 21.1 %collective-permute-start.133 = (bf16[1024,448]{0,1:T(8,128)(2,1)S(1)}, bf16[1024,448]{0,1:T(8,128)(2,1)S(1)}, u32[]{:S(2)}, u32[]{:S(2)}) collective-permute-start(bf16[1024,448]{0,1:T(8,128)(2,1)S(1)} %add_convert_fusion.5), channel_id=1, source_target_pairs={{0,8},{8,16},{16,24},{24,28},{28,20},{20,12},{12,4},{4,0},{1,9},{9... | collective-permute-start | bytes 2752520 | tf_op jit(solution)/shard_map/ppermute | solution.py:107
  718.6 28.8 %collective-permute-start.137 = (bf16[1024,448]{0,1:T(8,128)(2,1)}, bf16[1024,448]{0,1:T(8,128)(2,1)}, u32[]{:S(2)}, u32[]{:S(2)}) collective-permute-start(bf16[1024,448]{0,1:T(8,128)(2,1)} %add_convert_fusion.2), channel_id=1, source_target_pairs={{0,4},{8,0},{16,8},{24,16},{28,24},{20,28},{12,20},{4,12},{1,5},{9... | collective-permute-start | bytes 2752520 | tf_op jit(solution)/shard_map/ppermute | solution.py:107
  745.4 23.7 %collective-permute-start.134 = (bf16[1024,448]{0,1:T(8,128)(2,1)}, bf16[1024,448]{0,1:T(8,128)(2,1)}, u32[]{:S(2)}, u32[]{:S(2)}) collective-permute-start(bf16[1024,448]{0,1:T(8,128)(2,1)} %add_convert_fusion.4), channel_id=1, source_target_pairs={{0,8},{8,16},{16,24},{24,28},{28,20},{20,12},{12,4},{4,0},{1,9},{9... | collective-permute-start | bytes 2752520 | tf_op jit(solution)/shard_map/ppermute | solution.py:107
  750.4 27.3 %collective-permute-start.138 = (bf16[1024,448]{0,1:T(8,128)(2,1)}, bf16[1024,448]{0,1:T(8,128)(2,1)}, u32[]{:S(2)}, u32[]{:S(2)}) collective-permute-start(bf16[1024,448]{0,1:T(8,128)(2,1)} %add_convert_fusion.1), channel_id=1, source_target_pairs={{0,4},{8,0},{16,8},{24,16},{28,24},{20,28},{12,20},{4,12},{1,5},{9... | collective-permute-start | bytes 2752520 | tf_op jit(solution)/shard_map/ppermute | solution.py:107
  754.5 34.4 %all-to-all-start.7 = ((bf16[8,64,576]{2,1,0:T(8,128)(2,1)}), bf16[8,64,576]{2,1,0:T(8,128)(2,1)}, u32[]{:S(2)}, u32[]{:S(2)}) async-start(bf16[8,64,576]{2,1,0:T(8,128)(2,1)} %broadcast_in_dim.171), calls=%async_computation.7 | async-start | bytes 1310720 | tf_op jit(solution)/shard_map/all_to_all | solution.py:39
  763.6 17.2 %collective-permute-start.140 = (bf16[8,1,16,512]{3,2,0,1:T(8,128)(2,1)S(1)}, bf16[8,1,16,512]{3,2,0,1:T(8,128)(2,1)S(1)}, u32[]{:S(2)}, u32[]{:S(2)}) collective-permute-start(bf16[8,1,16,512]{3,2,0,1:T(8,128)(2,1)S(1)} %bitcast.1321), channel_id=1, source_target_pairs={{0,2},{1,3},{2,0},{3,1},{4,6},{5,7},{6,4},{7,5},{8,10},{9,11},{10,... | collective-permute-start | bytes 393224 | tf_op jit(solution)/shard_map/ppermute | solution.py:23
  772.1 23.1 %collective-permute-start.135 = (bf16[1024,448]{0,1:T(8,128)(2,1)}, bf16[1024,448]{0,1:T(8,128)(2,1)}, u32[]{:S(2)}, u32[]{:S(2)}) collective-permute-start(bf16[1024,448]{0,1:T(8,128)(2,1)} %add_convert_fusion.3), channel_id=1, source_target_pairs={{0,8},{8,16},{16,24},{24,28},{28,20},{20,12},{12,4},{4,0},{1,9},{9... | collective-permute-start | bytes 2752520 | tf_op jit(solution)/shard_map/ppermute | solution.py:107
  780.6 19.7 %collective-permute-start.139 = (bf16[1024,448]{0,1:T(8,128)(2,1)}, bf16[1024,448]{0,1:T(8,128)(2,1)}, u32[]{:S(2)}, u32[]{:S(2)}) collective-permute-start(bf16[1024,448]{0,1:T(8,128)(2,1)} %add_convert_fusion), channel_id=1, source_target_pairs={{0,4},{8,0},{16,8},{24,16},{28,24},{20,28},{12,20},{4,12},{1,5},{9... | collective-permute-start | bytes 2752520 | tf_op jit(solution)/shard_map/ppermute | solution.py:107
  831.5 23.2 %all-to-all-start.8 = ((bf16[8,32,1152]{2,1,0:T(8,128)(2,1)}), bf16[8,32,1152]{2,1,0:T(8,128)(2,1)}, u32[]{:S(2)}, u32[]{:S(2)}) async-start(bf16[8,32,1152]{2,1,0:T(8,128)(2,1)} %fusion.41), calls=%async_computation.8 | async-start | bytes 1179648 | tf_op jit(solution)/shard_map/all_to_all | solution.py:39
  875.2 34.5 %all-to-all-start.9 = ((bf16[8,144,448]{2,1,0:T(8,128)(2,1)}), bf16[8,144,448]{2,1,0:T(8,128)(2,1)}, u32[]{:S(2)}, u32[]{:S(2)}) async-start(bf16[8,144,448]{2,1,0:T(8,128)(2,1)} %bitcast.1196), calls=%async_computation.9 | async-start | bytes 2359296 | tf_op jit(solution)/shard_map/all_to_all | solution.py:39
  912.4 30.3 %all-to-all-start.10 = ((bf16[8,128,512]{2,1,0:T(8,128)(2,1)}), bf16[8,128,512]{2,1,0:T(8,128)(2,1)}, u32[]{:S(2)}, u32[]{:S(2)}) async-start(bf16[8,128,512]{2,1,0:T(8,128)(2,1)} %pad_maximum_fusion.1), calls=%async_computation.10 | async-start | bytes 2097152 | tf_op jit(solution)/shard_map/all_to_all | solution.py:39
  944.1 41.4 %all-to-all-start.11 = ((bf16[8,144,448]{2,1,0:T(8,128)(2,1)}), bf16[8,144,448]{2,1,0:T(8,128)(2,1)}, u32[]{:S(2)}, u32[]{:S(2)}) async-start(bf16[8,144,448]{2,1,0:T(8,128)(2,1)} %bitcast.1195), calls=%async_computation.11 | async-start | bytes 2359296 | tf_op jit(solution)/shard_map/all_to_all | solution.py:39
  948.4 120.0 %all-gather.19.cloned.1.call-start = ((), (), s32[]{:S(2)}) async-start(), calls=%async_computation.17 | async-start | bytes 2488320 | tf_op jit(solution)/shard_map/all_gather | solution.py:80
  951.7 20.9 %collective-permute-start.158 = (bf16[8,4,32,144]{3,2,1,0:T(8,128)(2,1)}, bf16[8,4,32,144]{3,2,1,0:T(8,128)(2,1)}, u32[]{:S(2)}, u32[]{:S(2)}) collective-permute-start(bf16[8,4,32,144]{3,2,1,0:T(8,128)(2,1)} %bitcast.370), channel_id=1, source_target_pairs={{0,2},{1,3},{2,0},{3,1},{4,6},{5,7},{6,4},{7,5},{8,10},{9,11},{10,... | collective-permute-start | bytes 884744 | tf_op jit(solution)/shard_map/ppermute | solution.py:23
  989.0 43.4 %collective-permute-start.150 = (f32[128,1152]{1,0:T(8,128)S(1)}, f32[128,1152]{1,0:T(8,128)S(1)}, u32[]{:S(2)}, u32[]{:S(2)}) collective-permute-start(f32[128,1152]{1,0:T(8,128)S(1)} %convolution_add_fusion.2), channel_id=1, source_target_pairs={{0,1},{1,0},{2,3},{3,2},{4,5},{5,4},{6,7},{7,6},{8,9},{9,8},{10,11... | collective-permute-start | bytes 1769480 | tf_op jit(solution)/shard_map/ppermute | solution.py:19
  1008.3 20.0 %collective-permute-start.162 = (bf16[128,864]{0,1:T(8,128)(2,1)S(1)}, bf16[128,864]{0,1:T(8,128)(2,1)S(1)}, u32[]{:S(2)}, u32[]{:S(2)}) collective-permute-start(bf16[128,864]{0,1:T(8,128)(2,1)S(1)} %collective-permute-done.161), channel_id=1, source_target_pairs={{0,4},{8,0},{16,8},{24,16},{28,24},{20,28},{12,20},{4,12},{1,5},{9... | collective-permute-start | bytes 663560 | tf_op jit(solution)/shard_map/ppermute | solution.py:107
  1010.8 17.7 %collective-permute-start.165 = (bf16[128,864]{0,1:T(8,128)(2,1)S(1)}, bf16[128,864]{0,1:T(8,128)(2,1)S(1)}, u32[]{:S(2)}, u32[]{:S(2)}) collective-permute-start(bf16[128,864]{0,1:T(8,128)(2,1)S(1)} %collective-permute-done.164), channel_id=1, source_target_pairs={{0,8},{8,16},{16,24},{24,28},{28,20},{20,12},{12,4},{4,0},{1,9},{9... | collective-permute-start | bytes 663560 | tf_op jit(solution)/shard_map/ppermute | solution.py:107
  (337 other events, 3289.6 us)
Sparse Core Ops, SparseCore 0:
  10.2 67.2 all-gather.10
  79.7 62.5 all-gather.12
  351.1 70.9 all-gather.14
  529.7 76.9 all-gather.16
  952.3 69.0 all-gather.18

commit v5 on v4

--- a/solution.py
+++ b/solution.py
@@ -536,8 +536,9 @@
     dvision_part = dot(dgate_low, gate_own, 1, 1) + dot(dup_low, up_own, 1, 1)
     dvision_sub = sum_every(dvision_part.reshape(4, blk, sub, wide))
     grad_gate = dot(vision_low, dgate_low, 0, 0).astype(BF).reshape(blk, wcol, unit)
-    grad_up = dot(vision_low, dup_low, 0, 0).astype(BF).reshape(blk, wcol, unit)
-    dvision_sub, grad_gate, grad_up = lax.optimization_barrier((dvision_sub, grad_gate, grad_up))
+    dvision_sub, grad_gate = lax.optimization_barrier((dvision_sub, grad_gate))
+    dup_late = after(dup_low, dvision_sub)
+    grad_up = dot(vision_low, dup_late, 0, 0).astype(BF).reshape(blk, wcol, unit)
     dvision_out = gather_tp(dvision_sub).reshape(tok, wide)
     grad_gate = exchange(grad_gate, "blk")
 

time: 1090 us -> 1090 us (level)
    unnamed x433 -> x463, local copies, waits for them, and re-layouts: 38.9 us -> 37.9 us
  transfers between devices with their start and end apart: 190 -> 190, of which waited for: 106 -> 105; matrix products, arithmetic and copies ran while one was open for 25% -> 26% of each run, Pallas kernels for 1% -> 1%
where the time goes in v5:
time: 1090 us; the launch traced here: 1080 us
  waiting for transfers between devices  447 us (41%)
  starting transfers between devices  239 us (22%)
  matrix products  142 us (13%)
  local copies, waits for them, and re-layouts  117 us (11%)
  other arithmetic  83.9 us (8%)
  between operations  35.7 us (3%)
  Pallas kernels  11.1 us (1%)
    ppermute x88, waiting for transfers between devices, pass_on(): return lax.ppermute(value, 'blk', route)  212 us
    all_to_all x13, waiting for transfers between devices, exchange(): return lax.all_to_all(chunks, axis, 0, 0, tiled=True)  121 us
    ppermute x88, starting transfers between devices, pass_on(): return lax.ppermute(value, 'blk', route)  116 us
    dot_general x58, matrix products, dot(): lax.dot_general(left, right, (((on_left,), (on_right,)), ((), ())), prefe...  113 us
    ppermute x42, waiting for transfers between devices, swap_x(): lax.ppermute(value, 'tp', [(i, i ^ 2) for i in range(lax.axis_size('tp'))])  103 us
    all_to_all x13, starting transfers between devices, exchange(): return lax.all_to_all(chunks, axis, 0, 0, tiled=True)  64.6 us
    ppermute x42, starting transfers between devices, swap_x(): lax.ppermute(value, 'tp', [(i, i ^ 2) for i in range(lax.axis_size('tp'))])  49.8 us
    unnamed x463, local copies, waits for them, and re-layouts  37.9 us
  transfers between devices with their start and end apart: 190, of which 105 were waited for; matrix products, arithmetic and copies ran while one was open for 26% of the time, Pallas kernels for 1%

profile of v5, /device:TPU:0, one launch (start us, length us, event | category | flops | bytes accessed | tf_op | source)
XLA Modules:
  0.0 1076.8 jit_solution(11332416993891386925)
XLA Ops:
  40.1 16.7 %collective-permute-done.6.refs_6_ = bf16[4,144,288]{2,1,0:T(8,128)(2,1)S(1)} collective-permute-done((bf16[4,144,288]{2,1,0:T(8,128)(2,1)S(1)}, bf16[4,144,288]{2,1,0:T(8,128)(2,1)S(1)}, u32[]{:S(2)}, u32[]{:S(2)}) %collective-permute-start.6) | collective-permute-done | bytes 331808 | tf_op jit(solution)/shard_map/ppermute | solution.py:107
  56.8 9.8 collective-permute-start.7
  70.9 6.1 reshape.2543
  96.3 6.6 collective-permute-done.10
  105.0 5.8 collective-permute-done.11
  118.1 9.4 collective-permute-done.17
  134.0 5.8 all-to-all-start
  142.3 7.3 collective-permute-done.19
  150.6 18.9 %all-to-all-done = bf16[8,144,448]{2,1,0:T(8,128)(2,1)S(1)} async-done(((bf16[8,144,448]{2,1,0:T(8,128)(2,1)}), bf16[8,144,448]{2,1,0:T(8,128)(2,1)S(1)}, u32[]{:S(2)}, u32[]{:S(2)}) %all-to-all-start) | async-done | bytes 1032224 | tf_op jit(solution)/shard_map/all_to_all | solution.py:39
  188.2 14.5 %all-to-all-done.1 = bf16[8,144,448]{2,1,0:T(8,128)(2,1)S(1)} async-done(((bf16[8,144,448]{2,1,0:T(8,128)(2,1)}), bf16[8,144,448]{2,1,0:T(8,128)(2,1)S(1)}, u32[]{:S(2)}, u32[]{:S(2)}) %all-to-all-start.1) | async-done | bytes 1032224 | tf_op jit(solution)/shard_map/all_to_all | solution.py:39
  223.6 8.1 collective-permute-done.30
  242.9 20.7 %collective-permute-done.33 = bf16[1024,448]{0,1:T(8,128)(2,1)} collective-permute-done((bf16[1024,448]{0,1:T(8,128)(2,1)}, bf16[1024,448]{0,1:T(8,128)(2,1)}, u32[]{:S(2)}, u32[]{:S(2)}) %collective-permute-start.33) | collective-permute-done | bytes 917536 | tf_op jit(solution)/shard_map/ppermute | solution.py:107
  266.4 4.6 all-to-all-start.2
  273.8 16.8 %all-to-all-done.2 = bf16[8,1,16,512]{3,2,1,0:T(8,128)(2,1)S(1)} async-done(((bf16[8,1,16,512]{3,2,1,0:T(8,128)(2,1)}), bf16[8,1,16,512]{3,2,1,0:T(8,128)(2,1)S(1)}, u32[]{:S(2)}, u32[]{:S(2)}) %all-to-all-start.2) | async-done | bytes 131104 | tf_op jit(solution)/shard_map/all_to_all | solution.py:39
  304.6 13.8 %collective-permute-done.37 = bf16[1024,448]{0,1:T(8,128)(2,1)S(1)} collective-permute-done((bf16[1024,448]{0,1:T(8,128)(2,1)S(1)}, bf16[1024,448]{0,1:T(8,128)(2,1)S(1)}, u32[]{:S(2)}, u32[]{:S(2)}) %collective-permute-start.37) | collective-permute-done | bytes 917536 | tf_op jit(solution)/shard_map/ppermute | solution.py:107
  323.3 7.3 collective-permute-done.38
  380.9 5.9 collective-permute-done.47
  392.7 4.8 all-to-all-start.3
  398.8 17.0 %all-to-all-done.3 = bf16[32,32,192]{2,1,0:T(8,128)(2,1)S(1)} async-done(((bf16[32,32,192]{2,1,0:T(8,128)(2,1)}), bf16[32,32,192]{2,1,0:T(8,128)(2,1)S(1)}, u32[]{:S(2)}, u32[]{:S(2)}) %all-to-all-start.3) | async-done | bytes 393248 | tf_op jit(solution)/shard_map/all_to_all | solution.py:39
  457.6 5.1 collective-permute-done.70
  466.9 4.5 fusion.2
  489.9 6.8 collective-permute-done.79
  532.7 6.9 collective-permute-done.98
  543.3 4.6 collective-permute-done.103
  572.7 4.5 fusion.4
  593.3 6.7 collective-permute-done.117
  639.7 5.1 all-to-all-start.4
  647.0 9.7 wide_gradient.1
  669.6 8.0 fusion.362
  677.6 5.3 all-to-all-done.5
  686.8 5.2 collective-permute-done.130
  705.9 8.1 collective-permute-done.132
  754.9 5.9 all-to-all-start.7
  764.5 4.9 collective-permute-done.134
  772.3 5.7 collective-permute-start.135
  795.7 5.1 collective-permute-done.139
  818.4 11.8 %collective-permute-done.143 = bf16[8,32,1152]{2,1,0:T(8,128)(2,1)S(1)} collective-permute-done((bf16[8,32,1152]{2,1,0:T(8,128)(2,1)S(1)}, bf16[8,32,1152]{2,1,0:T(8,128)(2,1)S(1)}, u32[]{:S(2)}, u32[]{:S(2)}) %collective-permute-start.143) | collective-permute-done | bytes 589856 | tf_op jit(solution)/shard_map/ppermute | solution.py:23
  831.3 7.4 all-to-all-start.8
  847.3 7.2 all-to-all-done.8
  893.5 14.5 %all-to-all-done.9 = bf16[8,144,448]{2,1,0:T(8,128)(2,1)} async-done(((bf16[8,144,448]{2,1,0:T(8,128)(2,1)}), bf16[8,144,448]{2,1,0:T(8,128)(2,1)}, u32[]{:S(2)}, u32[]{:S(2)}) %all-to-all-start.9) | async-done | bytes 1032224 | tf_op jit(solution)/shard_map/all_to_all | solution.py:39
  910.8 4.7 all-to-all-start.10
  929.2 11.9 %all-to-all-done.10 = bf16[8,128,512]{2,1,0:T(8,128)(2,1)} async-done(((bf16[8,128,512]{2,1,0:T(8,128)(2,1)}), bf16[8,128,512]{2,1,0:T(8,128)(2,1)}, u32[]{:S(2)}, u32[]{:S(2)}) %all-to-all-start.10) | async-done | bytes 1048608 | tf_op jit(solution)/shard_map/all_to_all | solution.py:39
  960.3 8.3 collective-permute-done.152
  998.2 7.8 collective-permute-done.161
  1011.6 4.9 copy.773
  1016.5 7.0 reshape.2632
  1044.1 6.4 all-to-all-start.12
  1052.7 6.8 all-to-all-done.12
  (1269 shorter events, 640.2 us)
Async XLA Ops:
  7.2 167.3 %all-gather.11.cloned.1.call-start = ((), (), s32[]{:S(2)}) async-start(), calls=%async_computation.13 | async-start | bytes 2985984 | tf_op jit(solution)/shard_map/all_gather | solution.py:80
  8.0 170.6 %all-gather.13.cloned.1.call-start = ((), (), s32[]{:S(2)}) async-start(), calls=%async_computation.14 | async-start | bytes 2985984 | tf_op jit(solution)/shard_map/all_gather | solution.py:80
  9.1 27.9 %collective-permute-start.5 = (bf16[4,144,288]{2,1,0:T(8,128)(2,1)S(1)}, bf16[4,144,288]{2,1,0:T(8,128)(2,1)S(1)}, u32[]{:S(2)}, u32[]{:S(2)}) collective-permute-start(bf16[4,144,288]{2,1,0:T(8,128)(2,1)S(1)} %pad_maximum_fusion.3.refs_0_), channel_id=1, source_target_pairs={{0,8},{8,16},{16,24},{24,28},{28,20},{20,12},{12,4},{4,0},{1,9},{9... | collective-permute-start | bytes 995336 | tf_op jit(solution)/shard_map/ppermute | solution.py:107
  12.2 26.9 %collective-permute-start.2 = (bf16[4,144,288]{2,1,0:T(8,128)(2,1)S(1)}, bf16[4,144,288]{2,1,0:T(8,128)(2,1)S(1)}, u32[]{:S(2)}, u32[]{:S(2)}) collective-permute-start(bf16[4,144,288]{2,1,0:T(8,128)(2,1)S(1)} %pad_maximum_fusion.3.refs_0_), channel_id=1, source_target_pairs={{0,4},{8,0},{16,8},{24,16},{28,24},{20,28},{12,20},{4,12},{1,5},{9... | collective-permute-start | bytes 995336 | tf_op jit(solution)/shard_map/ppermute | solution.py:107
  37.0 19.8 %collective-permute-start.6 = (bf16[4,144,288]{2,1,0:T(8,128)(2,1)S(1)}, bf16[4,144,288]{2,1,0:T(8,128)(2,1)S(1)}, u32[]{:S(2)}, u32[]{:S(2)}) collective-permute-start(bf16[4,144,288]{2,1,0:T(8,128)(2,1)S(1)} %collective-permute-done.5.refs_7_), channel_id=1, source_target_pairs={{0,8},{8,16},{16,24},{24,28},{28,20},{20,12},{12,4},{4,0},{1,9},{9... | collective-permute-start | bytes 995336 | tf_op jit(solution)/shard_map/ppermute | solution.py:107
  39.1 31.8 %collective-permute-start.3 = (bf16[4,144,288]{2,1,0:T(8,128)(2,1)S(1)}, bf16[4,144,288]{2,1,0:T(8,128)(2,1)S(1)}, u32[]{:S(2)}, u32[]{:S(2)}) collective-permute-start(bf16[4,144,288]{2,1,0:T(8,128)(2,1)S(1)} %collective-permute-done.2.refs_1_), channel_id=1, source_target_pairs={{0,4},{8,0},{16,8},{24,16},{28,24},{20,28},{12,20},{4,12},{1,5},{9... | collective-permute-start | bytes 995336 | tf_op jit(solution)/shard_map/ppermute | solution.py:107
  56.8 24.8 %collective-permute-start.7 = (bf16[4,144,288]{2,1,0:T(8,128)(2,1)S(1)}, bf16[4,144,288]{2,1,0:T(8,128)(2,1)S(1)}, u32[]{:S(2)}, u32[]{:S(2)}) collective-permute-start(bf16[4,144,288]{2,1,0:T(8,128)(2,1)S(1)} %collective-permute-done.6.refs_6_), channel_id=1, source_target_pairs={{0,8},{8,16},{16,24},{24,28},{28,20},{20,12},{12,4},{4,0},{1,9},{9... | collective-permute-start | bytes 995336 | tf_op jit(solution)/shard_map/ppermute | solution.py:107
  134.0 35.5 %all-to-all-start = ((bf16[8,144,448]{2,1,0:T(8,128)(2,1)}), bf16[8,144,448]{2,1,0:T(8,128)(2,1)S(1)}, u32[]{:S(2)}, u32[]{:S(2)}) async-start(bf16[8,144,448]{2,1,0:T(8,128)(2,1)} %get-tuple-element.67), calls=%async_computation | async-start | bytes 2359296 | tf_op jit(solution)/shard_map/all_to_all | solution.py:39
  170.6 32.1 %all-to-all-start.1 = ((bf16[8,144,448]{2,1,0:T(8,128)(2,1)}), bf16[8,144,448]{2,1,0:T(8,128)(2,1)S(1)}, u32[]{:S(2)}, u32[]{:S(2)}) async-start(bf16[8,144,448]{2,1,0:T(8,128)(2,1)} %get-tuple-element.70), calls=%async_computation.1 | async-start | bytes 2359296 | tf_op jit(solution)/shard_map/all_to_all | solution.py:39
  240.6 22.9 %collective-permute-start.33 = (bf16[1024,448]{0,1:T(8,128)(2,1)}, bf16[1024,448]{0,1:T(8,128)(2,1)}, u32[]{:S(2)}, u32[]{:S(2)}) collective-permute-start(bf16[1024,448]{0,1:T(8,128)(2,1)} %get-tuple-element.82), channel_id=1, source_target_pairs={{0,8},{8,16},{16,24},{24,28},{28,20},{20,12},{12,4},{4,0},{1,9},{9... | collective-permute-start | bytes 2752520 | tf_op jit(solution)/shard_map/ppermute | solution.py:107
  242.4 22.7 %collective-permute-start.32 = (bf16[1024,448]{0,1:T(8,128)(2,1)}, bf16[1024,448]{0,1:T(8,128)(2,1)}, u32[]{:S(2)}, u32[]{:S(2)}) collective-permute-start(bf16[1024,448]{0,1:T(8,128)(2,1)} %get-tuple-element.82), channel_id=1, source_target_pairs={{0,4},{8,0},{16,8},{24,16},{28,24},{20,28},{12,20},{4,12},{1,5},{9... | collective-permute-start | bytes 2752520 | tf_op jit(solution)/shard_map/ppermute | solution.py:107
  263.5 32.1 %collective-permute-start.35 = (bf16[1024,448]{0,1:T(8,128)(2,1)}, bf16[1024,448]{0,1:T(8,128)(2,1)S(1)}, u32[]{:S(2)}, u32[]{:S(2)}) collective-permute-start(bf16[1024,448]{0,1:T(8,128)(2,1)} %collective-permute-done.33), channel_id=1, source_target_pairs={{0,8},{8,16},{16,24},{24,28},{28,20},{20,12},{12,4},{4,0},{1,9},{9... | collective-permute-start | bytes 2752520 | tf_op jit(solution)/shard_map/ppermute | solution.py:107
  265.1 31.0 %collective-permute-start.34 = (bf16[1024,448]{0,1:T(8,128)(2,1)}, bf16[1024,448]{0,1:T(8,128)(2,1)}, u32[]{:S(2)}, u32[]{:S(2)}) collective-permute-start(bf16[1024,448]{0,1:T(8,128)(2,1)} %collective-permute-done.32), channel_id=1, source_target_pairs={{0,4},{8,0},{16,8},{24,16},{28,24},{20,28},{12,20},{4,12},{1,5},{9... | collective-permute-start | bytes 2752520 | tf_op jit(solution)/shard_map/ppermute | solution.py:107
  266.4 24.2 %all-to-all-start.2 = ((bf16[8,1,16,512]{3,2,1,0:T(8,128)(2,1)}), bf16[8,1,16,512]{3,2,1,0:T(8,128)(2,1)S(1)}, u32[]{:S(2)}, u32[]{:S(2)}) async-start(bf16[8,1,16,512]{3,2,1,0:T(8,128)(2,1)} %bitcast.1145), calls=%async_computation.2 | async-start | bytes 262144 | tf_op jit(solution)/shard_map/all_to_all | solution.py:39
  271.0 148.0 %all-gather.15.cloned.1.call-start = ((), (), s32[]{:S(2)}) async-start(), calls=%async_computation.15 | async-start | bytes 3538944 | tf_op jit(solution)/shard_map/all_gather | solution.py:80
  271.0 21.3 %collective-permute-start = (bf16[512,192]{0,1:T(8,128)(2,1)S(1)}, bf16[512,192]{0,1:T(8,128)(2,1)S(1)}, u32[]{:S(2)}, u32[]{:S(2)}) collective-permute-start(bf16[512,192]{0,1:T(8,128)(2,1)S(1)} %bitcast.1249), channel_id=1, source_target_pairs={{0,2},{1,3},{2,0},{3,1},{4,6},{5,7},{6,4},{7,5},{8,10},{9,11},{10,... | collective-permute-start | bytes 589832 | tf_op jit(solution)/shard_map/ppermute | solution.py:23
  292.4 41.5 %collective-permute-start.1 = (bf16[2,512,192]{1,2,0:T(8,128)(2,1)S(1)}, bf16[2,512,192]{1,2,0:T(8,128)(2,1)S(1)}, u32[]{:S(2)}, u32[]{:S(2)}) collective-permute-start(bf16[2,512,192]{1,2,0:T(8,128)(2,1)S(1)} %maximum_select_fusion.39), channel_id=1, source_target_pairs={{0,1},{1,0},{2,3},{3,2},{4,5},{5,4},{6,7},{7,6},{8,9},{9,8},{10,11... | collective-permute-start | bytes 1179656 | tf_op jit(solution)/shard_map/ppermute | solution.py:19
  295.6 39.3 %collective-permute-start.43 = (bf16[2,8,1,16,512]{4,3,1,2,0:T(8,128)(2,1)S(1)}, bf16[2,8,1,16,512]{4,3,1,2,0:T(8,128)(2,1)S(1)}, u32[]{:S(2)}, u32[]{:S(2)}) collective-permute-start(bf16[2,8,1,16,512]{4,3,1,2,0:T(8,128)(2,1)S(1)} %maximum_select_fusion.43), channel_id=1, source_target_pairs={{0,1},{1,0},{2,3},{3,2},{4,5},{5,4},{6,7},{7,6},{8,9},{9,8},{10,11... | collective-permute-start | bytes 786440 | tf_op jit(solution)/shard_map/ppermute | solution.py:19
  295.7 22.8 %collective-permute-start.37 = (bf16[1024,448]{0,1:T(8,128)(2,1)S(1)}, bf16[1024,448]{0,1:T(8,128)(2,1)S(1)}, u32[]{:S(2)}, u32[]{:S(2)}) collective-permute-start(bf16[1024,448]{0,1:T(8,128)(2,1)S(1)} %collective-permute-done.35), channel_id=1, source_target_pairs={{0,8},{8,16},{16,24},{24,28},{28,20},{20,12},{12,4},{4,0},{1,9},{9... | collective-permute-start | bytes 2752520 | tf_op jit(solution)/shard_map/ppermute | solution.py:107
  296.1 22.8 %collective-permute-start.36 = (bf16[1024,448]{0,1:T(8,128)(2,1)}, bf16[1024,448]{0,1:T(8,128)(2,1)S(1)}, u32[]{:S(2)}, u32[]{:S(2)}) collective-permute-start(bf16[1024,448]{0,1:T(8,128)(2,1)} %collective-permute-done.34), channel_id=1, source_target_pairs={{0,4},{8,0},{16,8},{24,16},{28,24},{20,28},{12,20},{4,12},{1,5},{9... | collective-permute-start | bytes 2752520 | tf_op jit(solution)/shard_map/ppermute | solution.py:107
  392.7 23.1 %all-to-all-start.3 = ((bf16[32,32,192]{2,1,0:T(8,128)(2,1)}), bf16[32,32,192]{2,1,0:T(8,128)(2,1)S(1)}, u32[]{:S(2)}, u32[]{:S(2)}) async-start(bf16[32,32,192]{2,1,0:T(8,128)(2,1)} %bitcast.101), calls=%async_computation.3 | async-start | bytes 1048576 | tf_op jit(solution)/shard_map/all_to_all | solution.py:39
  397.5 224.7 %all-gather.17.cloned.1.call-start = ((), (), s32[]{:S(2)}) async-start(), calls=%async_computation.16 | async-start | bytes 4257792 | tf_op jit(solution)/shard_map/all_gather | solution.py:80
  480.2 33.9 %collective-permute-start.73 = (bf16[16,4096]{1,0:T(8,128)(2,1)}, bf16[16,4096]{1,0:T(8,128)(2,1)}, u32[]{:S(2)}, u32[]{:S(2)}) collective-permute-start(bf16[16,4096]{1,0:T(8,128)(2,1)} %fusion.262), channel_id=1, source_target_pairs={{0,2},{1,3},{2,0},{3,1},{4,6},{5,7},{6,4},{7,5},{8,10},{9,11},{10,... | collective-permute-start | bytes 393224 | tf_op jit(solution)/shard_map/ppermute | solution.py:23
  529.4 22.7 %collective-permute-start.96 = (bf16[32,4096]{1,0:T(8,128)(2,1)S(1)}, bf16[32,4096]{1,0:T(8,128)(2,1)S(1)}, u32[]{:S(2)}, u32[]{:S(2)}) collective-permute-start(bf16[32,4096]{1,0:T(8,128)(2,1)S(1)} %constant_dynamic-update-slice_fusion.15), channel_id=1, source_target_pairs={{0,2},{1,3},{2,0},{3,1},{4,6},{5,7},{6,4},{7,5},{8,10},{9,11},{10,... | collective-permute-start | bytes 786440 | tf_op jit(solution)/shard_map/ppermute | solution.py:23
  530.5 22.6 %collective-permute-start.93 = (bf16[2,16,4096]{2,1,0:T(8,128)(2,1)S(1)}, bf16[2,16,4096]{2,1,0:T(8,128)(2,1)S(1)}, u32[]{:S(2)}, u32[]{:S(2)}) collective-permute-start(bf16[2,16,4096]{2,1,0:T(8,128)(2,1)S(1)} %maximum_select_fusion.46), channel_id=1, source_target_pairs={{0,1},{1,0},{2,3},{3,2},{4,5},{5,4},{6,7},{7,6},{8,9},{9,8},{10,11... | collective-permute-start | bytes 786440 | tf_op jit(solution)/shard_map/ppermute | solution.py:19
  581.4 35.8 %collective-permute-start.111 = (bf16[16,4096]{1,0:T(8,128)(2,1)S(1)}, bf16[16,4096]{1,0:T(8,128)(2,1)S(1)}, u32[]{:S(2)}, u32[]{:S(2)}) collective-permute-start(bf16[16,4096]{1,0:T(8,128)(2,1)S(1)} %fusion.264), channel_id=1, source_target_pairs={{0,2},{1,3},{2,0},{3,1},{4,6},{5,7},{6,4},{7,5},{8,10},{9,11},{10,... | collective-permute-start | bytes 393224 | tf_op jit(solution)/shard_map/ppermute | solution.py:23
  639.7 20.7 %all-to-all-start.4 = ((bf16[32,32,192]{2,1,0:T(8,128)(2,1)}), bf16[32,32,192]{2,1,0:T(8,128)(2,1)S(1)}, u32[]{:S(2)}, u32[]{:S(2)}) async-start(bf16[32,32,192]{2,1,0:T(8,128)(2,1)} %bitcast.259), calls=%async_computation.4 | async-start | bytes 1048576 | tf_op jit(solution)/shard_map/all_to_all | solution.py:39
  661.7 21.1 %all-to-all-start.5 = ((bf16[8,5,32,192]{3,2,1,0:T(8,128)(2,1)}), bf16[8,5,32,192]{3,2,1,0:T(8,128)(2,1)S(1)}, u32[]{:S(2)}, u32[]{:S(2)}) async-start(bf16[8,5,32,192]{3,2,1,0:T(8,128)(2,1)} %broadcast_in_dim.161), calls=%async_computation.5 | async-start | bytes 1310720 | tf_op jit(solution)/shard_map/all_to_all | solution.py:39
  692.9 115.2 %collective-permute-start.154 = (bf16[2,2,1024]{2,1,0:T(2,128)(2,1)S(1)}, bf16[2,2,1024]{2,1,0:T(2,128)(2,1)S(1)}, u32[]{:S(2)}, u32[]{:S(2)}) collective-permute-start(bf16[2,2,1024]{2,1,0:T(2,128)(2,1)S(1)} %fusion.302), channel_id=1, source_target_pairs={{0,1},{1,0},{2,3},{3,2},{4,5},{5,4},{6,7},{7,6},{8,9},{9,8},{10,11... | collective-permute-start | bytes 24584 | tf_op jit(solution)/shard_map/ppermute | solution.py:19
  693.5 119.3 %collective-permute-start.90 = (f32[16,4096]{1,0:T(8,128)S(1)}, f32[16,4096]{1,0:T(8,128)}, u32[]{:S(2)}, u32[]{:S(2)}) collective-permute-start(f32[16,4096]{1,0:T(8,128)S(1)} %copy-done.70), channel_id=1, source_target_pairs={{0,2},{1,3},{2,0},{3,1},{4,6},{5,7},{6,4},{7,5},{8,10},{9,11},{10,... | collective-permute-start | bytes 786440 | tf_op jit(solution)/shard_map/ppermute | solution.py:23
  715.9 21.2 %collective-permute-start.133 = (bf16[1024,448]{0,1:T(8,128)(2,1)S(1)}, bf16[1024,448]{0,1:T(8,128)(2,1)S(1)}, u32[]{:S(2)}, u32[]{:S(2)}) collective-permute-start(bf16[1024,448]{0,1:T(8,128)(2,1)S(1)} %add_convert_fusion.5), channel_id=1, source_target_pairs={{0,8},{8,16},{16,24},{24,28},{28,20},{20,12},{12,4},{4,0},{1,9},{9... | collective-permute-start | bytes 2752520 | tf_op jit(solution)/shard_map/ppermute | solution.py:107
  718.9 28.9 %collective-permute-start.137 = (bf16[1024,448]{0,1:T(8,128)(2,1)}, bf16[1024,448]{0,1:T(8,128)(2,1)}, u32[]{:S(2)}, u32[]{:S(2)}) collective-permute-start(bf16[1024,448]{0,1:T(8,128)(2,1)} %add_convert_fusion.2), channel_id=1, source_target_pairs={{0,4},{8,0},{16,8},{24,16},{28,24},{20,28},{12,20},{4,12},{1,5},{9... | collective-permute-start | bytes 2752520 | tf_op jit(solution)/shard_map/ppermute | solution.py:107
  745.8 23.6 %collective-permute-start.134 = (bf16[1024,448]{0,1:T(8,128)(2,1)}, bf16[1024,448]{0,1:T(8,128)(2,1)}, u32[]{:S(2)}, u32[]{:S(2)}) collective-permute-start(bf16[1024,448]{0,1:T(8,128)(2,1)} %add_convert_fusion.4), channel_id=1, source_target_pairs={{0,8},{8,16},{16,24},{24,28},{28,20},{20,12},{12,4},{4,0},{1,9},{9... | collective-permute-start | bytes 2752520 | tf_op jit(solution)/shard_map/ppermute | solution.py:107
  750.7 27.3 %collective-permute-start.138 = (bf16[1024,448]{0,1:T(8,128)(2,1)}, bf16[1024,448]{0,1:T(8,128)(2,1)}, u32[]{:S(2)}, u32[]{:S(2)}) collective-permute-start(bf16[1024,448]{0,1:T(8,128)(2,1)} %add_convert_fusion.1), channel_id=1, source_target_pairs={{0,4},{8,0},{16,8},{24,16},{28,24},{20,28},{12,20},{4,12},{1,5},{9... | collective-permute-start | bytes 2752520 | tf_op jit(solution)/shard_map/ppermute | solution.py:107
  754.9 34.4 %all-to-all-start.7 = ((bf16[8,64,576]{2,1,0:T(8,128)(2,1)}), bf16[8,64,576]{2,1,0:T(8,128)(2,1)}, u32[]{:S(2)}, u32[]{:S(2)}) async-start(bf16[8,64,576]{2,1,0:T(8,128)(2,1)} %broadcast_in_dim.171), calls=%async_computation.7 | async-start | bytes 1310720 | tf_op jit(solution)/shard_map/all_to_all | solution.py:39
  764.0 17.2 %collective-permute-start.140 = (bf16[8,1,16,512]{3,2,0,1:T(8,128)(2,1)S(1)}, bf16[8,1,16,512]{3,2,0,1:T(8,128)(2,1)S(1)}, u32[]{:S(2)}, u32[]{:S(2)}) collective-permute-start(bf16[8,1,16,512]{3,2,0,1:T(8,128)(2,1)S(1)} %bitcast.1320), channel_id=1, source_target_pairs={{0,2},{1,3},{2,0},{3,1},{4,6},{5,7},{6,4},{7,5},{8,10},{9,11},{10,... | collective-permute-start | bytes 393224 | tf_op jit(solution)/shard_map/ppermute | solution.py:23
  772.3 23.4 %collective-permute-start.135 = (bf16[1024,448]{0,1:T(8,128)(2,1)}, bf16[1024,448]{0,1:T(8,128)(2,1)}, u32[]{:S(2)}, u32[]{:S(2)}) collective-permute-start(bf16[1024,448]{0,1:T(8,128)(2,1)} %add_convert_fusion.3), channel_id=1, source_target_pairs={{0,8},{8,16},{16,24},{24,28},{28,20},{20,12},{12,4},{4,0},{1,9},{9... | collective-permute-start | bytes 2752520 | tf_op jit(solution)/shard_map/ppermute | solution.py:107
  781.0 19.8 %collective-permute-start.139 = (bf16[1024,448]{0,1:T(8,128)(2,1)}, bf16[1024,448]{0,1:T(8,128)(2,1)}, u32[]{:S(2)}, u32[]{:S(2)}) collective-permute-start(bf16[1024,448]{0,1:T(8,128)(2,1)} %add_convert_fusion), channel_id=1, source_target_pairs={{0,4},{8,0},{16,8},{24,16},{28,24},{20,28},{12,20},{4,12},{1,5},{9... | collective-permute-start | bytes 2752520 | tf_op jit(solution)/shard_map/ppermute | solution.py:107
  831.3 23.2 %all-to-all-start.8 = ((bf16[8,32,1152]{2,1,0:T(8,128)(2,1)}), bf16[8,32,1152]{2,1,0:T(8,128)(2,1)}, u32[]{:S(2)}, u32[]{:S(2)}) async-start(bf16[8,32,1152]{2,1,0:T(8,128)(2,1)} %fusion.41), calls=%async_computation.8 | async-start | bytes 1179648 | tf_op jit(solution)/shard_map/all_to_all | solution.py:39
  841.2 27.7 %collective-permute-start.170 = (bf16[2,512,192]{1,2,0:T(8,128)(2,1)}, bf16[2,512,192]{1,2,0:T(8,128)(2,1)}, u32[]{:S(2)}, u32[]{:S(2)}) collective-permute-start(bf16[2,512,192]{1,2,0:T(8,128)(2,1)} %fusion.168), channel_id=1, source_target_pairs={{0,1},{1,0},{2,3},{3,2},{4,5},{5,4},{6,7},{7,6},{8,9},{9,8},{10,11... | collective-permute-start | bytes 1179656 | tf_op jit(solution)/shard_map/ppermute | solution.py:19
  874.7 41.0 %collective-permute-start.171 = (bf16[512,192]{0,1:T(8,128)(2,1)}, bf16[512,192]{0,1:T(8,128)(2,1)}, u32[]{:S(2)}, u32[]{:S(2)}) collective-permute-start(bf16[512,192]{0,1:T(8,128)(2,1)} %fusion.256), channel_id=1, source_target_pairs={{0,2},{1,3},{2,0},{3,1},{4,6},{5,7},{6,4},{7,5},{8,10},{9,11},{10,... | collective-permute-start | bytes 589832 | tf_op jit(solution)/shard_map/ppermute | solution.py:23
  875.2 32.8 %all-to-all-start.9 = ((bf16[8,144,448]{2,1,0:T(8,128)(2,1)}), bf16[8,144,448]{2,1,0:T(8,128)(2,1)}, u32[]{:S(2)}, u32[]{:S(2)}) async-start(bf16[8,144,448]{2,1,0:T(8,128)(2,1)} %bitcast.1195), calls=%async_computation.9 | async-start | bytes 2359296 | tf_op jit(solution)/shard_map/all_to_all | solution.py:39
  910.8 30.2 %all-to-all-start.10 = ((bf16[8,128,512]{2,1,0:T(8,128)(2,1)}), bf16[8,128,512]{2,1,0:T(8,128)(2,1)}, u32[]{:S(2)}, u32[]{:S(2)}) async-start(bf16[8,128,512]{2,1,0:T(8,128)(2,1)} %pad_maximum_fusion.1), calls=%async_computation.10 | async-start | bytes 2097152 | tf_op jit(solution)/shard_map/all_to_all | solution.py:39
  942.4 41.4 %all-to-all-start.11 = ((bf16[8,144,448]{2,1,0:T(8,128)(2,1)}), bf16[8,144,448]{2,1,0:T(8,128)(2,1)}, u32[]{:S(2)}, u32[]{:S(2)}) async-start(bf16[8,144,448]{2,1,0:T(8,128)(2,1)} %bitcast.345), calls=%async_computation.11 | async-start | bytes 2359296 | tf_op jit(solution)/shard_map/all_to_all | solution.py:39
  946.7 119.9 %all-gather.19.cloned.1.call-start = ((), (), s32[]{:S(2)}) async-start(), calls=%async_computation.17 | async-start | bytes 2488320 | tf_op jit(solution)/shard_map/all_gather | solution.py:80
  950.0 20.8 %collective-permute-start.158 = (bf16[8,4,32,144]{3,2,1,0:T(8,128)(2,1)}, bf16[8,4,32,144]{3,2,1,0:T(8,128)(2,1)}, u32[]{:S(2)}, u32[]{:S(2)}) collective-permute-start(bf16[8,4,32,144]{3,2,1,0:T(8,128)(2,1)} %bitcast.370), channel_id=1, source_target_pairs={{0,2},{1,3},{2,0},{3,1},{4,6},{5,7},{6,4},{7,5},{8,10},{9,11},{10,... | collective-permute-start | bytes 884744 | tf_op jit(solution)/shard_map/ppermute | solution.py:23
  987.3 41.9 %collective-permute-start.150 = (f32[128,1152]{1,0:T(8,128)S(1)}, f32[128,1152]{1,0:T(8,128)S(1)}, u32[]{:S(2)}, u32[]{:S(2)}) collective-permute-start(f32[128,1152]{1,0:T(8,128)S(1)} %convolution_add_fusion.2), channel_id=1, source_target_pairs={{0,1},{1,0},{2,3},{3,2},{4,5},{5,4},{6,7},{7,6},{8,9},{9,8},{10,11... | collective-permute-start | bytes 1769480 | tf_op jit(solution)/shard_map/ppermute | solution.py:19
  1005.9 17.6 %collective-permute-start.162 = (bf16[128,864]{0,1:T(8,128)(2,1)S(1)}, bf16[128,864]{0,1:T(8,128)(2,1)S(1)}, u32[]{:S(2)}, u32[]{:S(2)}) collective-permute-start(bf16[128,864]{0,1:T(8,128)(2,1)S(1)} %collective-permute-done.161), channel_id=1, source_target_pairs={{0,4},{8,0},{16,8},{24,16},{28,24},{20,28},{12,20},{4,12},{1,5},{9... | collective-permute-start | bytes 663560 | tf_op jit(solution)/shard_map/ppermute | solution.py:107
  (352 other events, 3409.7 us)
Sparse Core Ops, SparseCore 0:
  10.2 67.4 all-gather.10
  79.9 63.6 all-gather.12
  342.3 68.3 all-gather.14
  524.5 77.4 all-gather.16
  951.6 68.6 all-gather.18
